TPU v7x, 128 devices: a whole 4x4x4 slice. The times are simulated.
128 devices in a mesh: dp: 8 (over y, core), expert: 16 (over z, x).
Axes of the slice: x: 4, y: 4, z: 4, core: 2. Of those that a mesh axis runs over, the one named last changes fastest.
Arguments:
- inputs: bfloat16 [8, 2048, 1024], P('dp', 'expert'), may hold values from -6 to 6
- segments: int32 [8, 2048], P('dp'), may hold values from 0 to 3, as said below
- routes: int32 [8, 2048, 8], P('dp', 'expert'), may hold values from 0 to 31, all different within a row; in each aligned block of 128 rows (0 to 127, 128 to 255, ..., all dimensions but the last counted through in order) at most 40 rows name the same one
- gain_attn: bfloat16 [1024], P('dp'), may hold values from 0.5 to 1.5
- w_query: bfloat16 [1024, 1024], P('dp'), may hold values from -0.25 to 0.25
- w_key: bfloat16 [1024, 512], P('dp'), may hold values from -0.25 to 0.25
- w_value: bfloat16 [1024, 512], P('dp'), may hold values from -0.1875 to 0.1875
- w_out: bfloat16 [1024, 1024], P('dp'), may hold values from -1.5 to 1.5
- gain_ffn: bfloat16 [1024], P('dp'), may hold values from 0.5 to 1.5
- w_router: bfloat16 [1024, 32], P('dp'), may hold values from -0.09375 to 0.09375
- expert_gate: bfloat16 [32, 1024, 512], P('expert', 'dp'), may hold values from -0.1875 to 0.1875
- expert_up: bfloat16 [32, 1024, 512], P('expert', 'dp'), may hold values from -0.1875 to 0.1875
- expert_down: bfloat16 [32, 512, 1024], P('expert', 'dp'), may hold values from -4 to 4
- cotangent: bfloat16 [8, 2048, 1024], P('dp', 'expert'), may hold values from -6 to 6
Outputs:
- output: bfloat16 [8, 2048, 1024], P('dp', 'expert')
- grad_input: float32 [8, 2048, 1024], P('dp', 'expert')
- grad_gain_attn: float32 [1024], P('dp')
- grad_w_query: float32 [1024, 1024], P('dp')
- grad_w_key: float32 [1024, 512], P('dp')
- grad_w_value: float32 [1024, 512], P('dp')
- grad_w_out: float32 [1024, 1024], P('dp')
- grad_gain_ffn: float32 [1024], P('dp')
- grad_w_router: float32 [1024, 32], P('dp')
- grad_expert_gate: float32 [32, 1024, 512], P('expert', 'dp')
- grad_expert_up: float32 [32, 1024, 512], P('expert', 'dp')
- grad_expert_down: float32 [32, 512, 1024], P('expert', 'dp')
Inputs may be any that keep to these rules, and one draw needn't show every extreme that they name: Each row of routes names 8 different experts; among the rows of one device no expert is named by more than 40 rows, and some expert reaches 40. `segments`: segment numbers start at 0 in every packed row, never fall, and rise by one at each new document; in every row one document begins among the first 128 positions and ends among the last 128.
All inputs are finite; a program needn't handle non-finite values.
Results may differ from a plain program's by a relative error of at most 0.025.
Values may be sent and summed in bfloat16 or wider, within the bound.
No kernel may reach another device: no remote copies, remote signals or barrier semaphores. Data moves between devices by JAX's collectives and lax.ppermute only.
A program may use at most 128 MiB of HBM per device.

v0:
```python
import jax
import jax.numpy as jnp
from jax import lax
from jax.sharding import PartitionSpec as P

D = 1024
HEADS = 16
KV_HEADS = 8
HD = 64
TOPK = 8


eps = 1e-06
theta = 10000.0


def norm_apply(values, gain):
    return values * lax.rsqrt(jnp.mean(values * values, axis=-1, keepdims=True) + eps) * gain


def doc_positions(segment_row):
    index = jnp.arange(segment_row.shape[0], dtype=jnp.int32)
    fresh = jnp.concatenate([jnp.ones((1,), dtype=jnp.bool_), segment_row[1:] != segment_row[:-1]])
    return index - lax.cummax(jnp.where(fresh, index, 0), axis=0)


def rope_tables(positions):
    freqs = theta ** (-jnp.arange(0, HD, 2, dtype=jnp.float32) / HD)
    angles = positions.astype(jnp.float32)[:, None] * freqs[None, :]
    angles = jnp.concatenate([angles, angles], axis=-1)
    return (jnp.cos(angles), jnp.sin(angles))


def rotate(values, cosine, sine):
    half = HD // 2
    turned = jnp.concatenate([-values[..., half:], values[..., :half]], axis=-1)
    return values * cosine[:, None, :] + turned * sine[:, None, :]


def rotate_back(grads, cosine, sine):
    half = HD // 2
    turned = grads * sine[:, None, :]
    return grads * cosine[:, None, :] + jnp.concatenate(
        [turned[..., half:], -turned[..., :half]], axis=-1
    )


def swiglu(gate_pre, up_pre):
    return jax.nn.silu(gate_pre) * up_pre


def pick_gates(logits, choose):
    return jnp.sum(jax.nn.softmax(logits, axis=-1)[:, None, :] * choose, axis=-1)


def per_device(
    inputs,
    segments,
    routes,
    gain_attn,
    w_query,
    w_key,
    w_value,
    w_out,
    gain_ffn,
    w_router,
    expert_gate,
    expert_up,
    expert_down,
    cotangent,
):
    rows = inputs.shape[1]
    length = segments.shape[1]
    experts_total = w_router.shape[1]
    local_experts = expert_gate.shape[0]
    peers = lax.axis_size("expert")
    capacity = 5 * rows * TOPK // (4 * experts_total)
    scale = HD ** (-0.5)
    block = min(512, length)
    count = length // block
    offset = lax.axis_index("expert") * rows
    width = HEADS * HD
    kv_width = KV_HEADS * HD
    group = HEADS // KV_HEADS
    dense = (
        lax.all_gather(gain_attn, "dp", axis=0, tiled=True),
        lax.all_gather(w_query, "dp", axis=0, tiled=True),
        lax.all_gather(w_key, "dp", axis=0, tiled=True),
        lax.all_gather(w_value, "dp", axis=0, tiled=True),
        lax.all_gather(w_out, "dp", axis=0, tiled=True),
        lax.all_gather(gain_ffn, "dp", axis=0, tiled=True),
        lax.all_gather(w_router, "dp", axis=0, tiled=True),
    )
    full_gain_attn, full_query, full_key, full_value, full_out, full_gain_ffn, full_router = dense
    gate_full, up_full, down_full = (
        lax.all_gather(expert_gate, "dp", axis=1, tiled=True),
        lax.all_gather(expert_up, "dp", axis=1, tiled=True),
        lax.all_gather(expert_down, "dp", axis=1, tiled=True),
    )
    states = inputs[0].astype(jnp.float32)
    segment_row = segments[0]
    cosine, sine = rope_tables(doc_positions(segment_row))
    my_cosine = lax.dynamic_slice_in_dim(cosine, offset, rows, 0)
    my_sine = lax.dynamic_slice_in_dim(sine, offset, rows, 0)
    query_segment = lax.dynamic_slice_in_dim(segment_row, offset, rows, 0)
    query_index = offset + jnp.arange(rows, dtype=jnp.int32)
    normed, attn_norm_back = jax.vjp(norm_apply, states, full_gain_attn.astype(jnp.float32))
    normed_low = normed.astype(jnp.bfloat16)
    query = jnp.dot(normed_low, full_query, preferred_element_type=jnp.float32).reshape(
        rows, HEADS, HD
    )
    query_rot = (
        rotate(query, my_cosine, my_sine).astype(jnp.bfloat16).reshape(rows, KV_HEADS, group, HD)
    )
    keys = jnp.dot(normed_low, full_key, preferred_element_type=jnp.float32).reshape(
        rows, KV_HEADS, HD
    )
    key_rot = rotate(keys, my_cosine, my_sine).astype(jnp.bfloat16).reshape(rows, kv_width)
    value_low = jnp.dot(normed_low, full_value, preferred_element_type=jnp.float32).astype(
        jnp.bfloat16
    )
    key_full, value_full = (
        lax.all_gather(key_rot, "expert", axis=0, tiled=True),
        lax.all_gather(value_low, "expert", axis=0, tiled=True),
    )
    starts = jnp.arange(count, dtype=jnp.int32) * block

    def scores_at(start, key_source):
        key_rows = lax.dynamic_slice_in_dim(key_source, start, block, 0).reshape(
            block, KV_HEADS, HD
        )
        key_segment = lax.dynamic_slice_in_dim(segment_row, start, block, 0)
        key_index = start + jnp.arange(block, dtype=jnp.int32)
        unmasked = (
            jnp.einsum("qkgd,tkd->kgqt", query_rot, key_rows, preferred_element_type=jnp.float32)
            * scale
        )
        allowed = (query_segment[:, None] == key_segment[None, :]) & (
            query_index[:, None] >= key_index[None, :]
        )
        return (jnp.where(allowed[None, None], unmasked, -1000000000.0), key_rows)

    def find_ceiling(carry, start):
        ceiling, total = carry
        scores, _ = scores_at(start, key_full)
        higher = jnp.maximum(ceiling, jnp.max(scores, axis=-1))
        total = total * jnp.exp(ceiling - higher) + jnp.sum(
            jnp.exp(scores - higher[..., None]), axis=-1
        )
        return ((higher, total), None)

    (ceiling, total), _ = lax.scan(
        find_ceiling,
        (
            jnp.full((KV_HEADS, group, rows), -jnp.inf, jnp.float32),
            jnp.zeros((KV_HEADS, group, rows), jnp.float32),
        ),
        starts,
    )
    log_total = ceiling + jnp.log(total)

    def weigh(mixed, start):
        scores, _ = scores_at(start, key_full)
        chances = jnp.exp(scores - log_total[..., None]).astype(jnp.bfloat16)
        value_rows = lax.dynamic_slice_in_dim(value_full, start, block, 0).reshape(
            block, KV_HEADS, HD
        )
        return (
            mixed
            + jnp.einsum("kgqt,tkd->qkgd", chances, value_rows, preferred_element_type=jnp.float32),
            None,
        )

    mixed, _ = lax.scan(weigh, jnp.zeros((rows, KV_HEADS, group, HD), jnp.float32), starts)
    mixed_low = mixed.reshape(rows, width).astype(jnp.bfloat16)
    hidden = states + jnp.dot(mixed_low, full_out, preferred_element_type=jnp.float32)
    ffn_in, ffn_norm_back = jax.vjp(norm_apply, hidden, full_gain_ffn.astype(jnp.float32))
    ffn_low = ffn_in.astype(jnp.bfloat16)
    logits = jnp.dot(ffn_low, full_router, preferred_element_type=jnp.float32)
    my_routes = routes[0]
    choose = (my_routes[:, :, None] == jnp.arange(experts_total, dtype=jnp.int32)).astype(
        jnp.float32
    )
    gates, gate_back = jax.vjp(pick_gates, logits, choose)
    flat_routes = my_routes.reshape(rows * TOPK)
    choose_int = (
        flat_routes[:, None] == jnp.arange(experts_total, dtype=jnp.int32)[None, :]
    ).astype(jnp.int32)
    rank = jnp.cumsum(choose_int, axis=0) - choose_int
    places = flat_routes * capacity + jnp.sum(rank * choose_int, axis=1)
    slot_ids = jnp.arange(experts_total * capacity, dtype=jnp.int32)
    dispatch_table = jnp.any(
        places.reshape(rows, TOPK)[None, :, :] == slot_ids[:, None, None], axis=-1
    ).astype(jnp.bfloat16)
    send = jnp.dot(dispatch_table, ffn_low, preferred_element_type=jnp.float32).astype(jnp.bfloat16)
    send = send.reshape(peers, local_experts, capacity, D)
    arrived = lax.all_to_all(send, "expert", split_axis=0, concat_axis=0, tiled=True)
    gate_pre = jnp.einsum("sicd,idf->sicf", arrived, gate_full, preferred_element_type=jnp.float32)
    up_pre = jnp.einsum("sicd,idf->sicf", arrived, up_full, preferred_element_type=jnp.float32)
    acted = swiglu(gate_pre, up_pre).astype(jnp.bfloat16)
    result = jnp.einsum("sicf,ifd->sicd", acted, down_full, preferred_element_type=jnp.float32)
    result, arrived, acted, gate_pre, up_pre = (
        result.astype(jnp.bfloat16),
        arrived,
        acted,
        gate_pre,
        up_pre,
    )
    returned = lax.all_to_all(result, "expert", split_axis=0, concat_axis=0, tiled=True).reshape(
        experts_total * capacity, D
    )
    picked = jnp.take(returned, places, axis=0).reshape(rows, TOPK, D).astype(jnp.float32)
    routed = jnp.sum(gates[..., None] * picked, axis=1)
    output = hidden + routed
    query_back, key_back, value_back, out_back, router_back = (
        lax.all_gather(w_query, "dp", axis=0, tiled=True),
        lax.all_gather(w_key, "dp", axis=0, tiled=True),
        lax.all_gather(w_value, "dp", axis=0, tiled=True),
        lax.all_gather(w_out, "dp", axis=0, tiled=True),
        lax.all_gather(w_router, "dp", axis=0, tiled=True),
    )
    gate_back_w, up_back_w, down_back_w = (
        lax.all_gather(expert_gate, "dp", axis=1, tiled=True),
        lax.all_gather(expert_up, "dp", axis=1, tiled=True),
        lax.all_gather(expert_down, "dp", axis=1, tiled=True),
    )
    key_again, value_again = (
        lax.all_gather(key_rot, "expert", axis=0, tiled=True),
        lax.all_gather(value_low, "expert", axis=0, tiled=True),
    )
    grad_out = cotangent[0].astype(jnp.float32)
    gate_grad = jnp.sum(grad_out[:, None, :] * picked, axis=-1)
    logit_grad, _ = gate_back(gate_grad)
    logit_grad = logit_grad.astype(jnp.bfloat16)
    grad_w_router = jnp.dot(ffn_low.T, logit_grad, preferred_element_type=jnp.float32)
    token_of = jnp.arange(rows * TOPK, dtype=jnp.int32) // TOPK
    slot_owner = jnp.zeros((experts_total * capacity,), jnp.int32).at[places].set(token_of)
    slot_gate = (
        jnp.zeros((experts_total * capacity,), jnp.float32).at[places].set(gates.reshape(-1))
    )
    slot_grad = (slot_gate[:, None] * jnp.take(grad_out, slot_owner, axis=0)).astype(jnp.bfloat16)
    slot_grad = slot_grad.reshape(peers, local_experts, capacity, D)
    arrived_grad = lax.all_to_all(slot_grad, "expert", split_axis=0, concat_axis=0, tiled=True)
    grad_expert_down = jnp.einsum(
        "sicf,sicd->ifd", acted, arrived_grad, preferred_element_type=jnp.float32
    )
    acted_grad = jnp.einsum(
        "sicd,ifd->sicf", arrived_grad, down_back_w, preferred_element_type=jnp.float32
    )
    _, expert_act_back = jax.vjp(swiglu, gate_pre, up_pre)
    expert_gate_grad, expert_up_grad = expert_act_back(acted_grad)
    expert_gate_grad = expert_gate_grad.astype(jnp.bfloat16)
    expert_up_grad = expert_up_grad.astype(jnp.bfloat16)
    grad_expert_gate = jnp.einsum(
        "sicd,sicf->idf", arrived, expert_gate_grad, preferred_element_type=jnp.float32
    )
    grad_expert_up = jnp.einsum(
        "sicd,sicf->idf", arrived, expert_up_grad, preferred_element_type=jnp.float32
    )
    buffer_grad = jnp.einsum(
        "sicf,idf->sicd", expert_gate_grad, gate_back_w, preferred_element_type=jnp.float32
    ) + jnp.einsum("sicf,idf->sicd", expert_up_grad, up_back_w, preferred_element_type=jnp.float32)
    buffer_grad = buffer_grad.astype(jnp.bfloat16)
    sent_grad = lax.all_to_all(
        buffer_grad, "expert", split_axis=0, concat_axis=0, tiled=True
    ).reshape(experts_total * capacity, D)
    ffn_in_grad = jnp.dot(logit_grad, router_back.T, preferred_element_type=jnp.float32) + jnp.dot(
        dispatch_table.T, sent_grad, preferred_element_type=jnp.float32
    )
    hidden_norm_grad, grad_gain_ffn = ffn_norm_back(ffn_in_grad)
    hidden_grad = grad_out + hidden_norm_grad
    attn_grad = hidden_grad.astype(jnp.bfloat16)
    grad_w_out = jnp.dot(mixed_low.T, attn_grad, preferred_element_type=jnp.float32)
    mixed_grad = jnp.dot(attn_grad, out_back.T, preferred_element_type=jnp.float32).astype(
        jnp.bfloat16
    )
    mixed_grad = mixed_grad.reshape(rows, KV_HEADS, group, HD)

    def gather_delta(delta, start):
        scores, _ = scores_at(start, key_again)
        expo = jnp.exp(scores - log_total[..., None])
        value_rows = lax.dynamic_slice_in_dim(value_again, start, block, 0).reshape(
            block, KV_HEADS, HD
        )
        chance_grad = jnp.einsum(
            "qkgd,tkd->kgqt", mixed_grad, value_rows, preferred_element_type=jnp.float32
        )
        return (delta + jnp.sum(expo * chance_grad, axis=-1), None)

    delta, _ = lax.scan(gather_delta, jnp.zeros((KV_HEADS, group, rows), jnp.float32), starts)

    def attention_back(query_grad, start):
        scores, key_rows = scores_at(start, key_again)
        expo = jnp.exp(scores - log_total[..., None])
        value_rows = lax.dynamic_slice_in_dim(value_again, start, block, 0).reshape(
            block, KV_HEADS, HD
        )
        chance_grad = jnp.einsum(
            "qkgd,tkd->kgqt", mixed_grad, value_rows, preferred_element_type=jnp.float32
        )
        score_grad = (expo * (chance_grad - delta[..., None])).astype(jnp.bfloat16)
        query_grad = query_grad + jnp.einsum(
            "kgqt,tkd->qkgd", score_grad, key_rows, preferred_element_type=jnp.float32
        )
        key_term = (
            jnp.einsum("kgqt,qkgd->tkd", score_grad, query_rot, preferred_element_type=jnp.float32)
            * scale
        )
        value_term = jnp.einsum(
            "kgqt,qkgd->tkd",
            expo.astype(jnp.bfloat16),
            mixed_grad,
            preferred_element_type=jnp.float32,
        )
        return (
            query_grad,
            (key_term.reshape(block, kv_width), value_term.reshape(block, kv_width)),
        )

    query_grad, (key_terms, value_terms) = lax.scan(
        attention_back, jnp.zeros((rows, KV_HEADS, group, HD), jnp.float32), starts
    )
    key_grad, value_grad = (
        lax.psum_scatter(
            key_terms.reshape(length, kv_width).astype(jnp.bfloat16),
            "expert",
            scatter_dimension=0,
            tiled=True,
        ).astype(jnp.float32),
        lax.psum_scatter(
            value_terms.reshape(length, kv_width).astype(jnp.bfloat16),
            "expert",
            scatter_dimension=0,
            tiled=True,
        ).astype(jnp.float32),
    )
    query_low_grad = rotate_back((query_grad * scale).reshape(rows, HEADS, HD), my_cosine, my_sine)
    query_low_grad = query_low_grad.astype(jnp.bfloat16).reshape(rows, width)
    key_low_grad = rotate_back(key_grad.reshape(rows, KV_HEADS, HD), my_cosine, my_sine)
    key_low_grad = key_low_grad.astype(jnp.bfloat16).reshape(rows, kv_width)
    value_low_grad = value_grad.astype(jnp.bfloat16)
    grad_w_query = jnp.dot(normed_low.T, query_low_grad, preferred_element_type=jnp.float32)
    grad_w_key = jnp.dot(normed_low.T, key_low_grad, preferred_element_type=jnp.float32)
    grad_w_value = jnp.dot(normed_low.T, value_low_grad, preferred_element_type=jnp.float32)
    normed_grad = (
        jnp.dot(query_low_grad, query_back.T, preferred_element_type=jnp.float32)
        + jnp.dot(key_low_grad, key_back.T, preferred_element_type=jnp.float32)
        + jnp.dot(value_low_grad, value_back.T, preferred_element_type=jnp.float32)
    )
    states_grad, grad_gain_attn = attn_norm_back(normed_grad)
    grad_input = hidden_grad + states_grad
    shard_sums = (
        lax.psum_scatter(
            grad_gain_attn.astype(jnp.bfloat16), "dp", scatter_dimension=0, tiled=True
        ).astype(jnp.float32),
        lax.psum_scatter(
            grad_w_query.astype(jnp.bfloat16), "dp", scatter_dimension=0, tiled=True
        ).astype(jnp.float32),
        lax.psum_scatter(
            grad_w_key.astype(jnp.bfloat16), "dp", scatter_dimension=0, tiled=True
        ).astype(jnp.float32),
        lax.psum_scatter(
            grad_w_value.astype(jnp.bfloat16), "dp", scatter_dimension=0, tiled=True
        ).astype(jnp.float32),
        lax.psum_scatter(
            grad_w_out.astype(jnp.bfloat16), "dp", scatter_dimension=0, tiled=True
        ).astype(jnp.float32),
        lax.psum_scatter(
            grad_gain_ffn.astype(jnp.bfloat16), "dp", scatter_dimension=0, tiled=True
        ).astype(jnp.float32),
        lax.psum_scatter(
            grad_w_router.astype(jnp.bfloat16), "dp", scatter_dimension=0, tiled=True
        ).astype(jnp.float32),
    )
    sum_gain_attn, sum_query, sum_key, sum_value, sum_out, sum_gain_ffn, sum_router = (
        lax.psum(shard_sums[0].astype(jnp.bfloat16), "expert").astype(jnp.float32),
        lax.psum(shard_sums[1].astype(jnp.bfloat16), "expert").astype(jnp.float32),
        lax.psum(shard_sums[2].astype(jnp.bfloat16), "expert").astype(jnp.float32),
        lax.psum(shard_sums[3].astype(jnp.bfloat16), "expert").astype(jnp.float32),
        lax.psum(shard_sums[4].astype(jnp.bfloat16), "expert").astype(jnp.float32),
        lax.psum(shard_sums[5].astype(jnp.bfloat16), "expert").astype(jnp.float32),
        lax.psum(shard_sums[6].astype(jnp.bfloat16), "expert").astype(jnp.float32),
    )
    sum_expert_gate, sum_expert_up, sum_expert_down = (
        lax.psum_scatter(
            grad_expert_gate.astype(jnp.bfloat16), "dp", scatter_dimension=1, tiled=True
        ).astype(jnp.float32),
        lax.psum_scatter(
            grad_expert_up.astype(jnp.bfloat16), "dp", scatter_dimension=1, tiled=True
        ).astype(jnp.float32),
        lax.psum_scatter(
            grad_expert_down.astype(jnp.bfloat16), "dp", scatter_dimension=1, tiled=True
        ).astype(jnp.float32),
    )
    return (
        output.astype(jnp.bfloat16)[None],
        grad_input[None],
        sum_gain_attn,
        sum_query,
        sum_key,
        sum_value,
        sum_out,
        sum_gain_ffn,
        sum_router,
        sum_expert_gate,
        sum_expert_up,
        sum_expert_down,
    )


def solution(mesh):
    placed = (
        P("dp", "expert", None),
        P("dp", None),
        P("dp", "expert", None),
        P("dp"),
        P("dp", None),
        P("dp", None),
        P("dp", None),
        P("dp", None),
        P("dp"),
        P("dp", None),
        P("expert", "dp", None),
        P("expert", "dp", None),
        P("expert", "dp", None),
        P("dp", "expert", None),
    )
    return jax.shard_map(
        per_device,
        mesh=mesh,
        in_specs=placed,
        out_specs=(
            P("dp", "expert", None),
            P("dp", "expert", None),
            P("dp"),
            P("dp", None),
            P("dp", None),
            P("dp", None),
            P("dp", None),
            P("dp"),
            P("dp", None),
            P("expert", "dp", None),
            P("expert", "dp", None),
            P("expert", "dp", None),
        ),
        check_vma=False,
    )
```

profile of v0, /device:TPU:0, one launch (start us, length us, event | category | flops | bytes accessed | tf_op | source)
XLA Modules:
  0.0 1097.3 jit_solution(13485042428282990163)
XLA Ops:
  11.4 11.0 %all-gather = bf16[8,1,128]{2,1,0:T(2,128)(2,1)S(1)} all-gather(bf16[1,1,128]{2,1,0:T(2,128)(2,1)} %bitcast.509), channel_id=1, replica_groups=mesh['dp'=8,'expert'=16] {'dp'}, dimensions={0}, use_global_device_ids=true | all-gather | bytes 2304 | tf_op jit(solution)/shard_map/all_gather | solution.py:86
  23.5 12.2 %all-gather.16.cloned.1.call-done = bf16[1024,512]{1,0:T(8,128)(2,1)} async-done(((bf16[128,512]{1,0:T(8,128)(2,1)}), bf16[1024,512]{1,0:T(8,128)(2,1)}) %all-gather.16.cloned.1.call-update) | async-done | bytes 1048592 | tf_op jit(solution)/shard_map/all_gather | solution.py:88
  38.5 22.1 %all-gather.12.cloned.1.call-done = bf16[1024,512]{1,0:T(8,128)(2,1)} async-done(((bf16[128,512]{1,0:T(8,128)(2,1)}), bf16[1024,512]{1,0:T(8,128)(2,1)}) %all-gather.12.cloned.1.call-update) | async-done | bytes 1048592 | tf_op jit(solution)/shard_map/all_gather | solution.py:89
  65.9 9.1 all-gather.1
  75.1 9.0 reduce-window.19
  84.7 4.7 fusion.37
  93.3 44.8 %all-gather.18.cloned.1.call-done = bf16[2048,512]{0,1:T(8,128)(2,1)} async-done(((bf16[128,512]{0,1:T(8,128)(2,1)}), bf16[2048,512]{0,1:T(8,128)(2,1)}) %all-gather.18.cloned.1.call-update) | async-done | bytes 2097168 | tf_op jit(solution)/shard_map/all_gather | solution.py:123
  138.1 46.0 %while.50 = (s32[]{:T(128)}, f32[8,2,128]{2,1,0:T(2,128)S(1)}, f32[8,2,128]{2,1,0:T(2,128)S(1)}, s32[128]{0:T(128)S(1)}, s32[4]{0:T(128)S(1)}, /*index=5*/s32[20...) while((s32[]{:T(128)}, f32[8,2,128]{2,1,0:T(2,128)S(1)}, ...), condition=%wide.region_6.7_spmd.clone, body=%wide.region_3.6_spmd.clone.sunk | while | flops 141765248 | bytes 10538686 | solution.py:152
  185.2 3.9 copy.107
  189.1 30.0 %while.51 = (s32[]{:T(128)}, f32[128,8,2,64]{0,3,2,1:T(8,128)S(1)}, s32[4]{0:T(128)S(1)}, bf16[2048,512]{0,1:T(8,128)(2,1)}, s32[128]{0:T(128)S(1)}, /*index=5*/...) while((s32[]{:T(128)}, f32[128,8,2,64]{0,3,2,1:T(8,128)S(1)}, ...), condition=%wide.region_8.9_spmd.clone, body=%wide.region_7.8_spmd.clone.sunk | while | flops 273089152 | bytes 4607685 | solution.py:174
  225.6 5.0 all-to-all-start
  230.6 10.9 all-gather.28.cloned.1.call-start
  241.5 25.4 %all-to-all-done = bf16[16,2,40,1024]{3,2,1,0:T(8,128)(2,1)S(1)} async-done(((bf16[16,2,40,1024]{3,2,1,0:T(8,128)(2,1)}), bf16[16,2,40,1024]{3,2,1,0:T(8,128)(2,1)S(1)}, u32[]{:S(2)}, u32[]{:S(2)}) %all-to-all-start) | async-done | bytes 2621472 | tf_op jit(solution)/shard_map/all_to_all | solution.py:197
  266.9 5.6 fusion.54
  272.5 6.0 fusion.44
  278.5 14.5 %all-gather.28.cloned.1.call-done = bf16[2,512,1024]{2,1,0:T(8,128)(2,1)} async-done(((bf16[2,64,1024]{2,1,0:T(8,128)(2,1)}), bf16[2,512,1024]{2,1,0:T(8,128)(2,1)}) %all-gather.28.cloned.1.call-update) | async-done | bytes 2097168 | tf_op jit(solution)/shard_map/all_gather | solution.py:98
  298.4 6.9 all-to-all-start.1
  305.7 4.3 scatter_custom_fusion.1
  311.7 5.2 gather_fusion.1
  316.9 11.2 %all_gather.54 = bf16[1024,32]{0,1:T(8,128)(2,1)S(1)} all-gather(bf16[128,32]{0,1:T(8,128)(2,1)S(1)} %copy-done.53), channel_id=1, replica_groups=mesh['dp'=8,'expert'=16] {'dp'}, dimensions={0}, use_global_device_ids=true | all-gather | bytes 73728 | tf_op jit(solution)/shard_map/all_gather | solution.py:92
  329.9 16.3 %all-to-all-done.1 = bf16[16,2,40,1024]{3,2,1,0:T(8,128)(2,1)S(1)} async-done(((bf16[16,2,40,1024]{3,2,1,0:T(8,128)(2,1)}), bf16[16,2,40,1024]{3,2,1,0:T(8,128)(2,1)S(1)}, u32[]{:S(2)}, u32[]{:S(2)}) %all-to-all-start.1) | async-done | bytes 2621472 | tf_op jit(solution)/shard_map/all_to_all | solution.py:209
  346.2 5.4 gather_fusion
  354.4 4.5 scatter_custom_fusion
  362.0 37.8 %all_to_all.20 = bf16[16,2,40,1024]{3,2,1,0:T(8,128)(2,1)S(1)} all-to-all(bf16[16,2,40,1024]{3,2,1,0:T(8,128)(2,1)S(1)} %multiply_convert_fusion), channel_id=1, replica_groups=mesh['dp'=8,'expert'=16] {'expert'}, dimensions={0} | all-to-all | bytes 5242880 | tf_op jit(solution)/shard_map/all_to_all | solution.py:243
  408.3 4.6 all-to-all-start.3
  416.4 32.1 %all-to-all-done.3 = bf16[16,2,40,1024]{3,2,1,0:T(8,128)(2,1)} async-done(((bf16[16,2,40,1024]{3,2,1,0:T(8,128)(2,1)}), bf16[16,2,40,1024]{3,2,1,0:T(8,128)(2,1)}, u32[]{:S(2)}, u32[]{:S(2)}) %all-to-all-start.3) | async-done | bytes 2621472 | tf_op jit(solution)/shard_map/all_to_all | solution.py:264
  454.7 29.6 %while.52 = (s32[]{:T(128)}, f32[8,2,128]{2,1,0:T(2,128)S(1)}, s32[128]{0:T(128)S(1)}, s32[4]{0:T(128)S(1)}, s32[2048]{0:T(1024)S(1)}, /*index=5*/bf16[2048,512]...) while((s32[]{:T(128)}, f32[8,2,128]{2,1,0:T(2,128)S(1)}, ...), condition=%wide.region_26.27_spmd.clone, body=%wide.region_24.26_spmd.clone.sunk | while | flops 273877632 | bytes 12242637 | solution.py:290
  484.3 88.3 %while.53 = (s32[]{:T(128)}, f32[128,8,2,64]{0,3,2,1:T(8,128)}, bf16[4,512,512]{2,1,0:T(8,128)(2,1)}, bf16[4,512,512]{2,1,0:T(8,128)(2,1)}, s32[4]{0:T(128)S(1)}...) while((s32[]{:T(128)}, f32[128,8,2,64]{0,3,2,1:T(8,128)}, ...), condition=%wide.region_28.29_spmd.clone, body=%wide.region_27.28_spmd.clone.sunk | while | flops 682558080 | bytes 48992572 | solution.py:320
  496.2 4.1 fusion.242
  517.5 4.1 fusion.242
  539.9 4.1 fusion.242
  562.1 4.1 fusion.242
  574.9 5.5 bitcast_convert_fusion
  580.4 4.5 bitcast_convert_fusion.2
  585.0 4.6 bitcast_convert_fusion.1
  595.8 47.7 %reduce-scatter.13.cloned.1.call-done = bf16[128,512]{1,0:T(8,128)(2,1)} async-done(((bf16[2048,512]{1,0:T(8,128)(2,1)}), bf16[128,512]{1,0:T(8,128)(2,1)}) %reduce-scatter.13.cloned.1.call-update) | async-done | bytes 131088 | tf_op jit(solution)/shard_map/reduce_scatter | solution.py:324
  648.0 72.8 %reduce-scatter.15.cloned.1.call-done = bf16[128,512]{1,0:T(8,128)(2,1)} async-done(((bf16[2048,512]{1,0:T(8,128)(2,1)}), bf16[128,512]{1,0:T(8,128)(2,1)}) %reduce-scatter.15.cloned.1.call-update) | async-done | bytes 131088 | tf_op jit(solution)/shard_map/reduce_scatter | solution.py:330
  724.5 28.7 %reduce-scatter.31.cloned.1.call-done = bf16[128,32]{1,0:T(8,128)(2,1)} async-done(((bf16[1024,32]{1,0:T(8,128)(2,1)}), bf16[128,32]{1,0:T(8,128)(2,1)}) %reduce-scatter.31.cloned.1.call-update) | async-done | bytes 8208
  756.1 32.2 %reduce-scatter.29.cloned.1.call-done = bf16[2,64,1024]{2,1,0:T(8,128)(2,1)} async-done(((bf16[2,512,1024]{2,1,0:T(8,128)(2,1)}), bf16[2,64,1024]{2,1,0:T(8,128)(2,1)}) %reduce-scatter.29.cloned.1.call-update) | async-done | bytes 262160 | tf_op jit(solution)/shard_map/reduce_scatter | solution.py:391
  790.0 33.1 %reduce-scatter.25.cloned.1.call-done = bf16[2,128,512]{2,1,0:T(8,128)(2,1)} async-done(((bf16[2,1024,512]{2,1,0:T(8,128)(2,1)}), bf16[2,128,512]{2,1,0:T(8,128)(2,1)}) %reduce-scatter.25.cloned.1.call-update) | async-done | bytes 262160 | tf_op jit(solution)/shard_map/reduce_scatter | solution.py:385
  824.9 33.0 %reduce-scatter.27.cloned.1.call-done = bf16[2,128,512]{2,1,0:T(8,128)(2,1)} async-done(((bf16[2,1024,512]{2,1,0:T(8,128)(2,1)}), bf16[2,128,512]{2,1,0:T(8,128)(2,1)}) %reduce-scatter.27.cloned.1.call-update) | async-done | bytes 262160 | tf_op jit(solution)/shard_map/reduce_scatter | solution.py:388
  859.7 33.1 %reduce-scatter.17.cloned.1.call-done = bf16[128,1024]{1,0:T(8,128)(2,1)} async-done(((bf16[1024,1024]{1,0:T(8,128)(2,1)}), bf16[128,1024]{1,0:T(8,128)(2,1)}) %reduce-scatter.17.cloned.1.call-update) | async-done | bytes 262160 | tf_op jit(solution)/shard_map/reduce_scatter | solution.py:356
  892.8 34.8 %reduce-scatter.23.cloned.1.call-done = bf16[128,1024]{1,0:T(8,128)(2,1)} async-done(((bf16[1024,1024]{1,0:T(8,128)(2,1)}), bf16[128,1024]{1,0:T(8,128)(2,1)}) %reduce-scatter.23.cloned.1.call-update) | async-done | bytes 262160 | tf_op jit(solution)/shard_map/reduce_scatter | solution.py:365
  927.6 33.1 %reduce-scatter.19.cloned.1.call-done = bf16[128,512]{1,0:T(8,128)(2,1)} async-done(((bf16[1024,512]{1,0:T(8,128)(2,1)}), bf16[128,512]{1,0:T(8,128)(2,1)}) %reduce-scatter.19.cloned.1.call-update) | async-done | bytes 131088 | tf_op jit(solution)/shard_map/reduce_scatter | solution.py:359
  960.7 33.2 %reduce-scatter.21.cloned.1.call-done = bf16[128,512]{1,0:T(8,128)(2,1)} async-done(((bf16[1024,512]{1,0:T(8,128)(2,1)}), bf16[128,512]{1,0:T(8,128)(2,1)}) %reduce-scatter.21.cloned.1.call-update) | async-done | bytes 131088 | tf_op jit(solution)/shard_map/reduce_scatter | solution.py:362
  996.0 12.8 %all-reduce.4 = (bf16[1024]{0:T(1024)(128)(2,1)S(1)}, bf16[1024]{0:T(1024)(128)(2,1)S(1)}) all-reduce(bf16[1024]{0:T(1024)(128)(2,1)S(1)} %get-tuple-element.548, bf16[1024]{0:T(1024)(128)(2,1)} %get-tuple-element.546), channel_id=4, replica_groups=mesh['dp'=8,'expert'=16] {'dp'}, use_global_device_ids=true, to_apply=%region_33.34.clone | all-reduce | flops 2048 | bytes 8192
  1009.0 41.6 %all-reduce.2 = (bf16[128]{0:T(256)(128)(2,1)S(1)}, bf16[128]{0:T(256)(128)(2,1)S(1)}, bf16[128,32]{0,1:T(8,128)(2,1)S(1)}) all-reduce(bf16[128]{0:T(256)(128)(2,1)S(1)} %dynamic-slice.2, bf16[128]{0:T(256)(128)(2,1)S(1)} %dynamic-slice.4, bf16[128,32]{0,1:T(8,128)(2,1)S(1)} %copy.154), channel_id=1, replica_groups=mesh['dp'=8,'expert'=16] {'expert'}, use_global_device_ids=true, to_apply=%region_34.35 | all-reduce | flops 4352 | bytes 17408 | tf_op jit(solution)/shard_map/psum | solution.py:376
  1053.9 29.5 %all-reduce.7.cloned.1.call-done = (bf16[128,1024]{1,0:T(8,128)(2,1)}, bf16[128,512]{1,0:T(8,128)(2,1)}, bf16[128,512]{1,0:T(8,128)(2,1)}, bf16[128,1024]{1,0:T(8,128)(2,1)}) async-done(((bf16[128,1024]{1,0:T(8,128)(2,1)}, bf16[128,512]{1,0:T(8,128)(2,1)}, bf16[128,512]{1,0:T(8,128)(2,1)}, bf16[128,1024]{1,0:T(8,128)(2,1)}), (bf16[128,1024]{1,0:T(8,128)(2,1)}, bf16[128,512]{1,0:T(8,128)(2,1)}, ...) | async-done | bytes 786448 | tf_op jit(solution)/shard_map/psum | solution.py:377
  (497 shorter events, 239.7 us)
Async XLA Ops:
  7.2 30.0 %copy-start.1 = (bf16[1,128,1024]{2,1,0:T(8,128)(2,1)S(1)}, bf16[1,128,1024]{2,1,0:T(8,128)(2,1)}, u32[]{:S(2)}) copy-start(bf16[1,128,1024]{2,1,0:T(8,128)(2,1)} %param.22) | copy-start | bytes 786436
  7.2 28.5 %all-gather.16.cloned.1.call-start = ((), (), s32[]{:S(2)}) async-start(), calls=%async_computation.16 | async-start | bytes 1179648 | tf_op jit(solution)/shard_map/all_gather | solution.py:88
  7.9 52.7 %all-gather.12.cloned.1.call-start = ((), (), s32[]{:S(2)}) async-start(), calls=%async_computation.14 | async-start | bytes 1179648 | tf_op jit(solution)/shard_map/all_gather | solution.py:89
  8.7 80.8 %all-gather.20.cloned.1.call-start = ((), (), s32[]{:S(2)}) async-start(), calls=%async_computation.18 | async-start | bytes 2359296 | tf_op jit(solution)/shard_map/all_gather | solution.py:87
  9.4 128.7 %all-gather.18.cloned.1.call-start = ((), (), s32[]{:S(2)}) async-start(), calls=%async_computation.17 | async-start | bytes 2228224 | tf_op jit(solution)/shard_map/all_gather | solution.py:123
  11.2 82.0 %copy-start.25 = (f32[128,64]{0,1:T(8,128)}, f32[128,64]{0,1:T(8,128)S(1)}, u32[]{:S(2)}) copy-start(f32[128,64]{0,1:T(8,128)S(1)} %get-tuple-element.649) | copy-start | bytes 98308
  11.3 81.9 %copy-start.30 = (f32[128,64]{0,1:T(8,128)}, f32[128,64]{0,1:T(8,128)S(1)}, u32[]{:S(2)}) copy-start(f32[128,64]{0,1:T(8,128)S(1)} %sin.3) | copy-start | bytes 98308
  22.4 70.0 %copy-start.33 = (f32[8,1,128]{2,1,0:T(1,128)}, f32[8,1,128]{2,1,0:T(1,128)S(1)}, u32[]{:S(2)}) copy-start(f32[8,1,128]{2,1,0:T(1,128)S(1)} %convert_element_type.303) | copy-start | bytes 12292
  23.5 39.4 %copy-start.60 = (f32[128]{0:T(128)}, f32[128]{0:T(128)S(1)}, u32[]{:S(2)}) copy-start(f32[128]{0:T(128)S(1)} %fusion.78) | copy-start | bytes 1540
  23.5 68.9 %copy-start.46 = (f32[128]{0:T(128)}, f32[128]{0:T(128)S(1)}, u32[]{:S(2)}) copy-start(f32[128]{0:T(128)S(1)} %fusion.117) | copy-start | bytes 1540
  37.1 28.5 %copy-start.49 = (s32[1,128,8]{1,2,0:T(8,128)S(1)}, s32[1,128,8]{1,2,0:T(8,128)}, u32[]{:S(2)}) copy-start(s32[1,128,8]{1,2,0:T(8,128)} %param.24) | copy-start | bytes 12292
  37.2 28.8 %copy-start.61 = (bf16[128]{0:T(256)(128)(2,1)S(1)}, bf16[128]{0:T(256)(128)(2,1)}, u32[]{:S(2)}) copy-start(bf16[128]{0:T(256)(128)(2,1)} %param.30) | copy-start | bytes 772
  38.4 146.8 %all-gather.14.cloned.1.call-start = ((), (), s32[]{:S(2)}) async-start(), calls=%async_computation.15 | async-start | bytes 2228224 | tf_op jit(solution)/shard_map/all_gather | solution.py:124
  62.9 156.4 %all-gather.22.cloned.1.call-start = ((), (), s32[]{:S(2)}) async-start(), calls=%async_computation.19 | async-start | bytes 2359296 | tf_op jit(solution)/shard_map/all_gather | solution.py:90
  63.5 178.1 %all-gather.24.cloned.1.call-start = ((), (), s32[]{:S(2)}) async-start(), calls=%async_computation.20 | async-start | bytes 2359296 | tf_op jit(solution)/shard_map/all_gather | solution.py:96
  64.2 208.3 %all-gather.26.cloned.1.call-start = ((), (), s32[]{:S(2)}) async-start(), calls=%async_computation.21 | async-start | bytes 2359296 | tf_op jit(solution)/shard_map/all_gather | solution.py:97
  75.1 146.5 %copy-start.42 = (f32[8,1,128]{2,1,0:T(1,128)}, f32[8,1,128]{2,1,0:T(1,128)S(1)}, u32[]{:S(2)}) copy-start(f32[8,1,128]{2,1,0:T(1,128)S(1)} %convert_element_type.304) | copy-start | bytes 12292
  89.4 133.0 %copy-start.22 = (pred[1280,128]{1,0:T(8,128)(4,1)}, pred[1280,128]{1,0:T(8,128)(4,1)S(1)}, u32[]{:S(2)}) copy-start(pred[1280,128]{1,0:T(8,128)(4,1)S(1)} %fusion.37) | copy-start | bytes 491524
  225.6 41.4 %all-to-all-start = ((bf16[16,2,40,1024]{3,2,1,0:T(8,128)(2,1)}), bf16[16,2,40,1024]{3,2,1,0:T(8,128)(2,1)S(1)}, u32[]{:S(2)}, u32[]{:S(2)}) async-start(bf16[16,2,40,1024]{3,2,1,0:T(8,128)(2,1)} %bitcast.23), calls=%async_computation | async-start | bytes 5242880 | tf_op jit(solution)/shard_map/all_to_all | solution.py:197
  230.6 62.5 %all-gather.28.cloned.1.call-start = ((), (), s32[]{:S(2)}) async-start(), calls=%async_computation.22 | async-start | bytes 2359296 | tf_op jit(solution)/shard_map/all_gather | solution.py:98
  298.4 47.9 %all-to-all-start.1 = ((bf16[16,2,40,1024]{3,2,1,0:T(8,128)(2,1)}), bf16[16,2,40,1024]{3,2,1,0:T(8,128)(2,1)S(1)}, u32[]{:S(2)}, u32[]{:S(2)}) async-start(bf16[16,2,40,1024]{3,2,1,0:T(8,128)(2,1)} %copy.119), calls=%async_computation.1 | async-start | bytes 5242880 | tf_op jit(solution)/shard_map/all_to_all | solution.py:209
  305.7 22.5 %copy-start.48 = (s32[1024,1]{0,1:T(1,128)}, s32[1024,1]{0,1:T(1,128)S(1)}, u32[]{:S(2)}) copy-start(s32[1024,1]{0,1:T(1,128)S(1)} %compare_select_fusion.1) | copy-start | bytes 12292
  359.0 40.9 %copy-start.69 = (f32[2,16,40,512]{3,2,1,0:T(8,128)S(1)}, f32[2,16,40,512]{3,2,1,0:T(8,128)}, u32[]{:S(2)}) copy-start(f32[2,16,40,512]{3,2,1,0:T(8,128)} %get-tuple-element.678) | copy-start | bytes 7864324
  362.0 37.8 %copy-start.64 = (bf16[2,512,1024]{2,1,0:T(8,128)(2,1)S(1)}, bf16[2,512,1024]{2,1,0:T(8,128)(2,1)}, u32[]{:S(2)}) copy-start(bf16[2,512,1024]{2,1,0:T(8,128)(2,1)} %all-gather.28.cloned.1.call-done) | copy-start | bytes 6291460
  362.0 37.8 %copy-start.68 = (f32[2,16,40,512]{3,2,1,0:T(8,128)S(1)}, f32[2,16,40,512]{3,2,1,0:T(8,128)}, u32[]{:S(2)}) copy-start(f32[2,16,40,512]{3,2,1,0:T(8,128)} %fusion.54) | copy-start | bytes 7864324
  408.3 40.2 %all-to-all-start.3 = ((bf16[16,2,40,1024]{3,2,1,0:T(8,128)(2,1)}), bf16[16,2,40,1024]{3,2,1,0:T(8,128)(2,1)}, u32[]{:S(2)}, u32[]{:S(2)}) async-start(bf16[16,2,40,1024]{3,2,1,0:T(8,128)(2,1)} %copy.123), calls=%async_computation.3 | async-start | bytes 5242880 | tf_op jit(solution)/shard_map/all_to_all | solution.py:264
  412.9 230.6 %reduce-scatter.13.cloned.1.call-start = ((), (), s32[]{:S(2)}) async-start(), calls=%async_computation.23 | async-start | bytes 2228224 | tf_op jit(solution)/shard_map/reduce_scatter | solution.py:324
  414.1 36.9 %copy-start.10 = (f32[128,1024]{1,0:T(8,128)S(1)}, f32[128,1024]{1,0:T(8,128)}, u32[]{:S(2)}) copy-start(f32[128,1024]{1,0:T(8,128)} %copy-done.9) | copy-start | bytes 1572868
  414.1 36.9 %copy-start.41 = (bf16[128,32]{0,1:T(8,128)(2,1)S(1)}, bf16[128,32]{0,1:T(8,128)(2,1)}, u32[]{:S(2)}) copy-start(bf16[128,32]{0,1:T(8,128)(2,1)} %multiply_convert_fusion.2) | copy-start | bytes 24580
  414.1 36.9 %copy-start.43 = (f32[8,1,128]{2,1,0:T(1,128)S(1)}, f32[8,1,128]{2,1,0:T(1,128)}, u32[]{:S(2)}) copy-start(f32[8,1,128]{2,1,0:T(1,128)} %copy-done.42) | copy-start | bytes 12292
  414.1 36.9 %copy-start.59 = (f32[128]{0:T(128)S(1)}, f32[128]{0:T(128)}, u32[]{:S(2)}) copy-start(f32[128]{0:T(128)} %copy-done.58) | copy-start | bytes 1540
  416.4 35.5 %copy-start.63 = (f32[128]{0:T(128)S(1)}, f32[128]{0:T(128)}, u32[]{:S(2)}) copy-start(f32[128]{0:T(128)} %copy-done.62) | copy-start | bytes 1540
  416.4 35.5 %copy-start.29 = (bf16[1,128,1024]{2,1,0:T(8,128)(2,1)S(1)}, bf16[1,128,1024]{2,1,0:T(8,128)(2,1)}, u32[]{:S(2)}) copy-start(bf16[1,128,1024]{2,1,0:T(8,128)(2,1)} %param.35) | copy-start | bytes 786436
  572.7 148.1 %reduce-scatter.15.cloned.1.call-start = ((), (), s32[]{:S(2)}) async-start(), calls=%async_computation.24 | async-start | bytes 2228224 | tf_op jit(solution)/shard_map/reduce_scatter | solution.py:330
  573.4 179.8 %reduce-scatter.31.cloned.1.call-start = ((), (), s32[]{:S(2)}) async-start(), calls=%async_computation.32 | async-start | bytes 294912
  574.6 213.6 %reduce-scatter.29.cloned.1.call-start = ((), (), s32[]{:S(2)}) async-start(), calls=%async_computation.31 | async-start | bytes 2359296 | tf_op jit(solution)/shard_map/reduce_scatter | solution.py:391
  580.3 242.7 %reduce-scatter.25.cloned.1.call-start = ((), (), s32[]{:S(2)}) async-start(), calls=%async_computation.29 | async-start | bytes 2359296 | tf_op jit(solution)/shard_map/reduce_scatter | solution.py:385
  584.9 273.0 %reduce-scatter.27.cloned.1.call-start = ((), (), s32[]{:S(2)}) async-start(), calls=%async_computation.30 | async-start | bytes 2359296 | tf_op jit(solution)/shard_map/reduce_scatter | solution.py:388
  589.6 303.2 %reduce-scatter.17.cloned.1.call-start = ((), (), s32[]{:S(2)}) async-start(), calls=%async_computation.25 | async-start | bytes 2359296 | tf_op jit(solution)/shard_map/reduce_scatter | solution.py:356
  593.5 334.2 %reduce-scatter.23.cloned.1.call-start = ((), (), s32[]{:S(2)}) async-start(), calls=%async_computation.28 | async-start | bytes 2359296 | tf_op jit(solution)/shard_map/reduce_scatter | solution.py:365
  595.6 365.2 %reduce-scatter.19.cloned.1.call-start = ((), (), s32[]{:S(2)}) async-start(), calls=%async_computation.26 | async-start | bytes 1179648 | tf_op jit(solution)/shard_map/reduce_scatter | solution.py:359
  646.4 76.9 %copy-start.65 = (u32[128]{0:T(128)S(1)}, u32[128]{0:T(128)}, u32[]{:S(2)}) copy-start(u32[128]{0:T(128)} %constant.180) | copy-start | bytes 1540
  647.9 107.3 %copy-start.5 = (bf16[1024,1024]{1,0:T(8,128)(2,1)S(1)}, bf16[1024,1024]{1,0:T(8,128)(2,1)}, u32[]{:S(2)}) copy-start(bf16[1024,1024]{1,0:T(8,128)(2,1)} %all-gather.20.cloned.1.call-done) | copy-start | bytes 6291460
  647.9 346.1 %reduce-scatter.21.cloned.1.call-start = ((), (), s32[]{:S(2)}) async-start(), calls=%async_computation.27 | async-start | bytes 1179648 | tf_op jit(solution)/shard_map/reduce_scatter | solution.py:362
  723.2 360.2 %all-reduce.7.cloned.1.call-start = ((), (), s32[]{:S(2)}) async-start(), calls=%async_computation.33 | async-start | bytes 1572864 | tf_op jit(solution)/shard_map/psum | solution.py:377
  755.2 238.8 %copy-start.28 = (bf16[128,512]{1,0:T(8,128)(2,1)S(1)}, bf16[128,512]{1,0:T(8,128)(2,1)}, u32[]{:S(2)}) copy-start(bf16[128,512]{1,0:T(8,128)(2,1)} %copy-done.27) | copy-start | bytes 393220
  756.0 238.0 %copy-start.11 = (bf16[1024,512]{1,0:T(8,128)(2,1)S(1)}, bf16[1024,512]{1,0:T(8,128)(2,1)}, u32[]{:S(2)}) copy-start(bf16[1024,512]{1,0:T(8,128)(2,1)} %all-gather.16.cloned.1.call-done) | copy-start | bytes 3145732
  756.1 238.5 %copy-start.12 = (bf16[1024,512]{1,0:T(8,128)(2,1)S(1)}, bf16[1024,512]{1,0:T(8,128)(2,1)}, u32[]{:S(2)}) copy-start(bf16[1024,512]{1,0:T(8,128)(2,1)} %all-gather.12.cloned.1.call-done) | copy-start | bytes 3145732
  (54 other events, 227.0 us)
Sparse Core Ops, SparseCore 0:
  9.7 25.8 all-gather.15
  37.4 23.2 all-gather.11
  62.3 25.0 all-gather.19
  90.0 48.0 all-gather.17
  140.6 44.5 all-gather.13
  186.8 24.4 all-gather.21
  213.0 25.6 all-gather.23
  240.4 25.4 all-gather.25
  267.6 25.4 all-gather.27
  572.8 70.6 reduce-scatter.12
  647.1 73.5 reduce-scatter.14
  723.5 29.6 reduce-scatter.30
  755.8 32.4 reduce-scatter.28
  790.6 32.4 reduce-scatter.24
  825.5 32.4 reduce-scatter.26
  860.3 32.4 reduce-scatter.16
  895.2 32.4 reduce-scatter.22
  930.0 30.6 reduce-scatter.18
  963.3 30.6 reduce-scatter.20
  997.9 85.4 all-reduce.6
where the time goes:
time: 1100 us
  waiting for transfers between devices  585 us (53%)
  matrix products  125 us (11%)
  blocking collectives  124 us (11%)
  local copies, waits for them, and re-layouts  113 us (10%)
  other arithmetic  73.4 us (7%)
  loops' own time  32.1 us (3%)
  starting transfers between devices  28.8 us (3%)
  between operations  16.5 us (2%)
    reduce_scatter x1, waiting for transfers between devices, per_device(): lax.psum_scatter(value_terms.reshape(length, kv_width).astype(jnp.bfloat1...  72.8 us
    reduce_scatter x1, waiting for transfers between devices, per_device(): lax.psum_scatter(key_terms.reshape(length, kv_width).astype(jnp.bfloat16)...  47.7 us
    all_gather x1, waiting for transfers between devices, per_device(): lax.all_gather(key_rot, 'expert', axis=0, tiled=True)  44.8 us
    psum x1, blocking collectives, per_device(): lax.psum(shard_sums[0].astype(jnp.bfloat16), 'expert').astype(jnp.float32)  41.6 us
    all_to_all x1, blocking collectives, per_device(): lax.all_to_all(slot_grad, 'expert', split_axis=0, concat_axis=0, tiled=True)  37.8 us
    reduce_scatter x1, waiting for transfers between devices, per_device(): lax.psum_scatter(grad_w_out.astype(jnp.bfloat16), 'dp', scatter_dimension...  34.8 us
    unnamed x21, waiting for transfers between devices  33.6 us
    reduce_scatter x1, waiting for transfers between devices, per_device(): lax.psum_scatter(grad_w_value.astype(jnp.bfloat16), 'dp', scatter_dimensi...  33.2 us
  transfers between devices with their start and end apart: 23, of which 19 were waited for; matrix products, arithmetic and copies ran while one was open for 15% of the time, Pallas kernels for 0%

commit v1 on v0

v1 whole, which is shorter than its diff:
```python
import jax
import jax.numpy as jnp
from jax import lax
from jax.experimental import pallas as pl
from jax.experimental.pallas import tpu as pltpu
from jax.sharding import PartitionSpec as P

D = 1024
HEADS = 16
HD = 64
EF = 512
EXPERTS = 32
CAP = 40
TOK = 128
SEQ = 2048
SIDE = 4
PEERS = 16
DP = 8
QB = 512
ROWS = PEERS * CAP
EXTRA = 16
PACK = 1152
WIDE = 3072

eps = 1e-06
theta = 10000.0
masked = -1000000000.0
bf16 = jnp.bfloat16
f32 = jnp.float32
MIB = 1 << 20

VM = pl.BlockSpec(memory_space=pltpu.VMEM)
SM = pl.BlockSpec(memory_space=pltpu.SMEM)
HB = pl.BlockSpec(memory_space=pl.ANY)
NN = (((1,), (0,)), ((), ()))
NT = (((1,), (1,)), ((), ()))
TN = (((0,), (0,)), ((), ()))


def mm(left, right, dims=NN):
    return lax.dot_general(left, right, dims, preferred_element_type=f32)


def shape(dims, dtype):
    return jax.ShapeDtypeStruct(dims, dtype)


def run(kernel, name, outs, ins, specs, scratch=(), limit=24, flops=0, moved=0):
    return pl.pallas_call(
        kernel,
        name=name,
        out_shape=outs,
        in_specs=specs,
        out_specs=jax.tree.map(lambda _: VM, outs),
        scratch_shapes=scratch,
        compiler_params=pltpu.CompilerParams(vmem_limit_bytes=limit * MIB),
        cost_estimate=pl.CostEstimate(flops=flops, bytes_accessed=moved, transcendentals=0),
    )(*ins)


def expert_from(values, dz, dx):
    pairs = [
        (z * SIDE + x, ((z - dz) % SIDE) * SIDE + (x - dx) % SIDE)
        for z in range(SIDE)
        for x in range(SIDE)
    ]
    return lax.ppermute(values, "expert", pairs)


def dp_from(values, dy):
    pairs = [(y * 2 + c, ((y - dy) % SIDE) * 2 + c) for y in range(SIDE) for c in range(2)]
    return lax.ppermute(values, "dp", pairs)


def core_swap(values):
    return lax.ppermute(values, "dp", [(d, d ^ 1) for d in range(DP)])


def gather_z(values):
    far = {m: expert_from(values, m, 0) for m in (1, 3, 2)}
    return [values, far[1], far[2], far[3]]


def gather_x(values):
    far = {m: expert_from(values, 0, m) for m in (1, 3, 2)}
    return [values, far[1], far[2], far[3]]


def gather_dp(values):
    far = {m: dp_from(values, m) for m in (1, 3, 2)}
    mine = [values, far[1], far[2], far[3]]
    return mine + [core_swap(part) for part in mine]


def reduce_dp(mine, other):
    swapped = core_swap(other)
    pairs = [(mine[m].astype(f32) + swapped[m].astype(f32)).astype(bf16) for m in range(SIDE)]
    total = pairs[0].astype(f32)
    for m in (1, 3, 2):
        total = total + dp_from(pairs[m], SIDE - m).astype(f32)
    return total


def swap_all(values):
    return lax.all_to_all(values, "expert", split_axis=0, concat_axis=0, tiled=True)


def part_place(info, r):
    return ((info[2] + r % SIDE) % SIDE) * 2 + (info[3] ^ (r // SIDE))


def rotated(values, c, s):
    w1, w2 = values[: HD // 2], values[HD // 2 :]
    return jnp.concatenate([w1 * c - w2 * s, w2 * c + w1 * s], axis=0)


def rotated_back(values, c, s):
    w1, w2 = values[: HD // 2], values[HD // 2 :]
    return jnp.concatenate([w1 * c + w2 * s, w2 * c - w1 * s], axis=0)


def allowed(ki, qi, start):
    key = ki * QB + lax.broadcasted_iota(jnp.int32, (QB, QB), 0)
    keep = key >= start
    if ki == qi:
        keep = keep & (key <= qi * QB + lax.broadcasted_iota(jnp.int32, (QB, QB), 1))
    return keep


def attend_kernel(info, *refs):
    a, b, parts = refs[0:4], refs[4:8], refs[8:16]
    cos, sin, start, normed, small, qz, kvt, out_t, lse, send = refs[16:26]
    w_block, w_turned, kvn, sems = refs[26:30]
    z, x = info[0], info[1]
    e = z * SIDE + x
    columns = (e // 2, 8 + e // 4, 12 + e // 4)
    copies = []
    for r in range(8):
        place = pl.multiple_of(part_place(info, r) * TOK, TOK)
        for j in range(3):
            copies.append(
                pltpu.make_async_copy(
                    parts[r].at[pl.ds(0, TOK), pl.ds(pl.multiple_of(columns[j] * 128, 128), 128)],
                    w_block.at[j, pl.ds(place, TOK), :],
                    sems.at[r * 6 + j],
                )
            )
            copies.append(
                pltpu.make_async_copy(
                    parts[r].at[pl.ds(TOK, EXTRA), pl.ds(j * 128, 128)],
                    small.at[pl.ds(j * EXTRA, EXTRA), pl.ds(place, 128)],
                    sems.at[r * 6 + 3 + j],
                )
            )
    for copy in copies:
        copy.start()
    for copy in copies:
        copy.wait()
    gain = small[2 * EXTRA : 3 * EXTRA, :].astype(f32)[0:1, :]
    for mz in range(SIDE):
        for mx in range(SIDE):
            block = ((z + mz) % SIDE) * SIDE + (x + mx) % SIDE
            rows = pl.ds(pl.multiple_of(block * TOK, TOK), TOK)
            left = a[mz][mx * TOK : (mx + 1) * TOK, :].astype(f32)
            right = b[mx][mz * TOK : (mz + 1) * TOK, :].astype(f32)
            square = jnp.sum(left * left + right * right, axis=-1, keepdims=True)
            r = lax.rsqrt(square * (1.0 / D) + eps)
            normed[rows, 0:512] = (left * r * gain[:, 0:512]).astype(bf16)
            normed[rows, 512:1024] = (right * r * gain[:, 512:1024]).astype(bf16)
    halves = (e % 2, (e // 2) % 2, (e // 2) % 2)
    for j in range(3):
        w_turned[j] = w_block[j].astype(f32).T.astype(bf16)
    w_head = jnp.concatenate(
        [w_turned[j, pl.ds(pl.multiple_of(halves[j] * HD, HD), HD), :] for j in range(3)], axis=0
    )
    for i in range(SEQ // QB):
        span = slice(i * QB, (i + 1) * QB)
        turned = mm(w_head, normed[span, :], NT)
        c, s = cos[:, span], sin[:, span]
        query = rotated(turned[0:HD], c, s).astype(bf16).astype(f32) * (HD**-0.5)
        key = rotated(turned[HD : 2 * HD], c, s)
        both = jnp.concatenate([key, turned[2 * HD : 3 * HD]], axis=0).astype(bf16)
        qz[0:HD, span] = query.astype(bf16)
        qz[HD:128, span] = jnp.zeros((HD, QB), bf16)
        kvt[:, span] = both
        kvn[span, :] = both.astype(f32).T.astype(bf16)
    for qi in range(SEQ // QB):
        span = slice(qi * QB, (qi + 1) * QB)
        query = qz[:, span]
        top = jnp.full((1, QB), -jnp.inf, f32)
        total = jnp.zeros((1, QB), f32)
        mixed = jnp.zeros((HD, QB), f32)
        for ki in range(qi, -1, -1):
            keys = slice(ki * QB, (ki + 1) * QB)
            scores = jnp.where(allowed(ki, qi, start[:, span]), mm(kvn[keys, :], query), masked)
            higher = jnp.maximum(top, jnp.max(scores, axis=0, keepdims=True))
            weights = jnp.exp(scores - higher)
            shrink = jnp.exp(top - higher)
            total = total * shrink + jnp.sum(weights, axis=0, keepdims=True)
            mixed = mixed * shrink + mm(kvt[HD:128, keys], weights.astype(bf16))
            top = higher
        mixed = mixed / total
        lse[:, span] = top + jnp.log(total)
        out_t[:, span] = mixed
        for j in range(QB // TOK):
            send[qi * (QB // TOK) + j] = mixed[:, j * TOK : (j + 1) * TOK].astype(bf16)


def load_rows(info, parts, column, width, target, sems):
    copies = []
    for r in range(8):
        place = pl.multiple_of(part_place(info, r) * TOK, TOK)
        copies.append(
            pltpu.make_async_copy(
                parts[r].at[pl.ds(0, TOK), pl.ds(column, width)],
                target.at[pl.ds(place, TOK), :],
                sems.at[r],
            )
        )
    return copies


def project_kernel(info, *refs):
    mixed_t, states, small, table = refs[0:4]
    parts = refs[4:12]
    hidden, send, w_out, sems = refs[12:16]
    copies = load_rows(info, parts, 2048, D, w_out, sems)
    for copy in copies:
        copy.start()
    mixed = mixed_t[...].astype(f32).T.astype(bf16)
    for copy in copies:
        copy.wait()
    gain = small[2 * EXTRA : 3 * EXTRA, :].astype(f32)[1:2, :]
    value = states[...].astype(f32) + mm(mixed, w_out[...])
    hidden[...] = value
    r = lax.rsqrt(jnp.mean(value * value, axis=-1, keepdims=True) + eps)
    ffn = (value * r * gain).astype(bf16)
    send[...] = mm(table[...], ffn).astype(bf16)


def unweave(source, spread, target):
    for s in range(PEERS):
        rows = source[s * 2 * CAP : (s + 1) * 2 * CAP, :].astype(f32)
        spread[0, s * CAP : (s + 1) * CAP, :] = rows[0:CAP]
        spread[1, s * CAP : (s + 1) * CAP, :] = rows[CAP : 2 * CAP]
    for i in range(2):
        target[i] = spread[i].astype(bf16)


def weave(spread, target):
    for s in range(PEERS):
        rows = slice(s * CAP, (s + 1) * CAP)
        target[s * 2 * CAP : (s + 1) * 2 * CAP, :] = jnp.concatenate(
            [spread[0, rows, :], spread[1, rows, :]], axis=0
        ).astype(bf16)


def expert_kernel(info, *refs):
    arrived, arrived_grad, small = refs[0:3]
    parts = refs[3:11]
    sent, xs, gs, acted, dgate, dup, gates, lgs = refs[11:19]
    spread, wg, wu, wd, sems = refs[19:24]
    copies = []
    for r in range(8):
        d = part_place(info, r)
        rows = pl.ds(pl.multiple_of(d * TOK, TOK), TOK)
        half = pl.ds(pl.multiple_of(d * HD, HD), HD)
        part = parts[r]
        for k, (first, count, target) in enumerate(
            (
                (0, 128, wg.at[:, rows, :]),
                (128, 128, wu.at[:, rows, :]),
                (256, 64, wd.at[:, half, 0:512]),
                (320, 64, wd.at[:, half, 512:1024]),
            )
        ):
            copies.append(
                pltpu.make_async_copy(
                    part.at[:, pl.ds(first, count), :], target, sems.at[r * 4 + k]
                )
            )
    for copy in copies:
        copy.start()
    unweave(arrived, spread, xs)
    unweave(arrived_grad, spread, gs)
    for copy in copies:
        copy.wait()
    router = small[0 : 2 * EXTRA, :]
    first = (info[0] * SIDE + info[1]) * 2
    chunk = ROWS // 2

    def step(n, carry):
        i = n // 2
        rows = pl.ds(pl.multiple_of((n % 2) * chunk, chunk), chunk)
        x = xs[i, rows, :]
        logits = mm(x, router, NT)
        peak = jnp.max(logits, axis=-1, keepdims=True)
        chances = jnp.exp(logits - peak)
        chances = chances / jnp.sum(chances, axis=-1, keepdims=True)
        mine = (lax.broadcasted_iota(jnp.int32, (chunk, EXPERTS), 1) == first + i).astype(f32)
        gate = jnp.sum(chances * mine, axis=-1, keepdims=True)
        gate_pre = mm(x, wg[i])
        up_pre = mm(x, wu[i])
        sigmoid = 1.0 / (1.0 + jnp.exp(-gate_pre))
        silu = gate_pre * sigmoid
        act = (silu * up_pre).astype(bf16)
        acted[i, rows, :] = act
        back = mm(gs[i, rows, :], wd[i], NT)
        dot = jnp.sum(act.astype(f32) * back, axis=-1, keepdims=True)
        back = back * gate
        gate_grad = (back * up_pre * (sigmoid * (1.0 + gate_pre * (1.0 - sigmoid)))).astype(bf16)
        up_grad = (back * silu).astype(bf16)
        dgate[i, rows, :] = gate_grad
        dup[i, rows, :] = up_grad
        lg = (dot * gate * (mine - chances)).astype(bf16)
        lgs[i, rows, :] = lg
        gates[i, rows, :] = jnp.broadcast_to(gate, (chunk, 128))
        spread[i, rows, :] = (
            mm(gate_grad, wg[i], NT) + mm(up_grad, wu[i], NT) + mm(lg, router)
        )
        return carry

    lax.fori_loop(0, 4, step, 0)
    weave(spread, sent)


def weights_kernel(info, *refs):
    xs, gs, acted, dgate, dup, gates, lgs = refs[0:7]
    parts = refs[7:15]
    returned, mine, other, router_grad = refs[15:19]
    spread, wd, sums, down_sums, sems = refs[19:24]
    copies = []
    for r in range(8):
        half = pl.ds(pl.multiple_of(part_place(info, r) * HD, HD), HD)
        for k in range(2):
            copies.append(
                pltpu.make_async_copy(
                    parts[r].at[:, pl.ds(256 + 64 * k, 64), :],
                    wd.at[:, half, k * 512 : (k + 1) * 512],
                    sems.at[r * 2 + k],
                )
            )
    for copy in copies:
        copy.start()
    for copy in copies:
        copy.wait()
    router_grad[...] = jnp.zeros_like(router_grad)

    def step(i, carry):
        x = xs[i]
        gate = gates[i][:, 0:1]
        spread[i] = mm(acted[i], wd[i]) * gate
        slot_grad = (gs[i].astype(f32) * gate).astype(bf16)
        router_grad[...] += mm(lgs[i], x, TN)
        sums[0] = mm(x, dgate[i], TN).astype(bf16)
        sums[1] = mm(x, dup[i], TN).astype(bf16)
        down_sums[...] = mm(acted[i], slot_grad, TN).astype(bf16)
        for r in range(8):
            d = part_place(info, r)
            rows = pl.ds(pl.multiple_of(d * TOK, TOK), TOK)
            half = pl.ds(pl.multiple_of(d * HD, HD), HD)
            target = mine if r < SIDE else other
            m = r % SIDE
            target[m, i, 0:128, :] = sums[0, rows, :]
            target[m, i, 128:256, :] = sums[1, rows, :]
            target[m, i, 256:320, :] = down_sums[half, 0:512]
            target[m, i, 320:384, :] = down_sums[half, 512:1024]
        return carry

    lax.fori_loop(0, 2, step, 0)
    weave(spread, returned)


def hidden_kernel(info, *refs):
    arrived, table_t, hidden_ref, cot, small = refs[0:5]
    parts = refs[5:13]
    hidden_grad, low, send, gain_grad, w_out, sems = refs[13:19]
    copies = load_rows(info, parts, 2048, D, w_out, sems)
    for copy in copies:
        copy.start()
    grad = mm(table_t[...], arrived[...])
    hidden = hidden_ref[...]
    gain = small[2 * EXTRA : 3 * EXTRA, :].astype(f32)[1:2, :]
    r = lax.rsqrt(jnp.mean(hidden * hidden, axis=-1, keepdims=True) + eps)
    scaled = grad * gain
    dot = jnp.mean(scaled * hidden, axis=-1, keepdims=True)
    total = cot[...].astype(f32) + r * scaled - hidden * (r * r * r * dot)
    gain_grad[...] = jnp.sum(grad * hidden * r, axis=0, keepdims=True)
    hidden_grad[...] = total
    low[...] = total.astype(bf16)
    for copy in copies:
        copy.wait()
    turned = mm(w_out[...], low[...], NT).astype(bf16)
    send[...] = turned.reshape(HEADS, HD, TOK)


def out_weights_kernel(info, *refs):
    mixed_t, low, router_grad, gain_grad = refs[0:4]
    mine, other, extra = refs[4:7]
    block = jnp.concatenate(
        [router_grad[...], jnp.broadcast_to(gain_grad[...], (8, D)), jnp.zeros((88, D), f32)],
        axis=0,
    )
    extra[...] = block.T
    for r in range(8):
        rows = pl.ds(pl.multiple_of(part_place(info, r) * TOK, TOK), TOK)
        target = mine if r < SIDE else other
        target[r % SIDE, :, 0:D] = mm(mixed_t[rows, :], low[...]).astype(bf16)
        target[r % SIDE, :, D:PACK] = extra[rows, :].astype(bf16)


def attend_back_kernel(info, *refs):
    qz, kvt, out_t, lse, arrived, cos, sin, start, normed = refs[0:9]
    send, mine, other = refs[9:12]
    kvn, oz, qon, dq, low, delta, sums = refs[12:19]
    steps = SEQ // QB
    for i in range(steps):
        span = slice(i * QB, (i + 1) * QB)
        kvn[span, :] = kvt[:, span].astype(f32).T.astype(bf16)
        got = jnp.concatenate([arrived[i * 4 + j] for j in range(4)], axis=1)
        oz[0:HD, span] = jnp.zeros((HD, QB), bf16)
        oz[HD:128, span] = got
        wide = got.astype(f32)
        delta[:, span] = jnp.sum(wide * out_t[:, span], axis=0, keepdims=True)
        qon[span, :] = jnp.concatenate([qz[0:HD, span].astype(f32), wide], axis=0).T.astype(bf16)
        dq[:, span] = jnp.zeros((HD, QB), f32)
    for ki in range(steps):
        keys = slice(ki * QB, (ki + 1) * QB)
        value_sum = jnp.zeros((QB, 128), f32)
        key_sum = jnp.zeros((QB, 128), f32)
        for qi in range(ki, steps):
            span = slice(qi * QB, (qi + 1) * QB)
            scores = mm(kvn[keys, :], qz[:, span])
            expo = jnp.where(
                allowed(ki, qi, start[:, span]), jnp.exp(scores - lse[:, span]), 0.0
            )
            back = mm(kvn[keys, :], oz[:, span])
            score_grad = (expo * (back - delta[:, span])).astype(bf16)
            value_sum = value_sum + mm(expo.astype(bf16), qon[span, :])
            key_sum = key_sum + mm(score_grad, qon[span, :])
            dq[:, span] += mm(kvt[0:HD, keys], score_grad)
        lane = lax.broadcasted_iota(jnp.int32, (QB, 128), 1)
        turned = jnp.where(lane < HD, key_sum, value_sum).T
        low[HD : 2 * HD, keys] = rotated_back(turned[0:HD], cos[:, keys], sin[:, keys]).astype(bf16)
        low[2 * HD : 3 * HD, keys] = turned[HD:128].astype(bf16)
    for i in range(steps):
        span = slice(i * QB, (i + 1) * QB)
        low[0:HD, span] = rotated_back(
            dq[:, span] * (HD**-0.5), cos[:, span], sin[:, span]
        ).astype(bf16)
    for j in range(PEERS):
        send[j] = low[:, j * TOK : (j + 1) * TOK]
    total = mm(low[...], normed[...]).astype(bf16)
    for d in range(DP):
        sums[d] = total[:, d * TOK : (d + 1) * TOK]
    for r in range(8):
        target = mine if r < SIDE else other
        target[r % SIDE] = sums[part_place(info, r)]


def input_kernel(info, *refs):
    arrived, hidden_grad, states, small = refs[0:4]
    parts = refs[4:12]
    grad, wide, sems = refs[12:15]
    copies = load_rows(info, parts, 0, 2048, wide, sems)
    for copy in copies:
        copy.start()
    turned = arrived[...].astype(f32)
    dq = turned[:, 0:HD].reshape(HEADS * HD, TOK).T.astype(bf16)
    pairs = turned[:, HD : 3 * HD].reshape(HEADS // 2, 2, 2 * HD, TOK)
    pairs = pairs[:, 0] + pairs[:, 1]
    dk = pairs[:, 0:HD].reshape(512, TOK).T.astype(bf16)
    dv = pairs[:, HD : 2 * HD].reshape(512, TOK).T.astype(bf16)
    for copy in copies:
        copy.wait()
    back = (
        mm(dq, wide[:, 0:1024], NT)
        + mm(dk, wide[:, 1024:1536], NT)
        + mm(dv, wide[:, 1536:2048], NT)
    )
    x = states[...].astype(f32)
    gain = small[2 * EXTRA : 3 * EXTRA, :].astype(f32)[0:1, :]
    r = lax.rsqrt(jnp.mean(x * x, axis=-1, keepdims=True) + eps)
    scaled = back * gain
    dot = jnp.mean(scaled * x, axis=-1, keepdims=True)
    grad[...] = hidden_grad[...] + r * scaled - x * (r * r * r * dot)


def unpack_kernel(*refs):
    arrived, query, key, value, out = refs
    turned = arrived[:, 0:192, :].astype(f32)
    query[...] = turned[:, 0:HD].reshape(HEADS * HD, TOK).T
    pairs = turned[:, HD : 3 * HD].reshape(HEADS // 2, 2, 2 * HD, TOK)
    pairs = pairs[:, 0] + pairs[:, 1]
    key[...] = pairs[:, 0:HD].reshape(512, TOK).T
    value[...] = pairs[:, HD : 2 * HD].reshape(512, TOK).T
    for j in range(PEERS):
        rows = arrived[j, 192:264, :].astype(f32)
        for g in range(9):
            out[j * 8 : (j + 1) * 8, g * 128 : (g + 1) * 128] = rows[g * 8 : (g + 1) * 8, :]


def per_device(
    inputs,
    segments,
    routes,
    gain_attn,
    w_query,
    w_key,
    w_value,
    w_out,
    gain_ffn,
    w_router,
    expert_gate,
    expert_up,
    expert_down,
    cotangent,
):
    place = lax.axis_index("expert")
    row = lax.axis_index("dp")
    info = jnp.stack([place // SIDE, place % SIDE, row // 2, row % 2]).astype(jnp.int32)
    states = inputs[0]
    cot = cotangent[0]

    first_a = jnp.concatenate(gather_x(states[:, 0:512]), axis=0)
    first_b = jnp.concatenate(gather_z(states[:, 512:1024]), axis=0)
    row_a = gather_z(first_a)
    row_b = gather_x(first_b)

    extra = jnp.concatenate(
        [
            w_router.T.reshape(2, EXTRA, TOK).transpose(1, 0, 2).reshape(EXTRA, 256),
            jnp.concatenate(
                [gain_attn[None, :], gain_ffn[None, :], jnp.zeros((EXTRA - 2, TOK), bf16)], axis=0
            ),
            jnp.zeros((EXTRA, WIDE - 384), bf16),
        ],
        axis=1,
    )
    dense = jnp.concatenate(
        [jnp.concatenate([w_query, w_key, w_value, w_out], axis=1), extra], axis=0
    )
    dense = gather_dp(dense)
    packed = jnp.concatenate(
        [expert_gate, expert_up, expert_down[:, :, 0:512], expert_down[:, :, 512:1024]], axis=1
    )
    packed = gather_dp(packed)

    segment_row = segments[0][None, :]
    index = jnp.arange(SEQ, dtype=jnp.int32)[None, :]
    start = jnp.zeros((1, SEQ), jnp.int32)
    for s in range(3):
        count = jnp.sum((segment_row == s).astype(jnp.int32))
        start = start + jnp.where(segment_row > s, count, 0)
    freqs = theta ** (-jnp.arange(0, HD, 2, dtype=f32) / HD)
    angles = freqs[:, None] * (index - start).astype(f32)
    cosine, sine = jnp.cos(angles), jnp.sin(angles)

    my_routes = routes[0]
    names = jnp.arange(EXPERTS, dtype=jnp.int32)
    choose = jnp.any(my_routes.T[None, :, :] == names[:, None, None], axis=1).astype(f32)
    order = jnp.arange(TOK, dtype=jnp.int32)
    before = (order[:, None] < order[None, :]).astype(f32)
    rank = jnp.dot(choose, before, preferred_element_type=f32).astype(jnp.int32)
    slots = jnp.arange(CAP, dtype=jnp.int32)
    table = ((rank[:, None, :] == slots[None, :, None]) & (choose[:, None, :] > 0)).astype(bf16)
    table = table.reshape(EXPERTS * CAP, TOK)
    table_t = table.T
    cot_send = jnp.dot(table, cot, preferred_element_type=f32).astype(bf16)
    cot_arrived = swap_all(cot_send)

    normed, small, qz, kvt, out_t, lse, mixed_send = run(
        attend_kernel,
        "attend",
        (
            shape((SEQ, D), bf16),
            shape((3 * EXTRA, D), bf16),
            shape((128, SEQ), bf16),
            shape((128, SEQ), bf16),
            shape((HD, SEQ), f32),
            shape((1, SEQ), f32),
            shape((HEADS, HD, TOK), bf16),
        ),
        (info, *row_a, *row_b, *dense, cosine, sine, start),
        [SM] + [VM] * 8 + [HB] * 8 + [VM] * 3,
        (
            pltpu.VMEM((3, D, 128), bf16),
            pltpu.VMEM((3, 128, D), bf16),
            pltpu.VMEM((SEQ, 128), bf16),
            pltpu.SemaphoreType.DMA((48,)),
        ),
        limit=32,
        flops=6 * 10**9,
        moved=10 * MIB,
    )
    mixed_t = swap_all(mixed_send).reshape(HEADS * HD, TOK)

    hidden, send = run(
        project_kernel,
        "project",
        (shape((TOK, D), f32), shape((2 * ROWS, D), bf16)),
        (info, mixed_t, states, small, table, *dense),
        [SM] + [VM] * 4 + [HB] * 8,
        (pltpu.VMEM((D, D), bf16), pltpu.SemaphoreType.DMA((8,))),
        flops=10**9,
        moved=6 * MIB,
    )
    arrived = swap_all(send)

    sent_grad, xs, gs, acted, dgate, dup, gates, lgs = run(
        expert_kernel,
        "experts",
        (
            shape((2 * ROWS, D), bf16),
            shape((2, ROWS, D), bf16),
            shape((2, ROWS, D), bf16),
            shape((2, ROWS, EF), bf16),
            shape((2, ROWS, EF), bf16),
            shape((2, ROWS, EF), bf16),
            shape((2, ROWS, 128), f32),
            shape((2, ROWS, EXPERTS), bf16),
        ),
        (info, arrived, cot_arrived, small, *packed),
        [SM] + [VM] * 3 + [HB] * 8,
        (
            pltpu.VMEM((2, ROWS, D), f32),
            pltpu.VMEM((2, D, EF), bf16),
            pltpu.VMEM((2, D, EF), bf16),
            pltpu.VMEM((2, EF, D), bf16),
            pltpu.SemaphoreType.DMA((32,)),
        ),
        limit=48,
        flops=7 * 10**9,
        moved=20 * MIB,
    )
    back = swap_all(sent_grad)

    returned, grads_mine, grads_other, router_grad = run(
        weights_kernel,
        "weights",
        (
            shape((2 * ROWS, D), bf16),
            shape((SIDE, 2, 384, 512), bf16),
            shape((SIDE, 2, 384, 512), bf16),
            shape((EXPERTS, D), f32),
        ),
        (info, xs, gs, acted, dgate, dup, gates, lgs, *packed),
        [SM] + [VM] * 7 + [HB] * 8,
        (
            pltpu.VMEM((2, ROWS, D), f32),
            pltpu.VMEM((2, EF, D), bf16),
            pltpu.VMEM((2, D, EF), bf16),
            pltpu.VMEM((EF, D), bf16),
            pltpu.SemaphoreType.DMA((16,)),
        ),
        limit=48,
        flops=6 * 10**9,
        moved=20 * MIB,
    )
    expert_sums = reduce_dp(grads_mine, grads_other)

    hidden_grad, low, grad_send, gain_grad = run(
        hidden_kernel,
        "hidden_grad",
        (
            shape((TOK, D), f32),
            shape((TOK, D), bf16),
            shape((HEADS, HD, TOK), bf16),
            shape((1, D), f32),
        ),
        (info, back, table_t, hidden, cot, small, *dense),
        [SM] + [VM] * 5 + [HB] * 8,
        (pltpu.VMEM((D, D), bf16), pltpu.SemaphoreType.DMA((8,))),
        flops=10**9,
        moved=6 * MIB,
    )
    mixed_grad = swap_all(grad_send)

    out_mine, out_other = run(
        out_weights_kernel,
        "out_weights",
        (shape((SIDE, TOK, PACK), bf16), shape((SIDE, TOK, PACK), bf16)),
        (info, mixed_t, low, router_grad, gain_grad),
        [SM] + [VM] * 4,
        (pltpu.VMEM((D, 128), f32),),
        flops=10**9,
        moved=4 * MIB,
    )
    out_sums = reduce_dp(out_mine, out_other).astype(bf16)
    out_sums = swap_all(out_sums).reshape(PEERS, 8, PACK)
    out_sums = jnp.sum(out_sums.astype(f32), axis=0).astype(bf16)
    out_sums = jnp.concatenate([out_sums[:, g * 128 : (g + 1) * 128] for g in range(9)], axis=0)

    grads_send, w_mine, w_other = run(
        attend_back_kernel,
        "attend_back",
        (
            shape((PEERS, 192, TOK), bf16),
            shape((SIDE, 192, TOK), bf16),
            shape((SIDE, 192, TOK), bf16),
        ),
        (info, qz, kvt, out_t, lse, mixed_grad, cosine, sine, start, normed),
        [SM] + [VM] * 9,
        (
            pltpu.VMEM((SEQ, 128), bf16),
            pltpu.VMEM((128, SEQ), bf16),
            pltpu.VMEM((SEQ, 128), bf16),
            pltpu.VMEM((HD, SEQ), f32),
            pltpu.VMEM((192, SEQ), bf16),
            pltpu.VMEM((1, SEQ), f32),
            pltpu.VMEM((DP, 192, TOK), bf16),
        ),
        limit=32,
        flops=8 * 10**9,
        moved=10 * MIB,
    )
    w_sums = reduce_dp(w_mine, w_other).astype(bf16)

    last = jnp.concatenate([w_sums, out_sums], axis=0)
    last = jnp.concatenate(
        [grads_send, jnp.broadcast_to(last[None], (PEERS, 264, TOK))], axis=1
    )
    last = swap_all(last)
    grads_arrived, sums_arrived = last[:, 0:192], last[:, 192:456]

    grad_input = run(
        input_kernel,
        "grad_input",
        shape((TOK, D), f32),
        (info, grads_arrived, hidden_grad, states, small, *dense),
        [SM] + [VM] * 4 + [HB] * 8,
        (pltpu.VMEM((D, 2048), bf16), pltpu.SemaphoreType.DMA((8,))),
        flops=10**9,
        moved=6 * MIB,
    )
    sum_query, sum_key, sum_value, sum_rest = run(
        unpack_kernel,
        "unpack",
        (
            shape((TOK, 1024), f32),
            shape((TOK, 512), f32),
            shape((TOK, 512), f32),
            shape((TOK, PACK), f32),
        ),
        (sums_arrived,),
        [VM],
        moved=4 * MIB,
    )
    weighted = (
        jnp.sum(sum_query * w_query.astype(f32), axis=-1)
        + jnp.sum(sum_key * w_key.astype(f32), axis=-1)
        + jnp.sum(sum_value * w_value.astype(f32), axis=-1)
    )
    sum_gain_attn = weighted / gain_attn.astype(f32)

    picked = swap_all(returned)
    output = hidden + jnp.dot(table_t, picked, preferred_element_type=f32)

    return (
        output.astype(bf16)[None],
        grad_input[None],
        sum_gain_attn,
        sum_query,
        sum_key,
        sum_value,
        sum_rest[:, 0:1024],
        sum_rest[:, 1056],
        sum_rest[:, 1024:1056],
        expert_sums[:, 0:128],
        expert_sums[:, 128:256],
        jnp.concatenate([expert_sums[:, 256:320], expert_sums[:, 320:384]], axis=2),
    )


def solution(mesh):
    placed = (
        P("dp", "expert", None),
        P("dp", None),
        P("dp", "expert", None),
        P("dp"),
        P("dp", None),
        P("dp", None),
        P("dp", None),
        P("dp", None),
        P("dp"),
        P("dp", None),
        P("expert", "dp", None),
        P("expert", "dp", None),
        P("expert", "dp", None),
        P("dp", "expert", None),
    )
    return jax.shard_map(
        per_device,
        mesh=mesh,
        in_specs=placed,
        out_specs=(
            P("dp", "expert", None),
            P("dp", "expert", None),
            P("dp"),
            P("dp", None),
            P("dp", None),
            P("dp", None),
            P("dp", None),
            P("dp"),
            P("dp", None),
            P("expert", "dp", None),
            P("expert", "dp", None),
            P("expert", "dp", None),
        ),
        check_vma=False,
    )
```

time: 1100 us -> 450 us (0.41)
  the two profiles are of different devices: /device:TPU:0 before, /device:TPU:24 now
where the time goes in v1:
time: 450 us; the launch traced here: 442 us
  waiting for transfers between devices  182 us (40%)
  starting transfers between devices  74.2 us (16%)
  local copies, waits for them, and re-layouts  71.9 us (16%)
  Pallas kernels  67.4 us (15%)
  other arithmetic  24.1 us (5%)
  blocking collectives  13.4 us (3%)
  matrix products  6.5 us (1%)
    all_to_all x7, waiting for transfers between devices, swap_all(): lax.all_to_all(values, 'expert', split_axis=0, concat_axis=0, tiled=True)  89.7 us
    pallas_call x9, Pallas kernels, run(): pl.pallas_call(kernel, name=name, out_shape=outs, in_specs=specs, out_spe...  67.4 us
    unnamed x208, local copies, waits for them, and re-layouts  55.3 us
    ppermute x15, waiting for transfers between devices, dp_from(): return lax.ppermute(values, 'dp', pairs)  50.7 us
    ppermute x12, waiting for transfers between devices, expert_from(): return lax.ppermute(values, 'expert', pairs)  42 us
    all_to_all x7, starting transfers between devices, swap_all(): lax.all_to_all(values, 'expert', split_axis=0, concat_axis=0, tiled=True)  34.4 us
    ppermute x12, starting transfers between devices, expert_from(): return lax.ppermute(values, 'expert', pairs)  20.6 us
    ppermute x15, starting transfers between devices, dp_from(): return lax.ppermute(values, 'dp', pairs)  18.2 us
  transfers between devices with their start and end apart: 45, of which 22 were waited for; matrix products, arithmetic and copies ran while one was open for 9% of the time, Pallas kernels for 7%

profile of v1, /device:TPU:24, one launch (start us, length us, event | category | flops | bytes accessed | tf_op | source)
XLA Modules:
  0.0 441.9 jit_solution(9199646180827851494)
XLA Ops:
  3.3 2.7 collective-permute-start.1
  8.5 3.6 collective-permute-done.1
  12.9 1.9 collective-permute-start.5
  14.8 1.9 collective-permute-start.8
  18.5 2.6 collective-permute-start.6
  23.6 8.3 %collective-permute-done.8 = bf16[128,512]{1,0:T(8,128)(2,1)S(1)} collective-permute-done((bf16[128,512]{1,0:T(8,128)(2,1)S(1)}, bf16[128,512]{1,0:T(8,128)(2,1)S(1)}, u32[]{:S(2)}, u32[]{:S(2)}) %collective-permute-start.8) | collective-permute-done | bytes 131104 | tf_op jit(solution)/shard_map/ppermute | solution.py:67
  37.8 2.6 subtract_convert_fusion
  41.5 7.4 %collective-permute-done.4.refs_2_ = bf16[512,512]{1,0:T(8,128)(2,1)} collective-permute-done((bf16[512,512]{1,0:T(8,128)(2,1)}, bf16[512,512]{1,0:T(8,128)(2,1)}, u32[]{:S(2)}, u32[]{:S(2)}) %collective-permute-start.4) | collective-permute-done | bytes 524320 | tf_op jit(solution)/shard_map/ppermute | solution.py:67
  50.7 5.4 %collective-permute-done.3.refs_1_ = bf16[512,512]{1,0:T(8,128)(2,1)} collective-permute-done((bf16[512,512]{1,0:T(8,128)(2,1)}, bf16[512,512]{1,0:T(8,128)(2,1)}, u32[]{:S(2)}, u32[]{:S(2)}) %collective-permute-start.3) | collective-permute-done | bytes 524320 | tf_op jit(solution)/shard_map/ppermute | solution.py:67
  57.7 4.0 collective-permute-done.11.refs_7_
  62.3 9.1 %collective-permute-done.12.refs_9_.refs_5_.refs_6_ = bf16[144,3072]{1,0:T(8,128)(2,1)S(1)} collective-permute-done((bf16[144,3072]{1,0:T(8,128)(2,1)S(1)}, bf16[144,3072]{1,0:T(8,128)(2,1)S(1)}, u32[]{:S(2)}, u32[]{:S(2)}) %collective-permute-start.12) | collective-permute-done | bytes 884768 | tf_op jit(solution)/shard_map/ppermute | solution.py:72
  72.8 2.4 collective-permute-start.9
  77.1 9.9 %collective-permute-done.9.refs_5_ = bf16[512,512]{1,0:T(8,128)(2,1)S(1)} collective-permute-done((bf16[512,512]{1,0:T(8,128)(2,1)S(1)}, bf16[512,512]{1,0:T(8,128)(2,1)S(1)}, u32[]{:S(2)}, u32[]{:S(2)}) %collective-permute-start.9) | collective-permute-done | bytes 524320 | tf_op jit(solution)/shard_map/ppermute | solution.py:67
  87.0 11.3 %attend.1 = (bf16[2048,1024]{1,0:T(8,128)(2,1)S(1)}, bf16[48,1024]{1,0:T(8,128)(2,1)S(1)}, bf16[128,2048]{1,0:T(8,128)(2,1)S(1)}, bf16[128,2048]{1,0:T(8,128)(2,...) custom-call(s32[4]{0:T(128)S(1)} %pad_add_fusion.info, ...), custom_call_target="tpu_custom_call" | custom-call | flops 6000000000 | bytes 10485760 | tf_op jit(solution)/shard_map/attend/pallas_call | solution.py:49
  99.7 2.0 copy-done.63
  104.7 6.3 %all-to-all-start = ((bf16[16,64,128]{2,1,0:T(8,128)(2,1)}), bf16[16,64,128]{2,1,0:T(8,128)(2,1)}, u32[]{:S(2)}, u32[]{:S(2)}) async-start(bf16[16,64,128]{2,1,0:T(8,128)(2,1)} %copy-done.47), calls=%async_computation | async-start | bytes 524288 | tf_op jit(solution)/shard_map/all_to_all | solution.py:105
  111.0 3.3 convolution_convert_fusion
  114.3 5.4 %all-to-all-done = bf16[16,64,128]{2,1,0:T(8,128)(2,1)} async-done(((bf16[16,64,128]{2,1,0:T(8,128)(2,1)}), bf16[16,64,128]{2,1,0:T(8,128)(2,1)}, u32[]{:S(2)}, u32[]{:S(2)}) %all-to-all-start) | async-done | bytes 262176 | tf_op jit(solution)/shard_map/all_to_all | solution.py:105
  119.8 4.9 %all-to-all-start.2 = ((bf16[16,80,1024]{2,1,0:T(8,128)(2,1)}), bf16[16,80,1024]{2,1,0:T(8,128)(2,1)}, u32[]{:S(2)}, u32[]{:S(2)}) async-start(bf16[16,80,1024]{2,1,0:T(8,128)(2,1)} %bitcast.88), calls=%async_computation.2 | async-start | bytes 5242880 | tf_op jit(solution)/shard_map/all_to_all | solution.py:105
  130.8 2.2 copy.36
  133.0 2.0 and_convert_fusion
  135.0 1.9 copy.38.refs_3_
  144.3 2.7 project.1
  149.3 11.3 %all-to-all-done.2 = bf16[16,80,1024]{2,1,0:T(8,128)(2,1)} async-done(((bf16[16,80,1024]{2,1,0:T(8,128)(2,1)}), bf16[16,80,1024]{2,1,0:T(8,128)(2,1)}, u32[]{:S(2)}, u32[]{:S(2)}) %all-to-all-start.2) | async-done | bytes 2621472 | tf_op jit(solution)/shard_map/all_to_all | solution.py:105
  160.6 4.6 %all-to-all-start.1 = ((bf16[16,80,1024]{2,1,0:T(8,128)(2,1)}), bf16[16,80,1024]{2,1,0:T(8,128)(2,1)}, u32[]{:S(2)}, u32[]{:S(2)}) async-start(bf16[16,80,1024]{2,1,0:T(8,128)(2,1)} %bitcast.83), calls=%async_computation.1 | async-start | bytes 5242880 | tf_op jit(solution)/shard_map/all_to_all | solution.py:105
  167.4 18.4 %collective-permute-done.21.refs_6_.refs_10_ = bf16[2,384,512]{2,1,0:T(8,128)(2,1)S(1)} collective-permute-done((bf16[2,384,512]{2,1,0:T(8,128)(2,1)S(1)}, bf16[2,384,512]{2,1,0:T(8,128)(2,1)S(1)}, u32[]{:S(2)}, u32[]{:S(2)}) %collective-permute-start.21) | collective-permute-done | bytes 786464 | tf_op jit(solution)/shard_map/ppermute | solution.py:72
  187.5 14.1 %collective-permute-done.19.refs_4_.refs_8_ = bf16[2,384,512]{2,1,0:T(8,128)(2,1)S(1)} collective-permute-done((bf16[2,384,512]{2,1,0:T(8,128)(2,1)S(1)}, bf16[2,384,512]{2,1,0:T(8,128)(2,1)S(1)}, u32[]{:S(2)}, u32[]{:S(2)}) %collective-permute-start.19) | collective-permute-done | bytes 786464 | tf_op jit(solution)/shard_map/ppermute | solution.py:72
  209.5 19.4 %experts.1 = (bf16[1280,1024]{1,0:T(8,128)(2,1)}, bf16[2,640,1024]{2,1,0:T(8,128)(2,1)}, bf16[2,640,1024]{2,1,0:T(8,128)(2,1)}, bf16[2,640,512]{2,1,0:T(8,128)(2...) custom-call(s32[4]{0:T(128)S(1)} %pad_add_fusion.info, ...), custom_call_target="tpu_custom_call" | custom-call | flops 7000000000 | bytes 20971520 | tf_op jit(solution)/shard_map/experts/pallas_call | solution.py:49
  230.6 6.9 %all-to-all-start.4 = ((bf16[16,80,1024]{2,1,0:T(8,128)(2,1)}), bf16[16,80,1024]{2,1,0:T(8,128)(2,1)S(1)}, u32[]{:S(2)}, u32[]{:S(2)}) async-start(bf16[16,80,1024]{2,1,0:T(8,128)(2,1)} %bitcast.90), calls=%async_computation.4 | async-start | bytes 5242880 | tf_op jit(solution)/shard_map/all_to_all | solution.py:105
  246.3 15.9 %weights.1 = (bf16[1280,1024]{1,0:T(8,128)(2,1)}, bf16[4,2,384,512]{3,2,1,0:T(8,128)(2,1)}, bf16[4,2,384,512]{3,2,1,0:T(8,128)(2,1)}, f32[32,1024]{1,0:T(8,128)S(1)}) custom-call(s32[4]{0:T(128)S(1)} %pad_add_fusion.info, bf16[2,640,1024]{2,1,0:T(8,128)(2,1)} %get-tuple-element.50.refs_0_, bf16[2,640,1024]{2,1,0:T(8,128)(2,1)} %get-tuple-element.51.refs_1_, ...), custom_call_target="tpu_custom_call" | custom-call | flops 6000000000 | bytes 20971520 | tf_op jit(solution)/shard_map/weights/pallas_call | solution.py:49
  263.1 16.0 %all-to-all-done.4 = bf16[16,80,1024]{2,1,0:T(8,128)(2,1)S(1)} async-done(((bf16[16,80,1024]{2,1,0:T(8,128)(2,1)}), bf16[16,80,1024]{2,1,0:T(8,128)(2,1)S(1)}, u32[]{:S(2)}, u32[]{:S(2)}) %all-to-all-start.4) | async-done | bytes 2621472 | tf_op jit(solution)/shard_map/all_to_all | solution.py:105
  291.2 2.2 hidden_grad.1
  293.5 1.9 out_weights.1
  295.5 13.4 %all_to_all.69.refs_4_ = bf16[16,64,128]{2,1,0:T(8,128)(2,1)S(1)} all-to-all(bf16[16,64,128]{2,1,0:T(8,128)(2,1)S(1)} %get-tuple-element.63), channel_id=1, replica_groups=mesh['dp'=8,'expert'=16] {'expert'}, dimensions={0} | all-to-all | bytes 524288 | tf_op jit(solution)/shard_map/all_to_all | solution.py:105
  309.0 9.0 %attend_back.1 = (bf16[16,192,128]{2,1,0:T(8,128)(2,1)S(1)}, bf16[4,192,128]{2,1,0:T(8,128)(2,1)S(1)}, bf16[4,192,128]{2,1,0:T(8,128)(2,1)S(1)}) custom-call(s32[4]{0:T(128)S(1)} %pad_add_fusion.info, bf16[128,2048]{1,0:T(8,128)(2,1)S(1)} %copy-done.72, bf16[128,2048]{1,0:T(8,128)(2,1)S(1)} %copy-done.74, f32[64,2048]{1,0:T(8,128)S(1)} %copy-done.76, ...), custom_call_target="tpu_custom_call" | custom-call | flops 8000000000 | bytes 10485760 | tf_op jit(solution)/shard_map/attend_back/pallas_call | solution.py:49
  320.6 2.6 collective-permute-start.27
  323.2 5.0 %collective-permute-done.31 = bf16[128,1152]{1,0:T(8,128)(2,1)S(1)} collective-permute-done((bf16[128,1152]{1,0:T(8,128)(2,1)S(1)}, bf16[128,1152]{1,0:T(8,128)(2,1)S(1)}, u32[]{:S(2)}, u32[]{:S(2)}) %collective-permute-start.31) | collective-permute-done | bytes 294944 | tf_op jit(solution)/shard_map/ppermute | solution.py:72
  329.9 4.8 %collective-permute-start.28 = (bf16[192,128]{1,0:T(8,128)(2,1)S(1)}, bf16[192,128]{1,0:T(8,128)(2,1)S(1)}, u32[]{:S(2)}, u32[]{:S(2)}) collective-permute-start(bf16[192,128]{1,0:T(8,128)(2,1)S(1)} %get-tuple-element.133), channel_id=1, source_target_pairs={{0,96},{16,112},{32,0},{48,16},{64,32},{80,48},{96,64},{112,80},{1... | collective-permute-start | bytes 147464 | tf_op jit(solution)/shard_map/ppermute | solution.py:72
  337.1 3.5 all-to-all-start.6
  340.7 9.3 %all-to-all-done.6 = bf16[16,8,1152]{2,1,0:T(8,128)(2,1)S(1)} async-done(((bf16[16,8,1152]{2,1,0:T(8,128)(2,1)}), bf16[16,8,1152]{2,1,0:T(8,128)(2,1)S(1)}, u32[]{:S(2)}, u32[]{:S(2)}) %all-to-all-start.6) | async-done | bytes 294944 | tf_op jit(solution)/shard_map/all_to_all | solution.py:105
  350.0 4.4 %all-to-all-start.3 = ((bf16[16,80,1024]{2,1,0:T(8,128)(2,1)}), bf16[16,80,1024]{2,1,0:T(8,128)(2,1)}, u32[]{:S(2)}, u32[]{:S(2)}) async-start(bf16[16,80,1024]{2,1,0:T(8,128)(2,1)} %bitcast.89), calls=%async_computation.3 | async-start | bytes 5242880 | tf_op jit(solution)/shard_map/all_to_all | solution.py:105
  354.5 4.1 fusion.5
  363.7 29.0 %all-to-all-done.3 = bf16[16,80,1024]{2,1,0:T(8,128)(2,1)} async-done(((bf16[16,80,1024]{2,1,0:T(8,128)(2,1)}), bf16[16,80,1024]{2,1,0:T(8,128)(2,1)}, u32[]{:S(2)}, u32[]{:S(2)}) %all-to-all-start.3) | async-done | bytes 2621472 | tf_op jit(solution)/shard_map/all_to_all | solution.py:105
  392.7 3.7 all-to-all-start.7
  396.5 3.0 fusion.3
  399.5 2.6 fusion.1
  404.0 18.8 %all-to-all-done.7 = bf16[16,456,128]{2,1,0:T(8,128)(2,1)S(1)} async-done(((bf16[16,456,128]{2,1,0:T(8,128)(2,1)}), bf16[16,456,128]{2,1,0:T(8,128)(2,1)S(1)}, u32[]{:S(2)}, u32[]{:S(2)}) %all-to-all-start.7) | async-done | bytes 1867808 | tf_op jit(solution)/shard_map/all_to_all | solution.py:105
  438.1 3.5 grad_input.1
  (309 shorter events, 108.7 us)
Async XLA Ops:
  1.8 6.7 %collective-permute-start.2 = (bf16[128,512]{1,0:T(8,128)(2,1)S(1)}, bf16[128,512]{1,0:T(8,128)(2,1)S(1)}, u32[]{:S(2)}, u32[]{:S(2)}) collective-permute-start(bf16[128,512]{1,0:T(8,128)(2,1)S(1)} %get-tuple-element.137), channel_id=1, source_target_pairs={{0,1},{1,2},{2,3},{3,0},{4,5},{5,6},{6,7},{7,4},{8,9},{9,10},{10,1... | collective-permute-start | bytes 393224 | tf_op jit(solution)/shard_map/ppermute | solution.py:67
  3.3 8.7 %collective-permute-start.1 = (bf16[128,512]{1,0:T(8,128)(2,1)S(1)}, bf16[128,512]{1,0:T(8,128)(2,1)S(1)}, u32[]{:S(2)}, u32[]{:S(2)}) collective-permute-start(bf16[128,512]{1,0:T(8,128)(2,1)S(1)} %get-tuple-element.137), channel_id=1, source_target_pairs={{0,2},{1,3},{2,0},{3,1},{4,6},{5,7},{6,4},{7,5},{8,10},{9,11},{10,... | collective-permute-start | bytes 393224 | tf_op jit(solution)/shard_map/ppermute | solution.py:67
  6.1 6.0 %collective-permute-start = (bf16[128,512]{1,0:T(8,128)(2,1)S(1)}, bf16[128,512]{1,0:T(8,128)(2,1)S(1)}, u32[]{:S(2)}, u32[]{:S(2)}) collective-permute-start(bf16[128,512]{1,0:T(8,128)(2,1)S(1)} %get-tuple-element.137), channel_id=1, source_target_pairs={{0,3},{1,0},{2,1},{3,2},{4,7},{5,4},{6,5},{7,6},{8,11},{9,8},{10,9... | collective-permute-start | bytes 393224 | tf_op jit(solution)/shard_map/ppermute | solution.py:67
  12.9 23.9 %collective-permute-start.5 = (bf16[512,512]{1,0:T(8,128)(2,1)}, bf16[512,512]{1,0:T(8,128)(2,1)S(1)}, u32[]{:S(2)}, u32[]{:S(2)}) collective-permute-start(bf16[512,512]{1,0:T(8,128)(2,1)} %pad_maximum_fusion.2.refs_0_), channel_id=1, source_target_pairs={{0,4},{1,5},{2,6},{3,7},{4,8},{5,9},{6,10},{7,11},{8,12},{9,13},{1... | collective-permute-start | bytes 1572872 | tf_op jit(solution)/shard_map/ppermute | solution.py:67
  14.8 17.1 %collective-permute-start.8 = (bf16[128,512]{1,0:T(8,128)(2,1)S(1)}, bf16[128,512]{1,0:T(8,128)(2,1)S(1)}, u32[]{:S(2)}, u32[]{:S(2)}) collective-permute-start(bf16[128,512]{1,0:T(8,128)(2,1)S(1)} %get-tuple-element.136), channel_id=1, source_target_pairs={{0,4},{1,5},{2,6},{3,7},{4,8},{5,9},{6,10},{7,11},{8,12},{9,13},{1... | collective-permute-start | bytes 393224 | tf_op jit(solution)/shard_map/ppermute | solution.py:67
  16.8 18.3 %collective-permute-start.7 = (bf16[128,512]{1,0:T(8,128)(2,1)S(1)}, bf16[128,512]{1,0:T(8,128)(2,1)S(1)}, u32[]{:S(2)}, u32[]{:S(2)}) collective-permute-start(bf16[128,512]{1,0:T(8,128)(2,1)S(1)} %get-tuple-element.136), channel_id=1, source_target_pairs={{0,8},{1,9},{2,10},{3,11},{4,12},{5,13},{6,14},{7,15},{8,0},{9,1},... | collective-permute-start | bytes 393224 | tf_op jit(solution)/shard_map/ppermute | solution.py:67
  18.5 17.3 %collective-permute-start.6 = (bf16[128,512]{1,0:T(8,128)(2,1)S(1)}, bf16[128,512]{1,0:T(8,128)(2,1)S(1)}, u32[]{:S(2)}, u32[]{:S(2)}) collective-permute-start(bf16[128,512]{1,0:T(8,128)(2,1)S(1)} %get-tuple-element.136), channel_id=1, source_target_pairs={{0,12},{1,13},{2,14},{3,15},{4,0},{5,1},{6,2},{7,3},{8,4},{9,5},{1... | collective-permute-start | bytes 393224 | tf_op jit(solution)/shard_map/ppermute | solution.py:67
  22.6 39.1 %collective-permute-start.14 = (bf16[144,3072]{1,0:T(8,128)(2,1)S(1)}, bf16[144,3072]{1,0:T(8,128)(2,1)S(1)}, u32[]{:S(2)}, u32[]{:S(2)}) collective-permute-start(bf16[144,3072]{1,0:T(8,128)(2,1)S(1)} %maximum_maximum_fusion.refs_8_.refs_4_.refs_5_), channel_id=1, source_target_pairs={{0,32},{16,48},{32,64},{48,80},{64,96},{80,112},{96,0},{112,16},{1... | collective-permute-start | bytes 2654216 | tf_op jit(solution)/shard_map/ppermute | solution.py:72
  31.9 30.3 %collective-permute-start.13 = (bf16[144,3072]{1,0:T(8,128)(2,1)S(1)}, bf16[144,3072]{1,0:T(8,128)(2,1)S(1)}, u32[]{:S(2)}, u32[]{:S(2)}) collective-permute-start(bf16[144,3072]{1,0:T(8,128)(2,1)S(1)} %maximum_maximum_fusion.refs_8_.refs_4_.refs_5_), channel_id=1, source_target_pairs={{0,64},{16,80},{32,96},{48,112},{64,0},{80,16},{96,32},{112,48},{1... | collective-permute-start | bytes 2654216 | tf_op jit(solution)/shard_map/ppermute | solution.py:72
  35.0 36.3 %collective-permute-start.12 = (bf16[144,3072]{1,0:T(8,128)(2,1)S(1)}, bf16[144,3072]{1,0:T(8,128)(2,1)S(1)}, u32[]{:S(2)}, u32[]{:S(2)}) collective-permute-start(bf16[144,3072]{1,0:T(8,128)(2,1)S(1)} %maximum_maximum_fusion.refs_8_.refs_4_.refs_5_), channel_id=1, source_target_pairs={{0,96},{16,112},{32,0},{48,16},{64,32},{80,48},{96,64},{112,80},{1... | collective-permute-start | bytes 2654216 | tf_op jit(solution)/shard_map/ppermute | solution.py:72
  35.8 13.1 %collective-permute-start.4 = (bf16[512,512]{1,0:T(8,128)(2,1)}, bf16[512,512]{1,0:T(8,128)(2,1)}, u32[]{:S(2)}, u32[]{:S(2)}) collective-permute-start(bf16[512,512]{1,0:T(8,128)(2,1)} %pad_maximum_fusion.2.refs_0_), channel_id=1, source_target_pairs={{0,8},{1,9},{2,10},{3,11},{4,12},{5,13},{6,14},{7,15},{8,0},{9,1},... | collective-permute-start | bytes 1572872 | tf_op jit(solution)/shard_map/ppermute | solution.py:67
  37.6 18.6 %collective-permute-start.3 = (bf16[512,512]{1,0:T(8,128)(2,1)}, bf16[512,512]{1,0:T(8,128)(2,1)}, u32[]{:S(2)}, u32[]{:S(2)}) collective-permute-start(bf16[512,512]{1,0:T(8,128)(2,1)} %pad_maximum_fusion.2.refs_0_), channel_id=1, source_target_pairs={{0,12},{1,13},{2,14},{3,15},{4,0},{5,1},{6,2},{7,3},{8,4},{9,5},{1... | collective-permute-start | bytes 1572872 | tf_op jit(solution)/shard_map/ppermute | solution.py:67
  48.9 12.8 %collective-permute-start.11 = (bf16[512,512]{1,0:T(8,128)(2,1)S(1)}, bf16[512,512]{1,0:T(8,128)(2,1)S(1)}, u32[]{:S(2)}, u32[]{:S(2)}) collective-permute-start(bf16[512,512]{1,0:T(8,128)(2,1)S(1)} %pad_maximum_fusion.3.refs_4_), channel_id=1, source_target_pairs={{0,1},{1,2},{2,3},{3,0},{4,5},{5,6},{6,7},{7,4},{8,9},{9,10},{10,1... | collective-permute-start | bytes 1572872 | tf_op jit(solution)/shard_map/ppermute | solution.py:67
  56.1 16.7 %collective-permute-start.10 = (bf16[512,512]{1,0:T(8,128)(2,1)S(1)}, bf16[512,512]{1,0:T(8,128)(2,1)S(1)}, u32[]{:S(2)}, u32[]{:S(2)}) collective-permute-start(bf16[512,512]{1,0:T(8,128)(2,1)S(1)} %pad_maximum_fusion.3.refs_4_), channel_id=1, source_target_pairs={{0,2},{1,3},{2,0},{3,1},{4,6},{5,7},{6,4},{7,5},{8,10},{9,11},{10,... | collective-permute-start | bytes 1572872 | tf_op jit(solution)/shard_map/ppermute | solution.py:67
  61.7 25.3 %collective-permute-start.15 = (bf16[144,3072]{1,0:T(8,128)(2,1)S(1)}, bf16[144,3072]{1,0:T(8,128)(2,1)S(1)}, u32[]{:S(2)}, u32[]{:S(2)}) collective-permute-start(bf16[144,3072]{1,0:T(8,128)(2,1)S(1)} %maximum_maximum_fusion.refs_8_.refs_4_.refs_5_), channel_id=1, source_target_pairs={{0,16},{16,0},{32,48},{48,32},{64,80},{80,64},{96,112},{112,96},{1... | collective-permute-start | bytes 2654216 | tf_op jit(solution)/shard_map/ppermute | solution.py:76
  61.7 75.1 %copy-start = (bf16[144,3072]{1,0:T(8,128)(2,1)}, bf16[144,3072]{1,0:T(8,128)(2,1)S(1)}, u32[]{:S(2)}) copy-start(bf16[144,3072]{1,0:T(8,128)(2,1)S(1)} %collective-permute-done.14.refs_11_.refs_7_.refs_8_) | copy-start | bytes 2654212
  61.7 25.3 %collective-permute-start.18 = (bf16[144,3072]{1,0:T(8,128)(2,1)S(1)}, bf16[144,3072]{1,0:T(8,128)(2,1)S(1)}, u32[]{:S(2)}, u32[]{:S(2)}) collective-permute-start(bf16[144,3072]{1,0:T(8,128)(2,1)S(1)} %collective-permute-done.14.refs_11_.refs_7_.refs_8_), channel_id=1, source_target_pairs={{0,16},{16,0},{32,48},{48,32},{64,80},{80,64},{96,112},{112,96},{1... | collective-permute-start | bytes 2654216 | tf_op jit(solution)/shard_map/ppermute | solution.py:76
  62.2 74.6 %copy-start.3 = (bf16[144,3072]{1,0:T(8,128)(2,1)}, bf16[144,3072]{1,0:T(8,128)(2,1)S(1)}, u32[]{:S(2)}) copy-start(bf16[144,3072]{1,0:T(8,128)(2,1)S(1)} %collective-permute-done.13.refs_10_.refs_6_.refs_7_) | copy-start | bytes 2654212
  62.2 24.8 %collective-permute-start.17 = (bf16[144,3072]{1,0:T(8,128)(2,1)S(1)}, bf16[144,3072]{1,0:T(8,128)(2,1)S(1)}, u32[]{:S(2)}, u32[]{:S(2)}) collective-permute-start(bf16[144,3072]{1,0:T(8,128)(2,1)S(1)} %collective-permute-done.13.refs_10_.refs_6_.refs_7_), channel_id=1, source_target_pairs={{0,16},{16,0},{32,48},{48,32},{64,80},{80,64},{96,112},{112,96},{1... | collective-permute-start | bytes 2654216 | tf_op jit(solution)/shard_map/ppermute | solution.py:76
  71.4 65.5 %copy-start.6 = (bf16[144,3072]{1,0:T(8,128)(2,1)}, bf16[144,3072]{1,0:T(8,128)(2,1)S(1)}, u32[]{:S(2)}) copy-start(bf16[144,3072]{1,0:T(8,128)(2,1)S(1)} %collective-permute-done.12.refs_9_.refs_5_.refs_6_) | copy-start | bytes 2654212
  71.4 15.6 %collective-permute-start.16 = (bf16[144,3072]{1,0:T(8,128)(2,1)S(1)}, bf16[144,3072]{1,0:T(8,128)(2,1)S(1)}, u32[]{:S(2)}, u32[]{:S(2)}) collective-permute-start(bf16[144,3072]{1,0:T(8,128)(2,1)S(1)} %collective-permute-done.12.refs_9_.refs_5_.refs_6_), channel_id=1, source_target_pairs={{0,16},{16,0},{32,48},{48,32},{64,80},{80,64},{96,112},{112,96},{1... | collective-permute-start | bytes 2654216 | tf_op jit(solution)/shard_map/ppermute | solution.py:76
  72.8 14.1 %collective-permute-start.9 = (bf16[512,512]{1,0:T(8,128)(2,1)S(1)}, bf16[512,512]{1,0:T(8,128)(2,1)S(1)}, u32[]{:S(2)}, u32[]{:S(2)}) collective-permute-start(bf16[512,512]{1,0:T(8,128)(2,1)S(1)} %pad_maximum_fusion.3.refs_4_), channel_id=1, source_target_pairs={{0,3},{1,0},{2,1},{3,2},{4,7},{5,4},{6,5},{7,6},{8,11},{9,8},{10,9... | collective-permute-start | bytes 1572872 | tf_op jit(solution)/shard_map/ppermute | solution.py:67
  104.7 15.1 %all-to-all-start = ((bf16[16,64,128]{2,1,0:T(8,128)(2,1)}), bf16[16,64,128]{2,1,0:T(8,128)(2,1)}, u32[]{:S(2)}, u32[]{:S(2)}) async-start(bf16[16,64,128]{2,1,0:T(8,128)(2,1)} %copy-done.47), calls=%async_computation | async-start | bytes 524288 | tf_op jit(solution)/shard_map/all_to_all | solution.py:105
  119.8 40.9 %all-to-all-start.2 = ((bf16[16,80,1024]{2,1,0:T(8,128)(2,1)}), bf16[16,80,1024]{2,1,0:T(8,128)(2,1)}, u32[]{:S(2)}, u32[]{:S(2)}) async-start(bf16[16,80,1024]{2,1,0:T(8,128)(2,1)} %bitcast.88), calls=%async_computation.2 | async-start | bytes 5242880 | tf_op jit(solution)/shard_map/all_to_all | solution.py:105
  160.6 45.5 %all-to-all-start.1 = ((bf16[16,80,1024]{2,1,0:T(8,128)(2,1)}), bf16[16,80,1024]{2,1,0:T(8,128)(2,1)}, u32[]{:S(2)}, u32[]{:S(2)}) async-start(bf16[16,80,1024]{2,1,0:T(8,128)(2,1)} %bitcast.83), calls=%async_computation.1 | async-start | bytes 5242880 | tf_op jit(solution)/shard_map/all_to_all | solution.py:105
  165.3 20.6 %collective-permute-start.21 = (bf16[2,384,512]{2,1,0:T(8,128)(2,1)S(1)}, bf16[2,384,512]{2,1,0:T(8,128)(2,1)S(1)}, u32[]{:S(2)}, u32[]{:S(2)}) collective-permute-start(bf16[2,384,512]{2,1,0:T(8,128)(2,1)S(1)} %pad_maximum_fusion.1.refs_3_.refs_7_), channel_id=1, source_target_pairs={{0,32},{16,48},{32,64},{48,80},{64,96},{80,112},{96,0},{112,16},{1... | collective-permute-start | bytes 2359304 | tf_op jit(solution)/shard_map/ppermute | solution.py:72
  165.4 22.1 %collective-permute-start.20 = (bf16[2,384,512]{2,1,0:T(8,128)(2,1)S(1)}, bf16[2,384,512]{2,1,0:T(8,128)(2,1)S(1)}, u32[]{:S(2)}, u32[]{:S(2)}) collective-permute-start(bf16[2,384,512]{2,1,0:T(8,128)(2,1)S(1)} %pad_maximum_fusion.1.refs_3_.refs_7_), channel_id=1, source_target_pairs={{0,64},{16,80},{32,96},{48,112},{64,0},{80,16},{96,32},{112,48},{1... | collective-permute-start | bytes 2359304 | tf_op jit(solution)/shard_map/ppermute | solution.py:72
  166.6 35.1 %collective-permute-start.19 = (bf16[2,384,512]{2,1,0:T(8,128)(2,1)S(1)}, bf16[2,384,512]{2,1,0:T(8,128)(2,1)S(1)}, u32[]{:S(2)}, u32[]{:S(2)}) collective-permute-start(bf16[2,384,512]{2,1,0:T(8,128)(2,1)S(1)} %pad_maximum_fusion.1.refs_3_.refs_7_), channel_id=1, source_target_pairs={{0,96},{16,112},{32,0},{48,16},{64,32},{80,48},{96,64},{112,80},{1... | collective-permute-start | bytes 2359304 | tf_op jit(solution)/shard_map/ppermute | solution.py:72
  167.4 35.1 %collective-permute-start.22 = (bf16[2,384,512]{2,1,0:T(8,128)(2,1)S(1)}, bf16[2,384,512]{2,1,0:T(8,128)(2,1)S(1)}, u32[]{:S(2)}, u32[]{:S(2)}) collective-permute-start(bf16[2,384,512]{2,1,0:T(8,128)(2,1)S(1)} %pad_maximum_fusion.1.refs_3_.refs_7_), channel_id=1, source_target_pairs={{0,16},{16,0},{32,48},{48,32},{64,80},{80,64},{96,112},{112,96},{1... | collective-permute-start | bytes 2359304 | tf_op jit(solution)/shard_map/ppermute | solution.py:76
  185.9 17.6 %collective-permute-start.25 = (bf16[2,384,512]{2,1,0:T(8,128)(2,1)S(1)}, bf16[2,384,512]{2,1,0:T(8,128)(2,1)S(1)}, u32[]{:S(2)}, u32[]{:S(2)}) collective-permute-start(bf16[2,384,512]{2,1,0:T(8,128)(2,1)S(1)} %collective-permute-done.21.refs_6_.refs_10_), channel_id=1, source_target_pairs={{0,16},{16,0},{32,48},{48,32},{64,80},{80,64},{96,112},{112,96},{1... | collective-permute-start | bytes 2359304 | tf_op jit(solution)/shard_map/ppermute | solution.py:76
  187.5 16.0 %collective-permute-start.24 = (bf16[2,384,512]{2,1,0:T(8,128)(2,1)S(1)}, bf16[2,384,512]{2,1,0:T(8,128)(2,1)S(1)}, u32[]{:S(2)}, u32[]{:S(2)}) collective-permute-start(bf16[2,384,512]{2,1,0:T(8,128)(2,1)S(1)} %collective-permute-done.20.refs_5_.refs_9_), channel_id=1, source_target_pairs={{0,16},{16,0},{32,48},{48,32},{64,80},{80,64},{96,112},{112,96},{1... | collective-permute-start | bytes 2359304 | tf_op jit(solution)/shard_map/ppermute | solution.py:76
  201.6 3.6 collective-permute-start.23
  230.6 48.6 %all-to-all-start.4 = ((bf16[16,80,1024]{2,1,0:T(8,128)(2,1)}), bf16[16,80,1024]{2,1,0:T(8,128)(2,1)S(1)}, u32[]{:S(2)}, u32[]{:S(2)}) async-start(bf16[16,80,1024]{2,1,0:T(8,128)(2,1)} %bitcast.90), calls=%async_computation.4 | async-start | bytes 5242880 | tf_op jit(solution)/shard_map/all_to_all | solution.py:105
  262.9 91.6 %collective-permute-start.34 = (bf16[4,2,384,512]{3,2,1,0:T(8,128)(2,1)}, bf16[4,2,384,512]{3,2,1,0:T(8,128)(2,1)}, u32[]{:S(2)}, u32[]{:S(2)}) collective-permute-start(bf16[4,2,384,512]{3,2,1,0:T(8,128)(2,1)} %get-tuple-element.79), channel_id=1, source_target_pairs={{0,16},{16,0},{32,48},{48,32},{64,80},{80,64},{96,112},{112,96},{1... | collective-permute-start | bytes 9437192 | tf_op jit(solution)/shard_map/ppermute | solution.py:76
  295.4 22.7 %collective-permute-start.30 = (bf16[4,128,1152]{2,1,0:T(8,128)(2,1)S(1)}, bf16[4,128,1152]{2,1,0:T(8,128)(2,1)S(1)}, u32[]{:S(2)}, u32[]{:S(2)}) collective-permute-start(bf16[4,128,1152]{2,1,0:T(8,128)(2,1)S(1)} %get-tuple-element.72), channel_id=1, source_target_pairs={{0,16},{16,0},{32,48},{48,32},{64,80},{80,64},{96,112},{112,96},{1... | collective-permute-start | bytes 3538952 | tf_op jit(solution)/shard_map/ppermute | solution.py:76
  317.9 2.6 collective-permute-start.26
  318.3 9.9 %collective-permute-start.31 = (bf16[128,1152]{1,0:T(8,128)(2,1)S(1)}, bf16[128,1152]{1,0:T(8,128)(2,1)S(1)}, u32[]{:S(2)}, u32[]{:S(2)}) collective-permute-start(bf16[128,1152]{1,0:T(8,128)(2,1)S(1)} %get-tuple-element.124), channel_id=1, source_target_pairs={{0,32},{16,48},{32,64},{48,80},{64,96},{80,112},{96,0},{112,16},{1... | collective-permute-start | bytes 884744 | tf_op jit(solution)/shard_map/ppermute | solution.py:72
  318.5 11.4 %collective-permute-start.33 = (bf16[128,1152]{1,0:T(8,128)(2,1)S(1)}, bf16[128,1152]{1,0:T(8,128)(2,1)S(1)}, u32[]{:S(2)}, u32[]{:S(2)}) collective-permute-start(bf16[128,1152]{1,0:T(8,128)(2,1)S(1)} %get-tuple-element.125), channel_id=1, source_target_pairs={{0,64},{16,80},{32,96},{48,112},{64,0},{80,16},{96,32},{112,48},{1... | collective-permute-start | bytes 884744 | tf_op jit(solution)/shard_map/ppermute | solution.py:72
  319.7 16.4 %collective-permute-start.32 = (bf16[128,1152]{1,0:T(8,128)(2,1)S(1)}, bf16[128,1152]{1,0:T(8,128)(2,1)S(1)}, u32[]{:S(2)}, u32[]{:S(2)}) collective-permute-start(bf16[128,1152]{1,0:T(8,128)(2,1)S(1)} %get-tuple-element.126), channel_id=1, source_target_pairs={{0,96},{16,112},{32,0},{48,16},{64,32},{80,48},{96,64},{112,80},{1... | collective-permute-start | bytes 884744 | tf_op jit(solution)/shard_map/ppermute | solution.py:72
  320.6 20.0 %collective-permute-start.27 = (bf16[192,128]{1,0:T(8,128)(2,1)S(1)}, bf16[192,128]{1,0:T(8,128)(2,1)S(1)}, u32[]{:S(2)}, u32[]{:S(2)}) collective-permute-start(bf16[192,128]{1,0:T(8,128)(2,1)S(1)} %get-tuple-element.131), channel_id=1, source_target_pairs={{0,32},{16,48},{32,64},{48,80},{64,96},{80,112},{96,0},{112,16},{1... | collective-permute-start | bytes 147464 | tf_op jit(solution)/shard_map/ppermute | solution.py:72
  328.1 12.5 %collective-permute-start.29 = (bf16[192,128]{1,0:T(8,128)(2,1)S(1)}, bf16[192,128]{1,0:T(8,128)(2,1)S(1)}, u32[]{:S(2)}, u32[]{:S(2)}) collective-permute-start(bf16[192,128]{1,0:T(8,128)(2,1)S(1)} %get-tuple-element.132), channel_id=1, source_target_pairs={{0,64},{16,80},{32,96},{48,112},{64,0},{80,16},{96,32},{112,48},{1... | collective-permute-start | bytes 147464 | tf_op jit(solution)/shard_map/ppermute | solution.py:72
  329.9 10.7 %collective-permute-start.28 = (bf16[192,128]{1,0:T(8,128)(2,1)S(1)}, bf16[192,128]{1,0:T(8,128)(2,1)S(1)}, u32[]{:S(2)}, u32[]{:S(2)}) collective-permute-start(bf16[192,128]{1,0:T(8,128)(2,1)S(1)} %get-tuple-element.133), channel_id=1, source_target_pairs={{0,96},{16,112},{32,0},{48,16},{64,32},{80,48},{96,64},{112,80},{1... | collective-permute-start | bytes 147464 | tf_op jit(solution)/shard_map/ppermute | solution.py:72
  337.1 13.0 %all-to-all-start.6 = ((bf16[16,8,1152]{2,1,0:T(8,128)(2,1)}), bf16[16,8,1152]{2,1,0:T(8,128)(2,1)S(1)}, u32[]{:S(2)}, u32[]{:S(2)}) async-start(bf16[16,8,1152]{2,1,0:T(8,128)(2,1)} %fusion.16), calls=%async_computation.6 | async-start | bytes 589824 | tf_op jit(solution)/shard_map/all_to_all | solution.py:105
  350.0 42.7 %all-to-all-start.3 = ((bf16[16,80,1024]{2,1,0:T(8,128)(2,1)}), bf16[16,80,1024]{2,1,0:T(8,128)(2,1)}, u32[]{:S(2)}, u32[]{:S(2)}) async-start(bf16[16,80,1024]{2,1,0:T(8,128)(2,1)} %bitcast.89), calls=%async_computation.3 | async-start | bytes 5242880 | tf_op jit(solution)/shard_map/all_to_all | solution.py:105
  358.6 40.9 %collective-permute-start.35 = (bf16[2,384,512]{2,1,0:T(8,128)(2,1)}, bf16[2,384,512]{2,1,0:T(8,128)(2,1)}, u32[]{:S(2)}, u32[]{:S(2)}) collective-permute-start(bf16[2,384,512]{2,1,0:T(8,128)(2,1)} %get-tuple-element.121), channel_id=1, source_target_pairs={{0,32},{16,48},{32,64},{48,80},{64,96},{80,112},{96,0},{112,16},{1... | collective-permute-start | bytes 2359304 | tf_op jit(solution)/shard_map/ppermute | solution.py:72
  359.0 40.5 %collective-permute-start.37 = (bf16[2,384,512]{2,1,0:T(8,128)(2,1)}, bf16[2,384,512]{2,1,0:T(8,128)(2,1)}, u32[]{:S(2)}, u32[]{:S(2)}) collective-permute-start(bf16[2,384,512]{2,1,0:T(8,128)(2,1)} %get-tuple-element.122), channel_id=1, source_target_pairs={{0,64},{16,80},{32,96},{48,112},{64,0},{80,16},{96,32},{112,48},{1... | collective-permute-start | bytes 2359304 | tf_op jit(solution)/shard_map/ppermute | solution.py:72
  360.7 38.8 %collective-permute-start.36 = (bf16[2,384,512]{2,1,0:T(8,128)(2,1)}, bf16[2,384,512]{2,1,0:T(8,128)(2,1)}, u32[]{:S(2)}, u32[]{:S(2)}) collective-permute-start(bf16[2,384,512]{2,1,0:T(8,128)(2,1)} %get-tuple-element.123), channel_id=1, source_target_pairs={{0,96},{16,112},{32,0},{48,16},{64,32},{80,48},{96,64},{112,80},{1... | collective-permute-start | bytes 2359304 | tf_op jit(solution)/shard_map/ppermute | solution.py:72
  392.7 30.1 %all-to-all-start.7 = ((bf16[16,456,128]{2,1,0:T(8,128)(2,1)}), bf16[16,456,128]{2,1,0:T(8,128)(2,1)S(1)}, u32[]{:S(2)}, u32[]{:S(2)}) async-start(bf16[16,456,128]{2,1,0:T(8,128)(2,1)} %pad_maximum_fusion), calls=%async_computation.7 | async-start | bytes 3735552 | tf_op jit(solution)/shard_map/all_to_all | solution.py:105
  (96 other events, 842.3 us)

commit v2 on v1

v2 whole, which is shorter than its diff:
```python
import jax
import jax.numpy as jnp
from jax import lax
from jax.experimental import pallas as pl
from jax.experimental.pallas import tpu as pltpu
from jax.sharding import PartitionSpec as P

D = 1024
HEADS = 16
HD = 64
EF = 512
EXPERTS = 32
CAP = 40
TOK = 128
SEQ = 2048
SIDE = 4
PEERS = 16
DP = 8
QB = 512
HALF = 512
ROWS = PEERS * CAP
EXTRA = 16
PACK = 1152
ROW_STEP = 2 * TOK + EXTRA

eps = 1e-06
theta = 10000.0
masked = -1000000000.0
bf16 = jnp.bfloat16
f32 = jnp.float32
MIB = 1 << 20

NN = (((1,), (0,)), ((), ()))
NT = (((1,), (1,)), ((), ()))
TN = (((0,), (0,)), ((), ()))


def mm(left, right, dims=NN):
    return lax.dot_general(left, right, dims, preferred_element_type=f32)


def shape(dims, dtype):
    return jax.ShapeDtypeStruct(dims, dtype)


def cuts(dims, dtype):
    size = jnp.dtype(dtype).itemsize
    for dim in dims:
        size *= dim
    step = 16 if len(dims) == 2 else 1
    for count in (8, 4, 2):
        if dims[0] % (count * step) == 0 and size // count >= MIB // 4:
            return count
    return 1


class Moved:
    def __init__(self, source, target, sems, first, dims, dtype):
        count = cuts(dims, dtype)
        rows = dims[0] // count
        self.copies = [
            pltpu.make_async_copy(
                source.at[pl.ds(k * rows, rows)], target.at[pl.ds(k * rows, rows)], sems.at[first + k]
            )
            for k in range(count)
        ]
        self.started = False
        self.waited = False

    def start(self):
        self.started = True
        for copy in self.copies:
            copy.start()

    def wait(self):
        if not self.waited:
            self.waited = True
            for copy in self.copies:
                copy.wait()


class In(Moved):
    def __init__(self, source, target, *rest):
        super().__init__(source, target, *rest)
        self.target = target

    def get(self):
        self.wait()
        return self.target


class Out(Moved):
    def __init__(self, source, target, *rest):
        super().__init__(source, target, *rest)
        self.ref = source

    def start_part(self, k):
        self.started = True
        self.copies[k].start()


class Near:
    def __init__(self, array):
        self.array = array


class Held:
    def __init__(self, ref):
        self.ref = ref

    def get(self):
        return self.ref

    def start(self):
        pass


def tied(value, *others):
    return lax.optimization_barrier((value, *others))[0]


def run(body, name, ins, raws, outs, scratch=(), limit=24, after=(), cost=0):
    info, arrays = ins[0], ins[1:]
    in_near = [isinstance(v, Near) for v in arrays]
    out_near = [isinstance(v, Near) for v in outs]
    arrays = [v.array if isinstance(v, Near) else v for v in arrays]
    outs = [v.array if isinstance(v, Near) else v for v in outs]
    both = list(zip((*arrays, *outs), (*in_near, *out_near)))
    count = sum(cuts(v.shape, v.dtype) for v, near in both if not near)
    held = [pltpu.VMEM(v.shape, v.dtype) for v, near in both if not near]

    def kernel(*refs):
        info_ref, refs = refs[0], refs[1:]
        in_refs, refs = refs[: len(arrays)], refs[len(arrays) :]
        raw_refs, refs = refs[: len(raws)], refs[len(raws) :]
        out_refs, refs = refs[: len(outs)], refs[len(outs) :]
        spaces, refs = list(refs[: len(held)]), refs[len(held) :]
        sems, rest = refs[0], refs[1:]
        first = 0
        fetched, sent = [], []
        for v, near, ref in zip(arrays, in_near, in_refs):
            if near:
                fetched.append(Held(ref))
                continue
            fetched.append(In(ref, spaces.pop(0), sems, first, v.shape, v.dtype))
            first += cuts(v.shape, v.dtype)
        for v, near, ref in zip(outs, out_near, out_refs):
            if near:
                sent.append(Held(ref))
                continue
            sent.append(Out(spaces.pop(0), ref, sems, first, v.shape, v.dtype))
            first += cuts(v.shape, v.dtype)
        for one in fetched:
            one.start()
        body(info_ref, fetched, raw_refs, sent, rest)
        for one in fetched:
            one.get()
        moves = [one for one in sent if isinstance(one, Out)]
        for one in moves:
            if not one.started:
                one.start()
        for one in moves:
            one.wait()

    if after:
        info = tied(info, *after)

    def pinned(v, near=False):
        return v if near else pltpu.with_memory_space_constraint(v, pltpu.HBM)

    def spec(near=False):
        return pl.BlockSpec(memory_space=pltpu.VMEM if near else pltpu.HBM)

    return pl.pallas_call(
        kernel,
        name=name,
        out_shape=tuple(
            shape(v.shape, v.dtype) if near else pltpu.HBM(v.shape, v.dtype)
            for v, near in zip(outs, out_near)
        ),
        in_specs=[pl.BlockSpec(memory_space=pltpu.SMEM)]
        + [spec(near) for near in in_near]
        + [spec()] * len(raws),
        out_specs=tuple(spec(near) for near in out_near),
        scratch_shapes=[*held, pltpu.SemaphoreType.DMA((max(count, 1),)), *scratch],
        compiler_params=pltpu.CompilerParams(vmem_limit_bytes=limit * MIB),
        cost_estimate=pl.CostEstimate(
            flops=1000 + cost * 10**9, bytes_accessed=1000, transcendentals=0
        ),
    )(info, *[pinned(v, near) for v, near in zip(arrays, in_near)], *[pinned(v) for v in raws])


def expert_from(values, dz, dx):
    pairs = [
        (z * SIDE + x, ((z - dz) % SIDE) * SIDE + (x - dx) % SIDE)
        for z in range(SIDE)
        for x in range(SIDE)
    ]
    return lax.ppermute(values, "expert", pairs)


def dp_from(values, dy):
    pairs = [(y * 2 + c, ((y - dy) % SIDE) * 2 + c) for y in range(SIDE) for c in range(2)]
    return lax.ppermute(values, "dp", pairs)


def core_swap(values):
    return lax.ppermute(values, "dp", [(d, d ^ 1) for d in range(DP)])


def gather_ring(values, step, *others):
    near = {m: step(values, m) for m in (1, 3)}
    far = step(tied(values, *others) if others else values, 2)
    return [values, near[1], far, near[3]]


def along_z(values, m):
    return expert_from(values, m, 0)


def along_x(values, m):
    return expert_from(values, 0, m)


def gather_dp(values, *others):
    far = {m: dp_from(values, m) for m in (1, 3, 2)}
    if others:
        far[2] = tied(far[2], *others)
    mine = [values, far[1], far[2], far[3]]
    return mine + [core_swap(part) for part in mine]


def send_pairs(pairs):
    return [dp_from(pairs[m], SIDE - m) for m in (1, 3, 2)]


def add_parts(first, others):
    total = first.astype(f32)
    for other in others:
        total = total + other.astype(f32)
    return total


def pair_kernel(info, ins, parts, outs, scratch):
    for m in range(SIDE):
        mine, other = ins[m].get()[...], ins[SIDE + m].get()[...]
        outs[m].ref[...] = (mine.astype(f32) + other.astype(f32)).astype(bf16)
        outs[m].start()


def pair_up(info, mine, other, name):
    swapped = [core_swap(part) for part in other]
    part = shape(mine[0].shape, bf16)
    return run(pair_kernel, name, (info, *mine, *swapped), (), (part,) * SIDE)


def swap_all(values):
    return lax.all_to_all(values, "expert", split_axis=0, concat_axis=0, tiled=True)


def part_place(info, r):
    return ((info[2] + r % SIDE) % SIDE) * 2 + (info[3] ^ (r // SIDE))


def aligned(index, step):
    return pl.ds(pl.multiple_of(index * step, step), step)


def rotated(values, c, s):
    w1, w2 = values[: HD // 2], values[HD // 2 :]
    return jnp.concatenate([w1 * c - w2 * s, w2 * c + w1 * s], axis=0)


def rotated_back(values, c, s):
    w1, w2 = values[: HD // 2], values[HD // 2 :]
    return jnp.concatenate([w1 * c + w2 * s, w2 * c - w1 * s], axis=0)


def allowed(ki, qi, start):
    key = ki * QB + lax.broadcasted_iota(jnp.int32, (QB, QB), 0)
    keep = key >= start
    if ki == qi:
        keep = keep & (key <= qi * QB + lax.broadcasted_iota(jnp.int32, (QB, QB), 1))
    return keep


def place_parts(info, parts, pieces, sems, place=part_place):
    copies = []
    for r in range(8):
        for k, piece in enumerate(pieces):
            source, target = piece(parts[r], place(info, r))
            copies.append(pltpu.make_async_copy(source, target, sems.at[r * len(pieces) + k]))
    for copy in copies:
        copy.start()
    return copies


def wait_all(copies):
    for copy in copies:
        copy.wait()


def dense_kernel(info, ins, parts, outs, scratch):
    router, gain_attn, gain_ffn, routes = ins
    query, key, value, cot, states = parts
    dense, cots = [out.ref for out in outs]
    sems = scratch[0]
    copies = [
        pltpu.make_async_copy(source, target, sems.at[k])
        for k, (source, target) in enumerate(
            (
                (query, dense.at[pl.ds(0, TOK), pl.ds(0, 1024)]),
                (key, dense.at[pl.ds(0, TOK), pl.ds(1024, 512)]),
                (value, dense.at[pl.ds(0, TOK), pl.ds(1536, 512)]),
                (cot, cots.at[pl.ds(0, TOK), :]),
                (states, cots.at[pl.ds(TOK + EXTRA, TOK), :]),
            )
        )
    ]
    for copy in copies:
        copy.start()
    rows = slice(TOK, TOK + EXTRA)
    dense[rows, 384:2048] = jnp.zeros((EXTRA, 2048 - 384), bf16)
    dense[rows, 0:128] = router.get()[0:EXTRA, :]
    dense[rows, 128:256] = router.get()[EXTRA : 2 * EXTRA, :]
    gains = [gain_attn.get()[...].astype(f32), gain_ffn.get()[...].astype(f32)]
    gains = jnp.concatenate([*gains, jnp.zeros((EXTRA - 2, TOK), f32)], axis=0)
    dense[rows, 256:384] = gains.astype(bf16)
    cots[rows, TOK:D] = jnp.zeros((EXTRA, D - TOK), bf16)
    names = jnp.concatenate([routes.get()[...].astype(f32), jnp.zeros((8, TOK), f32)], axis=0)
    cots[rows, 0:TOK] = names.astype(bf16)
    wait_all(copies)


def pack_kernel(info, ins, parts, outs, scratch):
    gate, up, down = parts
    packed = outs[0].ref
    sems = scratch[0]
    pairs = []
    for i in range(2):
        for k, source in enumerate(
            (
                gate.at[i],
                up.at[i],
                down.at[i, :, pl.ds(0, HALF)],
                down.at[i, :, pl.ds(HALF, HALF)],
            )
        ):
            row, count = i * 384 + (0, 128, 256, 320)[k], (128, 128, 64, 64)[k]
            pairs.append((source, packed.at[pl.ds(row, count), :]))
    copies = [
        pltpu.make_async_copy(source, target, sems.at[k])
        for k, (source, target) in enumerate(pairs)
    ]
    for copy in copies:
        copy.start()
    wait_all(copies)


def qkv_kernel(info, ins, parts, outs, scratch):
    states, cos, sin = ins
    small, send = outs
    wide, sems = scratch
    copies = place_parts(
        info,
        parts,
        [
            lambda part, d: (part.at[pl.ds(0, TOK), :], wide.at[aligned(d, TOK), :]),
            *(
                lambda part, d, k=k: (
                    part.at[pl.ds(TOK, EXTRA), pl.ds(128 * k, 128)],
                    small.ref.at[pl.ds(EXTRA * k, EXTRA), aligned(d, TOK)],
                )
                for k in range(3)
            ),
        ],
        sems,
    )
    x = states.get()[...].astype(f32)
    r = lax.rsqrt(jnp.mean(x * x, axis=-1, keepdims=True) + eps)
    cos, sin = cos.get()[...], sin.get()[...]
    wait_all(copies)
    small.start()
    gain = small.ref[2 * EXTRA : 3 * EXTRA, :].astype(f32)[0:1, :]
    low = (x * r * gain).astype(bf16)
    turned = mm(low, wide[:, 1024:2048]).T
    for g in range(HEADS // 2):
        key = rotated(turned[g * HD : (g + 1) * HD], cos, sin)
        value = turned[512 + g * HD : 512 + (g + 1) * HD]
        both = jnp.concatenate([key, value], axis=0).astype(bf16)
        send.ref[2 * g, HD : 3 * HD, :] = both
        send.ref[2 * g + 1, HD : 3 * HD, :] = both
    turned = mm(low, wide[:, 0:1024]).T
    for h in range(HEADS):
        query = rotated(turned[h * HD : (h + 1) * HD], cos, sin).astype(bf16).astype(f32)
        send.ref[h, 0:HD, :] = (query * (HD**-0.5)).astype(bf16)


def spread_heads(arrived, qz, kvt, kvn):
    for i in range(SEQ // QB):
        span = slice(i * QB, (i + 1) * QB)
        got = jnp.concatenate([arrived[i * 4 + j] for j in range(4)], axis=1)
        qz[0:HD, span] = got[0:HD]
        qz[HD:128, span] = jnp.zeros((HD, QB), bf16)
        kvt[:, span] = got[HD : 3 * HD]
        kvn[span, :] = got[HD : 3 * HD].astype(f32).T.astype(bf16)


def attend_kernel(info, ins, parts, outs, scratch):
    start = ins[1].get()
    out_t, lse, send = outs
    qz, kvt, kvn = scratch
    spread_heads(ins[0].get(), qz, kvt, kvn)
    for qi in range(SEQ // QB):
        span = slice(qi * QB, (qi + 1) * QB)
        query = qz[:, span]
        top = jnp.full((1, QB), -jnp.inf, f32)
        total = jnp.zeros((1, QB), f32)
        mixed = jnp.zeros((HD, QB), f32)
        for ki in range(qi, -1, -1):
            keys = slice(ki * QB, (ki + 1) * QB)
            scores = jnp.where(allowed(ki, qi, start[:, span]), mm(kvn[keys, :], query), masked)
            higher = jnp.maximum(top, jnp.max(scores, axis=0, keepdims=True))
            weights = jnp.exp(scores - higher)
            shrink = jnp.exp(top - higher)
            total = total * shrink + jnp.sum(weights, axis=0, keepdims=True)
            mixed = mixed * shrink + mm(kvt[HD:128, keys], weights.astype(bf16))
            top = higher
        mixed = mixed / total
        lse.ref[:, span] = top + jnp.log(total)
        out_t.ref[:, span] = mixed
        for j in range(QB // TOK):
            send.ref[qi * (QB // TOK) + j] = mixed[:, j * TOK : (j + 1) * TOK].astype(bf16)


def shards(gathered):
    return [gathered.at[d] for d in range(DP)]


def shard_place(info, r):
    return r


def w_out_pieces(target):
    return [lambda part, d: (part.at[:, :], target.at[aligned(d, TOK), :])]


def ranks(choose):
    order = lax.broadcasted_iota(jnp.int32, (TOK, TOK), 0)
    before = (order < lax.broadcasted_iota(jnp.int32, (TOK, TOK), 1)).astype(bf16)
    return mm(choose.astype(bf16), before).astype(jnp.int32)


def project_kernel(info, ins, parts, outs, scratch):
    mixed_t, states, small, routes = ins
    hidden, send, table = outs
    w_out, sems = scratch
    copies = place_parts(info, parts, w_out_pieces(w_out), sems)
    names = lax.broadcasted_iota(jnp.int32, (EXPERTS, TOK), 0)
    choose = jnp.zeros((EXPERTS, TOK), f32)
    routes = routes.get()
    for j in range(8):
        choose = choose + (names == routes[j : j + 1, :]).astype(f32)
    rank = jnp.where(choose > 0.0, ranks(choose), -1)
    slots = lax.broadcasted_iota(jnp.int32, (CAP, TOK), 0)
    for e in range(0, EXPERTS, 2):
        table.ref[e * CAP : (e + 2) * CAP, :] = jnp.concatenate(
            [(rank[e : e + 1] == slots).astype(f32), (rank[e + 1 : e + 2] == slots).astype(f32)],
            axis=0,
        ).astype(bf16)
    mixed = mixed_t.get()[...].astype(f32).T.astype(bf16)
    gain = small.get()[2 * EXTRA : 3 * EXTRA, :].astype(f32)[1:2, :]
    wait_all(copies)
    value = states.get()[...].astype(f32) + mm(mixed, w_out[...])
    hidden.ref[...] = value
    r = lax.rsqrt(jnp.mean(value * value, axis=-1, keepdims=True) + eps)
    ffn = (value * r * gain).astype(bf16)
    step = 2 * ROWS // len(send.copies)
    for k in range(len(send.copies)):
        rows = slice(k * step, (k + 1) * step)
        send.ref[rows, :] = mm(table.ref[rows, :], ffn).astype(bf16)
        send.start_part(k)


def rows_kernel(info, ins, parts, outs, scratch):
    grads, slots = outs
    cots, choose, spread, sems = scratch
    first = (info[0] * SIDE + info[1]) * 2
    copies = [
        pltpu.make_async_copy(
            parts[0].at[pl.ds(t * ROW_STEP, TOK + EXTRA), :], cots.at[t], sems.at[t]
        )
        for t in range(PEERS)
    ]
    for copy in copies:
        copy.start()
    wait_all(copies)
    for t in range(PEERS):
        routes = cots[t, TOK : TOK + EXTRA, 0:TOK].astype(f32)[0:8, :].astype(jnp.int32)
        for i in range(2):
            named = (routes == first + i).astype(f32)
            choose[2 * t + i : 2 * t + i + 1, :] = jnp.sum(named, axis=0, keepdims=True)
    rank = jnp.where(choose[...] > 0.0, ranks(choose[...]), -1)
    order = lax.broadcasted_iota(jnp.int32, (CAP, TOK), 0)
    for t in range(PEERS):
        hot = jnp.concatenate(
            [(rank[2 * t + i : 2 * t + i + 1] == order).astype(f32) for i in range(2)], axis=0
        )
        slots.ref[t] = hot.astype(bf16)
        rows = mm(hot.astype(bf16), cots[t, 0:TOK, :])
        for i in range(2):
            spread[i, t * CAP : (t + 1) * CAP, :] = rows[i * CAP : (i + 1) * CAP]
    for i in range(2):
        grads.ref[i] = spread[i].astype(bf16)


def norm_kernel(info, ins, parts, outs, scratch):
    gain = ins[0].get()[2 * EXTRA : 3 * EXTRA, :].astype(f32)[0:1, :]
    normed = outs[0]
    rows, sems = scratch
    copies = [
        pltpu.make_async_copy(
            parts[0].at[pl.ds(t * ROW_STEP + TOK + EXTRA, TOK), :], rows.at[t], sems.at[t]
        )
        for t in range(PEERS)
    ]
    for copy in copies:
        copy.start()
    step = PEERS // len(normed.copies)
    for t in range(PEERS):
        copies[t].wait()
        x = rows[t].astype(f32)
        r = lax.rsqrt(jnp.mean(x * x, axis=-1, keepdims=True) + eps)
        normed.ref[t * TOK : (t + 1) * TOK, :] = (x * r * gain).astype(bf16)
        if t % step == step - 1:
            normed.start_part(t // step)


def unweave(source, spread, target):
    for s in range(PEERS):
        rows = source[s * 2 * CAP : (s + 1) * 2 * CAP, :].astype(f32)
        spread[0, s * CAP : (s + 1) * CAP, :] = rows[0:CAP]
        spread[1, s * CAP : (s + 1) * CAP, :] = rows[CAP : 2 * CAP]
    for i in range(2):
        target[i] = spread[i].astype(bf16)


def weave(spread, sent):
    for s in range(PEERS):
        rows = slice(s * CAP, (s + 1) * CAP)
        sent.ref[s * 2 * CAP : (s + 1) * 2 * CAP, :] = jnp.concatenate(
            [spread[0, rows, :], spread[1, rows, :]], axis=0
        ).astype(bf16)
        if s % 2 == 1:
            sent.start_part(s // 2)


def expert_kernel(info, ins, parts, outs, scratch):
    arrived, grads, small = ins
    sent, xs, acted, dgate, dup, gates, lgs = [out.ref for out in outs]
    spread, wg, wu, wd, sems = scratch

    def piece(i, k):
        first, count, target, column = (
            (0, TOK, wg, 0),
            (128, TOK, wu, 0),
            (256, HD, wd, 0),
            (320, HD, wd, HALF),
        )[k]
        return lambda part, d: (
            part.at[pl.ds(i * 384 + first, count), :],
            target.at[i, aligned(d, count), pl.ds(column, HALF)],
        )

    copies = place_parts(
        info,
        shards(parts[0]),
        [piece(i, k) for i in range(2) for k in range(4)],
        sems,
        shard_place,
    )
    unweave(arrived.get(), spread, xs)
    outs[1].start()
    grads = grads.get()
    small = small.get()
    wait_all(copies)
    first = (info[0] * SIDE + info[1]) * 2
    chunk = ROWS // 2

    def step(n, carry):
        i = n // 2
        rows = aligned(n % 2, chunk)
        x = xs[i, rows, :]
        router = small[0 : 2 * EXTRA, :]
        logits = mm(x, router, NT)
        peak = jnp.max(logits, axis=-1, keepdims=True)
        chances = jnp.exp(logits - peak)
        chances = chances / jnp.sum(chances, axis=-1, keepdims=True)
        mine = (lax.broadcasted_iota(jnp.int32, (chunk, EXPERTS), 1) == first + i).astype(f32)
        gate = jnp.sum(chances * mine, axis=-1, keepdims=True)
        gate_pre = mm(x, wg[i])
        up_pre = mm(x, wu[i])
        sigmoid = 1.0 / (1.0 + jnp.exp(-gate_pre))
        silu = gate_pre * sigmoid
        act = (silu * up_pre).astype(bf16)
        acted[i, rows, :] = act
        back = mm(grads[i, rows, :], wd[i], NT)
        dot = jnp.sum(act.astype(f32) * back, axis=-1, keepdims=True)
        back = back * gate
        gate_grad = (back * up_pre * (sigmoid * (1.0 + gate_pre * (1.0 - sigmoid)))).astype(bf16)
        up_grad = (back * silu).astype(bf16)
        dgate[i, rows, :] = gate_grad
        dup[i, rows, :] = up_grad
        lg = (dot * gate * (mine - chances)).astype(bf16)
        lgs[i, rows, :] = jnp.concatenate([lg, jnp.zeros((chunk, 128 - EXPERTS), bf16)], axis=1)
        gates[i, rows, :] = jnp.broadcast_to(gate, (chunk, 128))
        spread[i, rows, :] = (
            mm(gate_grad, wg[i], NT) + mm(up_grad, wu[i], NT) + mm(lg, router)
        )
        return carry

    lax.fori_loop(0, 4, step, 0)
    for one in outs[2:]:
        one.start()
    weave(spread, outs[0])


def weights_kernel(info, ins, parts, outs, scratch):
    xs, gs, acted, dgate, dup, gates, lgs, slots = ins
    routed, router_grad = outs[0].ref, outs[9].ref
    mine, other = [out.ref for out in outs[1:5]], [out.ref for out in outs[5:9]]
    spread, wd, sums, down_sums, sems = scratch
    def piece(i, k):
        return lambda part, d: (
            part.at[pl.ds(i * 384 + 256 + HD * k, HD), :],
            wd.at[i, aligned(d, HD), pl.ds(k * HALF, HALF)],
        )

    copies = place_parts(
        info,
        shards(parts[0]),
        [piece(i, k) for i in range(2) for k in range(2)],
        sems,
        shard_place,
    )
    xs, gs, acted, dgate, dup, gates, lgs, slots = [one.get() for one in ins]
    wait_all(copies)
    router_grad[...] = jnp.zeros_like(router_grad)

    def step(i, carry):
        source = xs[i]
        gate = gates[i][:, 0:1]
        spread[i] = mm(acted[i], wd[i]) * gate
        slot_grad = (gs[i].astype(f32) * gate).astype(bf16)
        router_grad[...] += mm(lgs[i], source, TN)
        sums[0] = mm(source, dgate[i], TN).astype(bf16)
        sums[1] = mm(source, dup[i], TN).astype(bf16)
        down_sums[...] = mm(acted[i], slot_grad, TN).astype(bf16)
        for r in range(8):
            d = part_place(info, r)
            target = (*mine, *other)[r]
            target[i, 0:128, :] = sums[0, aligned(d, TOK), :]
            target[i, 128:256, :] = sums[1, aligned(d, TOK), :]
            target[i, 256:320, :] = down_sums[aligned(d, HD), 0:HALF]
            target[i, 320:384, :] = down_sums[aligned(d, HD), HALF:D]
        return carry

    lax.fori_loop(0, 2, step, 0)
    for one in (*outs[5:9], *outs[1:5]):
        one.start()
    for t in range(PEERS):
        span = slice(t * CAP, (t + 1) * CAP)
        rows = jnp.concatenate([spread[i, span, :] for i in range(2)], axis=0).astype(bf16)
        routed[t * TOK : (t + 1) * TOK, :] = mm(slots[t], rows, TN).astype(bf16)


def hidden_kernel(info, ins, parts, outs, scratch):
    arrived, table, hidden, cot, small = ins
    hidden_grad, low, send, gain_grad = outs
    w_out, sems = scratch
    copies = place_parts(info, parts, w_out_pieces(w_out), sems)
    grad = mm(table.get()[...], arrived.get()[...], TN)
    hidden = hidden.get()[...]
    gain = small.get()[2 * EXTRA : 3 * EXTRA, :].astype(f32)[1:2, :]
    r = lax.rsqrt(jnp.mean(hidden * hidden, axis=-1, keepdims=True) + eps)
    scaled = grad * gain
    dot = jnp.mean(scaled * hidden, axis=-1, keepdims=True)
    total = cot.get()[...].astype(f32) + r * scaled - hidden * (r * r * r * dot)
    gain_grad.ref[...] = jnp.sum(grad * hidden * r, axis=0, keepdims=True)
    hidden_grad.ref[...] = total
    low.ref[...] = total.astype(bf16)
    wait_all(copies)
    turned = mm(w_out[...], low.ref[...], NT).astype(bf16)
    send.ref[...] = turned.reshape(HEADS, HD, TOK)


def out_weights_kernel(info, ins, parts, outs, scratch):
    mixed_t, low, router_grad, gain_grad = [one.get() for one in ins]
    extra = scratch[0]
    block = jnp.concatenate(
        [
            router_grad[0:EXPERTS, :],
            jnp.broadcast_to(gain_grad[...], (8, D)),
            jnp.zeros((128 - EXPERTS - 8, D), f32),
        ],
        axis=0,
    )
    extra[...] = block.T
    for r in (4, 5, 6, 7, 0, 1, 2, 3):
        rows = aligned(part_place(info, r), TOK)
        target = outs[r].ref
        target[:, 0:D] = mm(mixed_t[rows, :], low[...]).astype(bf16)
        target[:, D:PACK] = extra[rows, :].astype(bf16)
        outs[r].start()


def attend_back_kernel(info, ins, parts, outs, scratch):
    heads, out_t, lse, arrived, cos, sin, start = [one.get() for one in ins[0:7]]
    send = outs[0].ref
    qz, kvt, kvn, oz, qon, dq, low, delta, sums = scratch
    steps = SEQ // QB
    spread_heads(heads, qz, kvt, kvn)
    for i in range(steps):
        span = slice(i * QB, (i + 1) * QB)
        got = jnp.concatenate([arrived[i * 4 + j] for j in range(4)], axis=1)
        oz[0:HD, span] = jnp.zeros((HD, QB), bf16)
        oz[HD:128, span] = got
        wide = got.astype(f32)
        delta[:, span] = jnp.sum(wide * out_t[:, span], axis=0, keepdims=True)
        qon[span, :] = jnp.concatenate([qz[0:HD, span].astype(f32), wide], axis=0).T.astype(bf16)
        dq[:, span] = jnp.zeros((HD, QB), f32)
    for ki in range(steps):
        keys = slice(ki * QB, (ki + 1) * QB)
        value_sum = jnp.zeros((QB, 128), f32)
        key_sum = jnp.zeros((QB, 128), f32)
        for qi in range(ki, steps):
            span = slice(qi * QB, (qi + 1) * QB)
            scores = mm(kvn[keys, :], qz[:, span])
            expo = jnp.where(
                allowed(ki, qi, start[:, span]), jnp.exp(scores - lse[:, span]), 0.0
            )
            back = mm(kvn[keys, :], oz[:, span])
            score_grad = (expo * (back - delta[:, span])).astype(bf16)
            value_sum = value_sum + mm(expo.astype(bf16), qon[span, :])
            key_sum = key_sum + mm(score_grad, qon[span, :])
            dq[:, span] += mm(kvt[0:HD, keys], score_grad)
        lane = lax.broadcasted_iota(jnp.int32, (QB, 128), 1)
        turned = jnp.where(lane < HD, key_sum, value_sum).T
        low[HD : 2 * HD, keys] = rotated_back(turned[0:HD], cos[:, keys], sin[:, keys]).astype(bf16)
        low[2 * HD : 3 * HD, keys] = turned[HD:128].astype(bf16)
    for i in range(steps):
        span = slice(i * QB, (i + 1) * QB)
        low[0:HD, span] = rotated_back(
            dq[:, span] * (HD**-0.5), cos[:, span], sin[:, span]
        ).astype(bf16)
    for j in range(PEERS):
        send[j] = low[:, j * TOK : (j + 1) * TOK]
    outs[0].start()
    total = mm(low[...], ins[7].get()[...]).astype(bf16)
    for d in range(DP):
        sums[d] = total[:, d * TOK : (d + 1) * TOK]
    for r in (4, 5, 6, 7, 0, 1, 2, 3):
        outs[1 + r].ref[...] = sums[part_place(info, r)]
        outs[1 + r].start()


def input_kernel(info, ins, parts, outs, scratch):
    arrived, hidden_grad, states, small = ins[0:4]
    grad, query, key, value, out, router, rest = [one.ref for one in outs]
    wide, sums, sems = scratch
    copies = place_parts(
        info,
        parts,
        [lambda part, d: (part.at[pl.ds(0, TOK), :], wide.at[aligned(d, TOK), :])],
        sems,
    )
    arrived = arrived.get()

    def pair_sum(first, count):
        pairs = arrived[:, first : first + count, :].astype(f32).reshape(HEADS // 2, 2, count, TOK)
        return (pairs[:, 0] + pairs[:, 1]).reshape(HEADS // 2 * count, TOK)

    dq = arrived[:, 0:HD, :].astype(f32).reshape(HEADS * HD, TOK).T.astype(bf16)
    dk = pair_sum(HD, HD).T.astype(bf16)
    dv = pair_sum(2 * HD, HD).T.astype(bf16)
    query[...] = arrived[:, 192 : 192 + HD, :].astype(f32).reshape(HEADS * HD, TOK).T
    key[...] = pair_sum(192 + HD, HD).T
    value[...] = pair_sum(192 + 2 * HD, HD).T
    for j in range(PEERS):
        rows = arrived[j, 384:456, :].astype(f32)
        for g in range(9):
            target = out.at[:, g * 128 : (g + 1) * 128] if g < 8 else sums
            target[j * 8 : (j + 1) * 8, :] = rows[g * 8 : (g + 1) * 8, :]
    for one in outs[1:5]:
        one.start()
    turned = sums[...].T
    router[...] = turned[0:EXPERTS, :]
    rest[1:2, :] = turned[EXPERTS : EXPERTS + 1, :]
    weighted = sum(
        jnp.sum(total[...] * own.get()[...].astype(f32), axis=-1, keepdims=True)
        for total, own in zip((query, key, value), ins[4:7])
    )
    weighted = jnp.concatenate([weighted, jnp.zeros((TOK, 127), f32)], axis=1).T
    rest[0:1, :] = weighted[0:1, :] / ins[7].get()[...].astype(f32)
    wait_all(copies)
    back = (
        mm(dq, wide[:, 0:1024], NT)
        + mm(dk, wide[:, 1024:1536], NT)
        + mm(dv, wide[:, 1536:2048], NT)
    )
    x = states.get()[...].astype(f32)
    gain = small.get()[2 * EXTRA : 3 * EXTRA, :].astype(f32)[0:1, :]
    r = lax.rsqrt(jnp.mean(x * x, axis=-1, keepdims=True) + eps)
    scaled = back * gain
    dot = jnp.mean(scaled * x, axis=-1, keepdims=True)
    grad[...] = hidden_grad.get()[...] + r * scaled - x * (r * r * r * dot)


def per_device(
    inputs,
    segments,
    routes,
    gain_attn,
    w_query,
    w_key,
    w_value,
    w_out,
    gain_ffn,
    w_router,
    expert_gate,
    expert_up,
    expert_down,
    cotangent,
):
    place = lax.axis_index("expert")
    row = lax.axis_index("dp")
    info = jnp.stack([place // SIDE, place % SIDE, row // 2, row % 2]).astype(jnp.int32)
    states = inputs[0]
    cot = cotangent[0]
    my_routes = routes[0].T

    segment_row = segments[0][None, :]
    index = jnp.arange(SEQ, dtype=jnp.int32)[None, :]
    start = jnp.zeros((1, SEQ), jnp.int32)
    for s in range(3):
        count = jnp.sum((segment_row == s).astype(jnp.int32))
        start = start + jnp.where(segment_row > s, count, 0)
    freqs = theta ** (-jnp.arange(0, HD, 2, dtype=f32) / HD)
    angles = freqs[:, None] * (index - start).astype(f32)
    cosine, sine = jnp.cos(angles), jnp.sin(angles)
    my_angles = lax.dynamic_slice_in_dim(angles, place * TOK, TOK, 1)
    my_cosine, my_sine = jnp.cos(my_angles), jnp.sin(my_angles)

    packed = run(
        pack_kernel,
        "pack",
        (info,),
        (expert_gate, expert_up, expert_down),
        (shape((768, HALF), bf16),),
        (pltpu.SemaphoreType.DMA((8,)),),
    )[0]
    dense, cots = run(
        dense_kernel,
        "dense",
        (info, w_router.T, Near(gain_attn[None, :]), Near(gain_ffn[None, :]), Near(my_routes)),
        (w_query, w_key, w_value, cot, states),
        (shape((TOK + EXTRA, 2048), bf16), shape((ROW_STEP, D), bf16)),
        (pltpu.SemaphoreType.DMA((5,)),),
    )
    cots = lax.all_gather(cots, "expert", axis=0, tiled=True)
    dense = gather_dp(dense, packed, cosine, sine, my_cosine, my_sine)

    small, heads = run(
        qkv_kernel,
        "qkv",
        (info, states, Near(my_cosine), Near(my_sine)),
        dense,
        (
            shape((3 * EXTRA, D), bf16),
            shape((HEADS, 3 * HD, TOK), bf16),
        ),
        (pltpu.VMEM((D, 2048), bf16), pltpu.SemaphoreType.DMA((32,))),
        cost=25,
    )
    heads = swap_all(heads)

    packed = lax.all_gather(tied(packed, small), "dp", axis=0)
    outward = gather_dp(tied(w_out, small))

    out_t, lse, mixed_send = run(
        attend_kernel,
        "attend",
        (info, Near(heads), Near(start)),
        (),
        (
            shape((HD, SEQ), f32),
            shape((1, SEQ), f32),
            shape((HEADS, HD, TOK), bf16),
        ),
        (
            pltpu.VMEM((128, SEQ), bf16),
            pltpu.VMEM((128, SEQ), bf16),
            pltpu.VMEM((SEQ, 128), bf16),
        ),
        cost=30,
    )
    mixed_t = swap_all(mixed_send).reshape(HEADS * HD, TOK)

    hidden, send, table = run(
        project_kernel,
        "project",
        (info, Near(mixed_t), states, small, my_routes),
        outward,
        (shape((TOK, D), f32), shape((2 * ROWS, D), bf16), shape((2 * ROWS, TOK), bf16)),
        (pltpu.VMEM((D, D), bf16), pltpu.SemaphoreType.DMA((8,))),
        cost=25,
    )
    arrived = swap_all(send)

    grad_rows, slots = run(
        rows_kernel,
        "grad_rows",
        (info,),
        (cots,),
        (shape((2, ROWS, D), bf16), shape((PEERS, 2 * CAP, TOK), bf16)),
        (
            pltpu.VMEM((PEERS, TOK + EXTRA, D), bf16),
            pltpu.VMEM((2 * PEERS, TOK), f32),
            pltpu.VMEM((2, ROWS, D), f32),
            pltpu.SemaphoreType.DMA((PEERS,)),
        ),
        limit=32,
    )
    sent_grad, xs, acted, dgate, dup, gates, lgs = run(
        expert_kernel,
        "experts",
        (info, Near(arrived), grad_rows, small),
        (packed,),
        (
            shape((2 * ROWS, D), bf16),
            shape((2, ROWS, D), bf16),
            shape((2, ROWS, EF), bf16),
            shape((2, ROWS, EF), bf16),
            shape((2, ROWS, EF), bf16),
            shape((2, ROWS, 128), f32),
            shape((2, ROWS, 128), bf16),
        ),
        (
            pltpu.VMEM((2, ROWS, D), f32),
            pltpu.VMEM((2, D, EF), bf16),
            pltpu.VMEM((2, D, EF), bf16),
            pltpu.VMEM((2, EF, D), bf16),
            pltpu.SemaphoreType.DMA((64,)),
        ),
        limit=40,
        cost=60,
    )
    back = swap_all(sent_grad)

    routed, *expert_grads, router_grad = run(
        weights_kernel,
        "weights",
        (info, xs, grad_rows, acted, dgate, dup, gates, lgs, slots),
        (packed,),
        (
            shape((SEQ, D), bf16),
            *(shape((2, 384, 512), bf16),) * 8,
            shape((128, D), f32),
        ),
        (
            pltpu.VMEM((2, ROWS, D), f32),
            pltpu.VMEM((2, EF, D), bf16),
            pltpu.VMEM((2, D, EF), bf16),
            pltpu.VMEM((EF, D), bf16),
            pltpu.SemaphoreType.DMA((32,)),
        ),
        limit=40,
    )
    expert_pairs = pair_up(info, expert_grads[0:4], expert_grads[4:8], "expert_pairs")
    expert_far = send_pairs(expert_pairs)

    normed = run(
        norm_kernel,
        "normed",
        (info, small),
        (cots,),
        (shape((SEQ, D), bf16),),
        (pltpu.VMEM((PEERS, TOK, D), bf16), pltpu.SemaphoreType.DMA((PEERS,))),
        after=(sent_grad,),
    )[0]

    hidden_grad, low, grad_send, gain_grad = run(
        hidden_kernel,
        "hidden_grad",
        (info, Near(back), table, hidden, cot, small),
        outward,
        (
            shape((TOK, D), f32),
            shape((TOK, D), bf16),
            shape((HEADS, HD, TOK), bf16),
            shape((1, D), f32),
        ),
        (pltpu.VMEM((D, D), bf16), pltpu.SemaphoreType.DMA((8,))),
        after=(router_grad, normed, *expert_pairs),
        cost=20,
    )
    mixed_grad = swap_all(grad_send)

    out_grads = run(
        out_weights_kernel,
        "out_weights",
        (info, Near(mixed_t), low, router_grad, gain_grad),
        (),
        (shape((TOK, PACK), bf16),) * 8,
        (pltpu.VMEM((D, 128), f32),),
    )
    out_pairs = pair_up(info, out_grads[0:4], out_grads[4:8], "out_pairs")

    routed = lax.psum_scatter(tied(routed, low), "expert", scatter_dimension=0, tiled=True)
    output = (hidden + routed.astype(f32)).astype(bf16)

    grads_send, *w_grads = run(
        attend_back_kernel,
        "attend_back",
        (info, heads, out_t, lse, Near(mixed_grad), cosine, sine, start, normed),
        (),
        (
            shape((PEERS, 192, TOK), bf16),
            *(shape((192, TOK), bf16),) * 8,
        ),
        (
            pltpu.VMEM((128, SEQ), bf16),
            pltpu.VMEM((128, SEQ), bf16),
            pltpu.VMEM((SEQ, 128), bf16),
            pltpu.VMEM((128, SEQ), bf16),
            pltpu.VMEM((SEQ, 128), bf16),
            pltpu.VMEM((HD, SEQ), f32),
            pltpu.VMEM((192, SEQ), bf16),
            pltpu.VMEM((1, SEQ), f32),
            pltpu.VMEM((DP, 192, TOK), bf16),
        ),
        limit=32,
        after=out_pairs,
        cost=60,
    )
    w_pairs = [
        (mine.astype(f32) + core_swap(other).astype(f32)).astype(bf16)
        for mine, other in zip(w_grads[0:4], w_grads[4:8])
    ]
    w_sums = add_parts(w_pairs[0], send_pairs(w_pairs)).astype(bf16)
    expert_sums = add_parts(expert_pairs[0], expert_far)
    out_sums = add_parts(out_pairs[0], send_pairs(out_pairs)).astype(bf16)
    out_sums = swap_all(out_sums).reshape(PEERS, 8, PACK)
    out_sums = jnp.sum(out_sums.astype(f32), axis=0).astype(bf16)
    out_sums = jnp.concatenate([out_sums[:, g * 128 : (g + 1) * 128] for g in range(9)], axis=0)

    ends = jnp.concatenate([w_sums, out_sums], axis=0)
    last = jnp.concatenate(
        [grads_send, jnp.broadcast_to(ends[None], (PEERS, 264, TOK))], axis=1
    )
    last = swap_all(last)

    grad_input, sum_query, sum_key, sum_value, sum_out, sum_router, sum_gains = run(
        input_kernel,
        "grad_input",
        (info, Near(last), hidden_grad, states, small, w_query, w_key, w_value, gain_attn[None, :]),
        dense,
        (
            shape((TOK, D), f32),
            shape((TOK, 1024), f32),
            shape((TOK, 512), f32),
            shape((TOK, 512), f32),
            shape((TOK, D), f32),
            Near(shape((EXPERTS, TOK), f32)),
            Near(shape((2, TOK), f32)),
        ),
        (
            pltpu.VMEM((D, 2048), bf16),
            pltpu.VMEM((TOK, 128), f32),
            pltpu.SemaphoreType.DMA((8,)),
        ),
        limit=32,
        after=(output,),
        cost=35,
    )
    return (
        output[None],
        grad_input[None],
        sum_gains[0],
        sum_query,
        sum_key,
        sum_value,
        sum_out,
        sum_gains[1],
        sum_router.T,
        expert_sums[:, 0:128],
        expert_sums[:, 128:256],
        jnp.concatenate([expert_sums[:, 256:320], expert_sums[:, 320:384]], axis=2),
    )


def solution(mesh):
    placed = (
        P("dp", "expert", None),
        P("dp", None),
        P("dp", "expert", None),
        P("dp"),
        P("dp", None),
        P("dp", None),
        P("dp", None),
        P("dp", None),
        P("dp"),
        P("dp", None),
        P("expert", "dp", None),
        P("expert", "dp", None),
        P("expert", "dp", None),
        P("dp", "expert", None),
    )
    return jax.shard_map(
        per_device,
        mesh=mesh,
        in_specs=placed,
        out_specs=(
            P("dp", "expert", None),
            P("dp", "expert", None),
            P("dp"),
            P("dp", None),
            P("dp", None),
            P("dp", None),
            P("dp", None),
            P("dp"),
            P("dp", None),
            P("expert", "dp", None),
            P("expert", "dp", None),
            P("expert", "dp", None),
        ),
        check_vma=False,
    )
```

time: 450 us -> 347 us (0.77)
  the two profiles are of different devices: /device:TPU:24 before, /device:TPU:0 now
where the time goes in v2:
time: 347 us; the launch traced here: 342 us
  waiting for transfers between devices  126 us (36%)
  Pallas kernels  106 us (31%)
  starting transfers between devices  71.8 us (21%)
  other arithmetic  15.1 us (4%)
  between operations  14.7 us (4%)
  local copies, waits for them, and re-layouts  7.53 us (2%)
    pallas_call x15, Pallas kernels, run(): pl.pallas_call(kernel, name=name, out_shape=tuple((shape(v.shape, v.dtype...  106 us
    ppermute x15, waiting for transfers between devices, dp_from(): return lax.ppermute(values, 'dp', pairs)  58.9 us
    all_to_all x7, waiting for transfers between devices, swap_all(): lax.all_to_all(values, 'expert', split_axis=0, concat_axis=0, tiled=True)  55.3 us
    all_to_all x7, starting transfers between devices, swap_all(): lax.all_to_all(values, 'expert', split_axis=0, concat_axis=0, tiled=True)  33.8 us
    ppermute x15, starting transfers between devices, dp_from(): return lax.ppermute(values, 'dp', pairs)  20.9 us
    ppermute x20, starting transfers between devices, core_swap(): return lax.ppermute(values, 'dp', [(d, d ^ 1) for d in range(DP)])  16.9 us
    reduce_scatter x1, waiting for transfers between devices, per_device(): lax.psum_scatter(tied(routed, low), 'expert', scatter_dimension=0, tiled=...  7.76 us
  transfers between devices with their start and end apart: 45, of which 16 were waited for; matrix products, arithmetic and copies ran while one was open for 5% of the time, Pallas kernels for 20%

profile of v2, /device:TPU:0, one launch (start us, length us, event | category | flops | bytes accessed | tf_op | source)
XLA Modules:
  0.0 341.8 jit_solution(10577851728184269017)
XLA Ops:
  9.3 2.9 dense.1
  12.4 1.7 collective-permute-start.2
  14.1 2.9 collective-permute-start.1
  18.4 1.4 fusion.4
  19.8 2.7 subtract_convert_fusion
  22.4 2.7 pack.1
  25.2 1.8 multiply_sine_fusion
  27.1 16.4 %collective-permute-done.1.refs_6_.refs_11_ = bf16[144,2048]{1,0:T(8,128)(2,1)S(1)} collective-permute-done((bf16[144,2048]{1,0:T(8,128)(2,1)}, bf16[144,2048]{1,0:T(8,128)(2,1)S(1)}, u32[]{:S(2)}, u32[]{:S(2)}) %collective-permute-start.1) | collective-permute-done | bytes 589856 | tf_op jit(solution)/shard_map/ppermute | solution.py:204
  44.1 2.2 collective-permute-done.6.refs_11_.refs_16_
  48.2 5.4 %qkv.1 = (bf16[48,1024]{1,0:T(8,128)(2,1)}, bf16[16,192,128]{2,1,0:T(8,128)(2,1)}) custom-call(s32[4]{0:T(128)S(1)} %pad_add_fusion.refs_0_, bf16[128,1024]{1,0:T(8,128)(2,1)} %bitcast.44, f32[32,128]{1,0:T(8,128)S(1)} %get-tuple-element.168.refs_2_, f32[32,128]{1,0:T(8,128)S(1)} %get-tuple-element.167.refs_3_, ...), custom_call_target="tpu_custom_call" | custom-call | flops 25000001536 | bytes 1000 | tf_op jit(solution)/shard_map/qkv/pallas_call | solution.py:174
  53.7 7.7 %all-to-all-start = ((bf16[16,192,128]{2,1,0:T(8,128)(2,1)}), bf16[16,192,128]{2,1,0:T(8,128)(2,1)S(1)}, u32[]{:S(2)}, u32[]{:S(2)}) async-start(bf16[16,192,128]{2,1,0:T(8,128)(2,1)} %get-tuple-element.87), calls=%async_computation | async-start | bytes 1572864 | tf_op jit(solution)/shard_map/all_to_all | solution.py:258
  61.5 2.4 collective-permute-start.8
  63.9 1.7 collective-permute-start.7
  65.6 10.8 %collective-permute-done.9.refs_8_.refs_9_ = bf16[128,1024]{1,0:T(8,128)(2,1)S(1)} collective-permute-done((bf16[128,1024]{1,0:T(8,128)(2,1)S(1)}, bf16[128,1024]{1,0:T(8,128)(2,1)S(1)}, u32[]{:S(2)}, u32[]{:S(2)}) %collective-permute-start.9) | collective-permute-done | bytes 262176 | tf_op jit(solution)/shard_map/ppermute | solution.py:204
  77.0 8.1 %all-to-all-done.refs_1_ = bf16[16,192,128]{2,1,0:T(8,128)(2,1)S(1)} async-done(((bf16[16,192,128]{2,1,0:T(8,128)(2,1)}), bf16[16,192,128]{2,1,0:T(8,128)(2,1)S(1)}, u32[]{:S(2)}, u32[]{:S(2)}) %all-to-all-start) | async-done | bytes 786464 | tf_op jit(solution)/shard_map/all_to_all | solution.py:258
  85.1 6.0 %attend.1 = (f32[64,2048]{1,0:T(8,128)}, f32[1,2048]{1,0:T(1,128)}, bf16[16,64,128]{2,1,0:T(8,128)(2,1)}) custom-call(s32[4]{0:T(128)S(1)} %pad_add_fusion.refs_0_, bf16[16,192,128]{2,1,0:T(8,128)(2,1)S(1)} %all-to-all-done.refs_1_, s32[1,2048]{1,0:T(1,128)S(1)} %get-tuple-element.162.refs_2_.refs_7_), custom_call_target="tpu_custom_call" | custom-call | flops 30000001024 | bytes 1000 | tf_op jit(solution)/shard_map/attend/pallas_call | solution.py:174
  91.2 3.8 %all-to-all-start.1 = ((bf16[16,64,128]{2,1,0:T(8,128)(2,1)}), bf16[16,64,128]{2,1,0:T(8,128)(2,1)S(1)}, u32[]{:S(2)}, u32[]{:S(2)}) async-start(bf16[16,64,128]{2,1,0:T(8,128)(2,1)} %get-tuple-element.88), calls=%async_computation.1 | async-start | bytes 524288 | tf_op jit(solution)/shard_map/all_to_all | solution.py:258
  95.1 8.6 %all-to-all-done.1 = bf16[16,64,128]{2,1,0:T(8,128)(2,1)S(1)} async-done(((bf16[16,64,128]{2,1,0:T(8,128)(2,1)}), bf16[16,64,128]{2,1,0:T(8,128)(2,1)S(1)}, u32[]{:S(2)}, u32[]{:S(2)}) %all-to-all-start.1) | async-done | bytes 262176 | tf_op jit(solution)/shard_map/all_to_all | solution.py:258
  103.7 4.9 %project.1 = (f32[128,1024]{1,0:T(8,128)}, bf16[1280,1024]{1,0:T(8,128)(2,1)}, bf16[1280,128]{1,0:T(8,128)(2,1)}) custom-call(s32[4]{0:T(128)S(1)} %pad_add_fusion.refs_0_, bf16[1024,128]{1,0:T(8,128)(2,1)S(1)} %bitcast.30, bf16[128,1024]{1,0:T(8,128)(2,1)} %bitcast.45, bf16[48,1024]{1,0:T(8,128)(2,1)} %get-tuple-element.89.refs_3_.refs_1_.refs_5_.refs_4_, ...), custom_call_target="tpu_custom_call" | custom-call | flops 25000001536 | bytes 1000 | tf_op jit(solution)/shard_map/project/pallas_call | solution.py:174
  108.6 3.7 %all-to-all-start.2 = ((bf16[16,80,1024]{2,1,0:T(8,128)(2,1)}), bf16[16,80,1024]{2,1,0:T(8,128)(2,1)S(1)}, u32[]{:S(2)}, u32[]{:S(2)}) async-start(bf16[16,80,1024]{2,1,0:T(8,128)(2,1)} %bitcast.40), calls=%async_computation.2 | async-start | bytes 5242880 | tf_op jit(solution)/shard_map/all_to_all | solution.py:258
  112.4 5.6 %grad_rows.1 = (bf16[2,640,1024]{2,1,0:T(8,128)(2,1)}, bf16[16,80,128]{2,1,0:T(8,128)(2,1)}) custom-call(s32[4]{0:T(128)S(1)} %pad_add_fusion.refs_0_, bf16[4352,1024]{1,0:T(8,128)(2,1)} %all-gather.4.cloned.1.call-done.refs_1_.refs_2_), custom_call_target="tpu_custom_call" | custom-call | flops 1000 | bytes 1000 | tf_op jit(solution)/shard_map/grad_rows/pallas_call | solution.py:174
  118.0 29.6 %all-to-all-done.2 = bf16[16,80,1024]{2,1,0:T(8,128)(2,1)S(1)} async-done(((bf16[16,80,1024]{2,1,0:T(8,128)(2,1)}), bf16[16,80,1024]{2,1,0:T(8,128)(2,1)S(1)}, u32[]{:S(2)}, u32[]{:S(2)}) %all-to-all-start.2) | async-done | bytes 2621472 | tf_op jit(solution)/shard_map/all_to_all | solution.py:258
  147.6 20.4 %experts.1 = (bf16[1280,1024]{1,0:T(8,128)(2,1)}, bf16[2,640,1024]{2,1,0:T(8,128)(2,1)}, bf16[2,640,512]{2,1,0:T(8,128)(2,1)}, bf16[2,640,512]{2,1,0:T(8,128)(2,...) custom-call(s32[4]{0:T(128)S(1)} %pad_add_fusion.refs_0_, ...), custom_call_target="tpu_custom_call" | custom-call | flops 60000002048 | bytes 1000 | tf_op jit(solution)/shard_map/experts/pallas_call | solution.py:174
  168.0 3.7 %all-to-all-start.3 = ((bf16[16,80,1024]{2,1,0:T(8,128)(2,1)}), bf16[16,80,1024]{2,1,0:T(8,128)(2,1)S(1)}, u32[]{:S(2)}, u32[]{:S(2)}) async-start(bf16[16,80,1024]{2,1,0:T(8,128)(2,1)} %bitcast.39), calls=%async_computation.3 | async-start | bytes 5242880 | tf_op jit(solution)/shard_map/all_to_all | solution.py:258
  171.8 17.5 %weights.1 = (bf16[2048,1024]{1,0:T(8,128)(2,1)}, bf16[2,384,512]{2,1,0:T(8,128)(2,1)}, bf16[2,384,512]{2,1,0:T(8,128)(2,1)}, bf16[2,384,512]{2,1,0:T(8,128)(2,1...) custom-call(s32[4]{0:T(128)S(1)} %pad_add_fusion.refs_0_, ...), custom_call_target="tpu_custom_call" | custom-call | flops 1000 | bytes 1000 | tf_op jit(solution)/shard_map/weights/pallas_call | solution.py:174
  190.0 13.0 %collective-permute-start.17 = (bf16[2,384,512]{2,1,0:T(8,128)(2,1)}, bf16[2,384,512]{2,1,0:T(8,128)(2,1)S(1)}, u32[]{:S(2)}, u32[]{:S(2)}) collective-permute-start(bf16[2,384,512]{2,1,0:T(8,128)(2,1)} %get-tuple-element.114), channel_id=1, source_target_pairs={{0,16},{16,0},{32,48},{48,32},{64,80},{80,64},{96,112},{112,96},{1... | collective-permute-start | bytes 2359304 | tf_op jit(solution)/shard_map/ppermute | solution.py:208
  203.0 5.9 %normed.1.refs_8_ = bf16[2048,1024]{1,0:T(8,128)(2,1)} custom-call(s32[4]{0:T(128)S(1)} %pad_add_fusion.refs_0_, bf16[48,1024]{1,0:T(8,128)(2,1)} %get-tuple-element.89.refs_3_.refs_1_.refs_5_.refs_4_, bf16[4352,1024]{1,0:T(8,128)(2,1)} %all-gather.4.cloned.1.call-done.refs_1_.refs_2_), custom_call_target="tpu_custom_call" | custom-call | flops 1000 | bytes 1000 | tf_op jit(solution)/shard_map/normed/pallas_call | solution.py:174
  210.6 4.7 %expert_pairs.1 = (bf16[2,384,512]{2,1,0:T(8,128)(2,1)}, bf16[2,384,512]{2,1,0:T(8,128)(2,1)}, bf16[2,384,512]{2,1,0:T(8,128)(2,1)}, bf16[2,384,512]{2,1,0:T(8,128)(2,1)}) custom-call(s32[4]{0:T(128)S(1)} %pad_add_fusion.refs_0_, bf16[2,384,512]{2,1,0:T(8,128)(2,1)} %get-tuple-element.107.refs_1_, bf16[2,384,512]{2,1,0:T(8,128)(2,1)} %get-tuple-element.108.refs_2_, ...), custom_call_target="tpu_custom_call" | custom-call | flops 1000 | bytes 1000 | tf_op jit(solution)/shard_map/expert_pairs/pallas_call | solution.py:174
  215.3 4.3 %hidden_grad.1 = (f32[128,1024]{1,0:T(8,128)}, bf16[128,1024]{1,0:T(8,128)(2,1)}, bf16[16,64,128]{2,1,0:T(8,128)(2,1)}, f32[1,1024]{1,0:T(1,128)}) custom-call(s32[4]{0:T(128)S(1)} %pad_add_fusion.refs_0_, bf16[1280,1024]{1,0:T(8,128)(2,1)S(1)} %bitcast.28, bf16[1280,128]{1,0:T(8,128)(2,1)} %get-tuple-element.120.refs_2_, ...), custom_call_target="tpu_custom_call" | custom-call | flops 20000000000 | bytes 1000 | tf_op jit(solution)/shard_map/hidden_grad/pallas_call | solution.py:174
  219.6 3.7 %out_weights.1 = (bf16[128,1152]{1,0:T(8,128)(2,1)}, bf16[128,1152]{1,0:T(8,128)(2,1)}, bf16[128,1152]{1,0:T(8,128)(2,1)}, bf16[128,1152]{1,0:T(8,128)(2,1)}, bf...) custom-call(s32[4]{0:T(128)S(1)} %pad_add_fusion.refs_0_, ...), custom_call_target="tpu_custom_call" | custom-call | flops 1000 | bytes 1000 | tf_op jit(solution)/shard_map/out_weights/pallas_call | solution.py:174
  224.5 7.1 %all-to-all-start.4 = ((bf16[16,64,128]{2,1,0:T(8,128)(2,1)}), bf16[16,64,128]{2,1,0:T(8,128)(2,1)S(1)}, u32[]{:S(2)}, u32[]{:S(2)}) async-start(bf16[16,64,128]{2,1,0:T(8,128)(2,1)} %get-tuple-element.140), calls=%async_computation.5 | async-start | bytes 524288 | tf_op jit(solution)/shard_map/all_to_all | solution.py:258
  233.4 3.0 out_pairs.1
  236.4 4.1 %all-to-all-done.4.refs_4_ = bf16[16,64,128]{2,1,0:T(8,128)(2,1)S(1)} async-done(((bf16[16,64,128]{2,1,0:T(8,128)(2,1)}), bf16[16,64,128]{2,1,0:T(8,128)(2,1)S(1)}, u32[]{:S(2)}, u32[]{:S(2)}) %all-to-all-start.4) | async-done | bytes 262176 | tf_op jit(solution)/shard_map/all_to_all | solution.py:258
  240.6 12.0 %attend_back.1 = (bf16[16,192,128]{2,1,0:T(8,128)(2,1)}, bf16[192,128]{1,0:T(8,128)(2,1)}, bf16[192,128]{1,0:T(8,128)(2,1)}, bf16[192,128]{1,0:T(8,128)(2,1)}, b...) custom-call(s32[4]{0:T(128)S(1)} %pad_add_fusion.refs_0_, ...), custom_call_target="tpu_custom_call" | custom-call | flops 60000002048 | bytes 1000 | tf_op jit(solution)/shard_map/attend_back/pallas_call | solution.py:174
  252.8 2.4 collective-permute-start.31
  255.2 1.7 collective-permute-start.30
  261.1 9.0 %collective-permute-done.29 = bf16[128,1152]{1,0:T(8,128)(2,1)S(1)} collective-permute-done((bf16[128,1152]{1,0:T(8,128)(2,1)S(1)}, bf16[128,1152]{1,0:T(8,128)(2,1)S(1)}, u32[]{:S(2)}, u32[]{:S(2)}) %collective-permute-start.29) | collective-permute-done | bytes 294944 | tf_op jit(solution)/shard_map/ppermute | solution.py:204
  271.4 3.8 %all-to-all-start.5 = ((bf16[16,8,1152]{2,1,0:T(8,128)(2,1)}), bf16[16,8,1152]{2,1,0:T(8,128)(2,1)S(1)}, u32[]{:S(2)}, u32[]{:S(2)}) async-start(bf16[16,8,1152]{2,1,0:T(8,128)(2,1)} %fusion), calls=%async_computation.6 | async-start | bytes 589824 | tf_op jit(solution)/shard_map/all_to_all | solution.py:258
  275.2 1.7 collective-permute-start.32
  276.8 4.1 %collective-permute-start.34 = (bf16[2,384,512]{2,1,0:T(8,128)(2,1)}, bf16[2,384,512]{2,1,0:T(8,128)(2,1)}, u32[]{:S(2)}, u32[]{:S(2)}) collective-permute-start(bf16[2,384,512]{2,1,0:T(8,128)(2,1)} %get-tuple-element.117), channel_id=1, source_target_pairs={{0,64},{16,80},{32,96},{48,112},{64,0},{80,16},{96,32},{112,48},{1... | collective-permute-start | bytes 2359304 | tf_op jit(solution)/shard_map/ppermute | solution.py:204
  281.0 4.9 %all-to-all-done.5 = bf16[16,8,1152]{2,1,0:T(8,128)(2,1)S(1)} async-done(((bf16[16,8,1152]{2,1,0:T(8,128)(2,1)}), bf16[16,8,1152]{2,1,0:T(8,128)(2,1)S(1)}, u32[]{:S(2)}, u32[]{:S(2)}) %all-to-all-start.5) | async-done | bytes 294944 | tf_op jit(solution)/shard_map/all_to_all | solution.py:258
  287.6 3.8 %all-to-all-start.6 = ((bf16[16,456,128]{2,1,0:T(8,128)(2,1)}), bf16[16,456,128]{2,1,0:T(8,128)(2,1)S(1)}, u32[]{:S(2)}, u32[]{:S(2)}) async-start(bf16[16,456,128]{2,1,0:T(8,128)(2,1)} %pad_maximum_fusion), calls=%async_computation.7 | async-start | bytes 3735552 | tf_op jit(solution)/shard_map/all_to_all | solution.py:258
  291.5 5.8 %collective-permute-done.32 = bf16[2,384,512]{2,1,0:T(8,128)(2,1)S(1)} collective-permute-done((bf16[2,384,512]{2,1,0:T(8,128)(2,1)}, bf16[2,384,512]{2,1,0:T(8,128)(2,1)S(1)}, u32[]{:S(2)}, u32[]{:S(2)}) %collective-permute-start.32) | collective-permute-done | bytes 786464 | tf_op jit(solution)/shard_map/ppermute | solution.py:204
  297.3 16.8 %collective-permute-done.34 = bf16[2,384,512]{2,1,0:T(8,128)(2,1)} collective-permute-done((bf16[2,384,512]{2,1,0:T(8,128)(2,1)}, bf16[2,384,512]{2,1,0:T(8,128)(2,1)}, u32[]{:S(2)}, u32[]{:S(2)}) %collective-permute-start.34) | collective-permute-done | bytes 786464 | tf_op jit(solution)/shard_map/ppermute | solution.py:204
  314.1 1.9 convert_add_fusion
  317.9 7.8 %reduce-scatter.2.cloned.1.call-done = bf16[128,1024]{1,0:T(8,128)(2,1)} async-done(((bf16[2048,1024]{1,0:T(8,128)(2,1)}), bf16[128,1024]{1,0:T(8,128)(2,1)}) %reduce-scatter.2.cloned.1.call-update) | async-done | bytes 262160 | tf_op jit(solution)/shard_map/reduce_scatter | solution.py:1019
  325.6 1.7 add_convert_fusion.1
  327.4 7.1 %grad_input.1 = (f32[128,1024]{1,0:T(8,128)}, f32[128,1024]{1,0:T(8,128)}, f32[128,512]{1,0:T(8,128)}, f32[128,512]{1,0:T(8,128)}, f32[128,1024]{1,0:T(8,128)}, /*index=5*/f32[32,128]{1,0:T(8,128)}, f32[2,128]{1,0:T(2,128)S(1)}) custom-call(s32[4]{0:T(128)S(1)} %pad_add_fusion.refs_0_, bf16[16,456,128]{2,1,0:T(8,128)(2,1)S(1)} %all-to-all-done.6.refs_1_, ...), custom_call_target="tpu_custom_call" | custom-call | flops 35000000512 | bytes 1000 | tf_op jit(solution)/shard_map/grad_input/pallas_call | solution.py:174
  (161 shorter events, 21.9 us)
Async XLA Ops:
  7.2 105.2 %all-gather.4.cloned.1.call-start = ((), (), s32[]{:S(2)}) async-start(), calls=%async_computation.8 | async-start | bytes 9469952 | tf_op jit(solution)/shard_map/all_gather | solution.py:870
  12.2 135.4 %all-gather.6.cloned.1.call-start = ((), (), s32[]{:S(2)}) async-start(), calls=%async_computation.10 | async-start | bytes 7077888 | tf_op jit(solution)/shard_map/all_gather | solution.py:887
  12.3 31.8 %collective-permute-start.3 = (bf16[144,2048]{1,0:T(8,128)(2,1)}, bf16[144,2048]{1,0:T(8,128)(2,1)S(1)}, u32[]{:S(2)}, u32[]{:S(2)}) collective-permute-start(bf16[144,2048]{1,0:T(8,128)(2,1)} %get-tuple-element.85.refs_4_.refs_9_), channel_id=1, source_target_pairs={{0,16},{16,0},{32,48},{48,32},{64,80},{80,64},{96,112},{112,96},{1... | collective-permute-start | bytes 1769480 | tf_op jit(solution)/shard_map/ppermute | solution.py:208
  12.4 31.1 %collective-permute-start.2 = (bf16[144,2048]{1,0:T(8,128)(2,1)}, bf16[144,2048]{1,0:T(8,128)(2,1)S(1)}, u32[]{:S(2)}, u32[]{:S(2)}) collective-permute-start(bf16[144,2048]{1,0:T(8,128)(2,1)} %get-tuple-element.85.refs_4_.refs_9_), channel_id=1, source_target_pairs={{0,32},{16,48},{32,64},{48,80},{64,96},{80,112},{96,0},{112,16},{1... | collective-permute-start | bytes 1769480 | tf_op jit(solution)/shard_map/ppermute | solution.py:204
  14.1 29.4 %collective-permute-start.1 = (bf16[144,2048]{1,0:T(8,128)(2,1)}, bf16[144,2048]{1,0:T(8,128)(2,1)S(1)}, u32[]{:S(2)}, u32[]{:S(2)}) collective-permute-start(bf16[144,2048]{1,0:T(8,128)(2,1)} %get-tuple-element.85.refs_4_.refs_9_), channel_id=1, source_target_pairs={{0,64},{16,80},{32,96},{48,112},{64,0},{80,16},{96,32},{112,48},{1... | collective-permute-start | bytes 1769480 | tf_op jit(solution)/shard_map/ppermute | solution.py:204
  17.0 27.0 %collective-permute-start = (bf16[144,2048]{1,0:T(8,128)(2,1)}, bf16[144,2048]{1,0:T(8,128)(2,1)S(1)}, u32[]{:S(2)}, u32[]{:S(2)}) collective-permute-start(bf16[144,2048]{1,0:T(8,128)(2,1)} %get-tuple-element.85.refs_4_.refs_9_), channel_id=1, source_target_pairs={{0,96},{16,112},{32,0},{48,16},{64,32},{80,48},{96,64},{112,80},{1... | collective-permute-start | bytes 1769480 | tf_op jit(solution)/shard_map/ppermute | solution.py:204
  22.4 62.7 %copy-start.1 = (s32[1,2048]{1,0:T(1,128)}, s32[1,2048]{1,0:T(1,128)S(1)}, u32[]{:S(2)}) copy-start(s32[1,2048]{1,0:T(1,128)S(1)} %get-tuple-element.162.refs_2_.refs_7_) | copy-start | bytes 24580
  43.5 2.9 collective-permute-start.5
  43.5 2.8 collective-permute-start.6
  44.0 3.2 collective-permute-start.4
  53.7 31.5 %all-to-all-start = ((bf16[16,192,128]{2,1,0:T(8,128)(2,1)}), bf16[16,192,128]{2,1,0:T(8,128)(2,1)S(1)}, u32[]{:S(2)}, u32[]{:S(2)}) async-start(bf16[16,192,128]{2,1,0:T(8,128)(2,1)} %get-tuple-element.87), calls=%async_computation | async-start | bytes 1572864 | tf_op jit(solution)/shard_map/all_to_all | solution.py:258
  61.4 15.0 %collective-permute-start.9 = (bf16[128,1024]{1,0:T(8,128)(2,1)S(1)}, bf16[128,1024]{1,0:T(8,128)(2,1)S(1)}, u32[]{:S(2)}, u32[]{:S(2)}) collective-permute-start(bf16[128,1024]{1,0:T(8,128)(2,1)S(1)} %copy-done.28), channel_id=1, source_target_pairs={{0,32},{16,48},{32,64},{48,80},{64,96},{80,112},{96,0},{112,16},{1... | collective-permute-start | bytes 786440 | tf_op jit(solution)/shard_map/ppermute | solution.py:204
  61.5 14.8 %collective-permute-start.8 = (bf16[128,1024]{1,0:T(8,128)(2,1)S(1)}, bf16[128,1024]{1,0:T(8,128)(2,1)S(1)}, u32[]{:S(2)}, u32[]{:S(2)}) collective-permute-start(bf16[128,1024]{1,0:T(8,128)(2,1)S(1)} %copy-done.28), channel_id=1, source_target_pairs={{0,64},{16,80},{32,96},{48,112},{64,0},{80,16},{96,32},{112,48},{1... | collective-permute-start | bytes 786440 | tf_op jit(solution)/shard_map/ppermute | solution.py:204
  63.9 13.1 %collective-permute-start.7 = (bf16[128,1024]{1,0:T(8,128)(2,1)S(1)}, bf16[128,1024]{1,0:T(8,128)(2,1)S(1)}, u32[]{:S(2)}, u32[]{:S(2)}) collective-permute-start(bf16[128,1024]{1,0:T(8,128)(2,1)S(1)} %copy-done.28), channel_id=1, source_target_pairs={{0,96},{16,112},{32,0},{48,16},{64,32},{80,48},{96,64},{112,80},{1... | collective-permute-start | bytes 786440 | tf_op jit(solution)/shard_map/ppermute | solution.py:204
  65.6 29.4 %collective-permute-start.10 = (bf16[128,1024]{1,0:T(8,128)(2,1)S(1)}, bf16[128,1024]{1,0:T(8,128)(2,1)S(1)}, u32[]{:S(2)}, u32[]{:S(2)}) collective-permute-start(bf16[128,1024]{1,0:T(8,128)(2,1)S(1)} %copy-done.28), channel_id=1, source_target_pairs={{0,16},{16,0},{32,48},{48,32},{64,80},{80,64},{96,112},{112,96},{1... | collective-permute-start | bytes 786440 | tf_op jit(solution)/shard_map/ppermute | solution.py:208
  76.4 18.7 %collective-permute-start.13 = (bf16[128,1024]{1,0:T(8,128)(2,1)S(1)}, bf16[128,1024]{1,0:T(8,128)(2,1)S(1)}, u32[]{:S(2)}, u32[]{:S(2)}) collective-permute-start(bf16[128,1024]{1,0:T(8,128)(2,1)S(1)} %collective-permute-done.9.refs_8_.refs_9_), channel_id=1, source_target_pairs={{0,16},{16,0},{32,48},{48,32},{64,80},{80,64},{96,112},{112,96},{1... | collective-permute-start | bytes 786440 | tf_op jit(solution)/shard_map/ppermute | solution.py:208
  76.4 18.7 %collective-permute-start.12 = (bf16[128,1024]{1,0:T(8,128)(2,1)S(1)}, bf16[128,1024]{1,0:T(8,128)(2,1)S(1)}, u32[]{:S(2)}, u32[]{:S(2)}) collective-permute-start(bf16[128,1024]{1,0:T(8,128)(2,1)S(1)} %collective-permute-done.8.refs_7_.refs_8_), channel_id=1, source_target_pairs={{0,16},{16,0},{32,48},{48,32},{64,80},{80,64},{96,112},{112,96},{1... | collective-permute-start | bytes 786440 | tf_op jit(solution)/shard_map/ppermute | solution.py:208
  77.0 18.1 %collective-permute-start.11 = (bf16[128,1024]{1,0:T(8,128)(2,1)S(1)}, bf16[128,1024]{1,0:T(8,128)(2,1)S(1)}, u32[]{:S(2)}, u32[]{:S(2)}) collective-permute-start(bf16[128,1024]{1,0:T(8,128)(2,1)S(1)} %collective-permute-done.7.refs_6_.refs_7_), channel_id=1, source_target_pairs={{0,16},{16,0},{32,48},{48,32},{64,80},{80,64},{96,112},{112,96},{1... | collective-permute-start | bytes 786440 | tf_op jit(solution)/shard_map/ppermute | solution.py:208
  91.2 12.5 %all-to-all-start.1 = ((bf16[16,64,128]{2,1,0:T(8,128)(2,1)}), bf16[16,64,128]{2,1,0:T(8,128)(2,1)S(1)}, u32[]{:S(2)}, u32[]{:S(2)}) async-start(bf16[16,64,128]{2,1,0:T(8,128)(2,1)} %get-tuple-element.88), calls=%async_computation.1 | async-start | bytes 524288 | tf_op jit(solution)/shard_map/all_to_all | solution.py:258
  108.6 39.0 %all-to-all-start.2 = ((bf16[16,80,1024]{2,1,0:T(8,128)(2,1)}), bf16[16,80,1024]{2,1,0:T(8,128)(2,1)S(1)}, u32[]{:S(2)}, u32[]{:S(2)}) async-start(bf16[16,80,1024]{2,1,0:T(8,128)(2,1)} %bitcast.40), calls=%async_computation.2 | async-start | bytes 5242880 | tf_op jit(solution)/shard_map/all_to_all | solution.py:258
  168.0 47.3 %all-to-all-start.3 = ((bf16[16,80,1024]{2,1,0:T(8,128)(2,1)}), bf16[16,80,1024]{2,1,0:T(8,128)(2,1)S(1)}, u32[]{:S(2)}, u32[]{:S(2)}) async-start(bf16[16,80,1024]{2,1,0:T(8,128)(2,1)} %bitcast.39), calls=%async_computation.3 | async-start | bytes 5242880 | tf_op jit(solution)/shard_map/all_to_all | solution.py:258
  189.3 19.6 %collective-permute-start.14 = (bf16[2,384,512]{2,1,0:T(8,128)(2,1)}, bf16[2,384,512]{2,1,0:T(8,128)(2,1)S(1)}, u32[]{:S(2)}, u32[]{:S(2)}) collective-permute-start(bf16[2,384,512]{2,1,0:T(8,128)(2,1)} %get-tuple-element.111), channel_id=1, source_target_pairs={{0,16},{16,0},{32,48},{48,32},{64,80},{80,64},{96,112},{112,96},{1... | collective-permute-start | bytes 2359304 | tf_op jit(solution)/shard_map/ppermute | solution.py:208
  189.4 19.5 %collective-permute-start.15 = (bf16[2,384,512]{2,1,0:T(8,128)(2,1)}, bf16[2,384,512]{2,1,0:T(8,128)(2,1)S(1)}, u32[]{:S(2)}, u32[]{:S(2)}) collective-permute-start(bf16[2,384,512]{2,1,0:T(8,128)(2,1)} %get-tuple-element.112), channel_id=1, source_target_pairs={{0,16},{16,0},{32,48},{48,32},{64,80},{80,64},{96,112},{112,96},{1... | collective-permute-start | bytes 2359304 | tf_op jit(solution)/shard_map/ppermute | solution.py:208
  189.9 19.0 %collective-permute-start.16 = (bf16[2,384,512]{2,1,0:T(8,128)(2,1)}, bf16[2,384,512]{2,1,0:T(8,128)(2,1)S(1)}, u32[]{:S(2)}, u32[]{:S(2)}) collective-permute-start(bf16[2,384,512]{2,1,0:T(8,128)(2,1)} %get-tuple-element.113), channel_id=1, source_target_pairs={{0,16},{16,0},{32,48},{48,32},{64,80},{80,64},{96,112},{112,96},{1... | collective-permute-start | bytes 2359304 | tf_op jit(solution)/shard_map/ppermute | solution.py:208
  190.0 19.0 %collective-permute-start.17 = (bf16[2,384,512]{2,1,0:T(8,128)(2,1)}, bf16[2,384,512]{2,1,0:T(8,128)(2,1)S(1)}, u32[]{:S(2)}, u32[]{:S(2)}) collective-permute-start(bf16[2,384,512]{2,1,0:T(8,128)(2,1)} %get-tuple-element.114), channel_id=1, source_target_pairs={{0,16},{16,0},{32,48},{48,32},{64,80},{80,64},{96,112},{112,96},{1... | collective-permute-start | bytes 2359304 | tf_op jit(solution)/shard_map/ppermute | solution.py:208
  223.4 9.0 %collective-permute-start.18 = (bf16[128,1152]{1,0:T(8,128)(2,1)}, bf16[128,1152]{1,0:T(8,128)(2,1)S(1)}, u32[]{:S(2)}, u32[]{:S(2)}) collective-permute-start(bf16[128,1152]{1,0:T(8,128)(2,1)} %get-tuple-element.129), channel_id=1, source_target_pairs={{0,16},{16,0},{32,48},{48,32},{64,80},{80,64},{96,112},{112,96},{1... | collective-permute-start | bytes 884744 | tf_op jit(solution)/shard_map/ppermute | solution.py:208
  223.5 8.8 %collective-permute-start.19 = (bf16[128,1152]{1,0:T(8,128)(2,1)}, bf16[128,1152]{1,0:T(8,128)(2,1)S(1)}, u32[]{:S(2)}, u32[]{:S(2)}) collective-permute-start(bf16[128,1152]{1,0:T(8,128)(2,1)} %get-tuple-element.130), channel_id=1, source_target_pairs={{0,16},{16,0},{32,48},{48,32},{64,80},{80,64},{96,112},{112,96},{1... | collective-permute-start | bytes 884744 | tf_op jit(solution)/shard_map/ppermute | solution.py:208
  224.0 8.4 %collective-permute-start.20 = (bf16[128,1152]{1,0:T(8,128)(2,1)}, bf16[128,1152]{1,0:T(8,128)(2,1)S(1)}, u32[]{:S(2)}, u32[]{:S(2)}) collective-permute-start(bf16[128,1152]{1,0:T(8,128)(2,1)} %get-tuple-element.131), channel_id=1, source_target_pairs={{0,16},{16,0},{32,48},{48,32},{64,80},{80,64},{96,112},{112,96},{1... | collective-permute-start | bytes 884744 | tf_op jit(solution)/shard_map/ppermute | solution.py:208
  224.0 8.4 %collective-permute-start.21 = (bf16[128,1152]{1,0:T(8,128)(2,1)}, bf16[128,1152]{1,0:T(8,128)(2,1)S(1)}, u32[]{:S(2)}, u32[]{:S(2)}) collective-permute-start(bf16[128,1152]{1,0:T(8,128)(2,1)} %get-tuple-element.132), channel_id=1, source_target_pairs={{0,16},{16,0},{32,48},{48,32},{64,80},{80,64},{96,112},{112,96},{1... | collective-permute-start | bytes 884744 | tf_op jit(solution)/shard_map/ppermute | solution.py:208
  224.5 16.1 %all-to-all-start.4 = ((bf16[16,64,128]{2,1,0:T(8,128)(2,1)}), bf16[16,64,128]{2,1,0:T(8,128)(2,1)S(1)}, u32[]{:S(2)}, u32[]{:S(2)}) async-start(bf16[16,64,128]{2,1,0:T(8,128)(2,1)} %get-tuple-element.140), calls=%async_computation.5 | async-start | bytes 524288 | tf_op jit(solution)/shard_map/all_to_all | solution.py:258
  231.6 94.0 %reduce-scatter.2.cloned.1.call-start = ((), (), s32[]{:S(2)}) async-start(), calls=%async_computation.9 | async-start | bytes 4456448 | tf_op jit(solution)/shard_map/reduce_scatter | solution.py:1019
  240.6 30.0 %copy-start.16 = (bf16[128,1152]{1,0:T(8,128)(2,1)S(1)}, bf16[128,1152]{1,0:T(8,128)(2,1)}, u32[]{:S(2)}) copy-start(bf16[128,1152]{1,0:T(8,128)(2,1)} %get-tuple-element.133) | copy-start | bytes 884740
  252.6 28.4 %copy-start.17 = (bf16[192,128]{1,0:T(8,128)(2,1)S(1)}, bf16[192,128]{1,0:T(8,128)(2,1)}, u32[]{:S(2)}) copy-start(bf16[192,128]{1,0:T(8,128)(2,1)} %get-tuple-element.142) | copy-start | bytes 147460
  252.6 4.3 %collective-permute-start.23 = (bf16[192,128]{1,0:T(8,128)(2,1)}, bf16[192,128]{1,0:T(8,128)(2,1)S(1)}, u32[]{:S(2)}, u32[]{:S(2)}) collective-permute-start(bf16[192,128]{1,0:T(8,128)(2,1)} %get-tuple-element.145), channel_id=1, source_target_pairs={{0,16},{16,0},{32,48},{48,32},{64,80},{80,64},{96,112},{112,96},{1... | collective-permute-start | bytes 147464 | tf_op jit(solution)/shard_map/ppermute | solution.py:208
  252.7 17.4 %collective-permute-start.29 = (bf16[128,1152]{1,0:T(8,128)(2,1)S(1)}, bf16[128,1152]{1,0:T(8,128)(2,1)S(1)}, u32[]{:S(2)}, u32[]{:S(2)}) collective-permute-start(bf16[128,1152]{1,0:T(8,128)(2,1)S(1)} %copy-done.27), channel_id=1, source_target_pairs={{0,32},{16,48},{32,64},{48,80},{64,96},{80,112},{96,0},{112,16},{1... | collective-permute-start | bytes 884744 | tf_op jit(solution)/shard_map/ppermute | solution.py:204
  252.8 17.3 %collective-permute-start.31 = (bf16[128,1152]{1,0:T(8,128)(2,1)S(1)}, bf16[128,1152]{1,0:T(8,128)(2,1)S(1)}, u32[]{:S(2)}, u32[]{:S(2)}) collective-permute-start(bf16[128,1152]{1,0:T(8,128)(2,1)S(1)} %copy-done.26), channel_id=1, source_target_pairs={{0,64},{16,80},{32,96},{48,112},{64,0},{80,16},{96,32},{112,48},{1... | collective-permute-start | bytes 884744 | tf_op jit(solution)/shard_map/ppermute | solution.py:204
  255.2 15.4 %collective-permute-start.30 = (bf16[128,1152]{1,0:T(8,128)(2,1)S(1)}, bf16[128,1152]{1,0:T(8,128)(2,1)S(1)}, u32[]{:S(2)}, u32[]{:S(2)}) collective-permute-start(bf16[128,1152]{1,0:T(8,128)(2,1)S(1)} %copy-done.25), channel_id=1, source_target_pairs={{0,96},{16,112},{32,0},{48,16},{64,32},{80,48},{96,64},{112,80},{1... | collective-permute-start | bytes 884744 | tf_op jit(solution)/shard_map/ppermute | solution.py:204
  256.9 20.0 %collective-permute-start.22 = (bf16[192,128]{1,0:T(8,128)(2,1)}, bf16[192,128]{1,0:T(8,128)(2,1)S(1)}, u32[]{:S(2)}, u32[]{:S(2)}) collective-permute-start(bf16[192,128]{1,0:T(8,128)(2,1)} %get-tuple-element.143), channel_id=1, source_target_pairs={{0,16},{16,0},{32,48},{48,32},{64,80},{80,64},{96,112},{112,96},{1... | collective-permute-start | bytes 147464 | tf_op jit(solution)/shard_map/ppermute | solution.py:208
  256.9 1.6 collective-permute-start.25
  258.5 1.4 collective-permute-start.27
  259.9 21.0 %collective-permute-start.24 = (bf16[192,128]{1,0:T(8,128)(2,1)S(1)}, bf16[192,128]{1,0:T(8,128)(2,1)S(1)}, u32[]{:S(2)}, u32[]{:S(2)}) collective-permute-start(bf16[192,128]{1,0:T(8,128)(2,1)S(1)} %add_convert_fusion.5), channel_id=1, source_target_pairs={{0,32},{16,48},{32,64},{48,80},{64,96},{80,112},{96,0},{112,16},{1... | collective-permute-start | bytes 147464 | tf_op jit(solution)/shard_map/ppermute | solution.py:204
  270.1 10.9 %collective-permute-start.26 = (bf16[192,128]{1,0:T(8,128)(2,1)S(1)}, bf16[192,128]{1,0:T(8,128)(2,1)S(1)}, u32[]{:S(2)}, u32[]{:S(2)}) collective-permute-start(bf16[192,128]{1,0:T(8,128)(2,1)S(1)} %add_convert_fusion.4), channel_id=1, source_target_pairs={{0,96},{16,112},{32,0},{48,16},{64,32},{80,48},{96,64},{112,80},{1... | collective-permute-start | bytes 147464 | tf_op jit(solution)/shard_map/ppermute | solution.py:204
  270.1 10.9 %collective-permute-start.28 = (bf16[192,128]{1,0:T(8,128)(2,1)S(1)}, bf16[192,128]{1,0:T(8,128)(2,1)S(1)}, u32[]{:S(2)}, u32[]{:S(2)}) collective-permute-start(bf16[192,128]{1,0:T(8,128)(2,1)S(1)} %add_convert_fusion.3), channel_id=1, source_target_pairs={{0,64},{16,80},{32,96},{48,112},{64,0},{80,16},{96,32},{112,48},{1... | collective-permute-start | bytes 147464 | tf_op jit(solution)/shard_map/ppermute | solution.py:204
  271.4 14.6 %all-to-all-start.5 = ((bf16[16,8,1152]{2,1,0:T(8,128)(2,1)}), bf16[16,8,1152]{2,1,0:T(8,128)(2,1)S(1)}, u32[]{:S(2)}, u32[]{:S(2)}) async-start(bf16[16,8,1152]{2,1,0:T(8,128)(2,1)} %fusion), calls=%async_computation.6 | async-start | bytes 589824 | tf_op jit(solution)/shard_map/all_to_all | solution.py:258
  275.2 22.1 %collective-permute-start.32 = (bf16[2,384,512]{2,1,0:T(8,128)(2,1)}, bf16[2,384,512]{2,1,0:T(8,128)(2,1)S(1)}, u32[]{:S(2)}, u32[]{:S(2)}) collective-permute-start(bf16[2,384,512]{2,1,0:T(8,128)(2,1)} %get-tuple-element.116), channel_id=1, source_target_pairs={{0,32},{16,48},{32,64},{48,80},{64,96},{80,112},{96,0},{112,16},{1... | collective-permute-start | bytes 2359304 | tf_op jit(solution)/shard_map/ppermute | solution.py:204
  276.8 37.3 %collective-permute-start.34 = (bf16[2,384,512]{2,1,0:T(8,128)(2,1)}, bf16[2,384,512]{2,1,0:T(8,128)(2,1)}, u32[]{:S(2)}, u32[]{:S(2)}) collective-permute-start(bf16[2,384,512]{2,1,0:T(8,128)(2,1)} %get-tuple-element.117), channel_id=1, source_target_pairs={{0,64},{16,80},{32,96},{48,112},{64,0},{80,16},{96,32},{112,48},{1... | collective-permute-start | bytes 2359304 | tf_op jit(solution)/shard_map/ppermute | solution.py:204
  280.9 33.1 %collective-permute-start.33 = (bf16[2,384,512]{2,1,0:T(8,128)(2,1)}, bf16[2,384,512]{2,1,0:T(8,128)(2,1)}, u32[]{:S(2)}, u32[]{:S(2)}) collective-permute-start(bf16[2,384,512]{2,1,0:T(8,128)(2,1)} %get-tuple-element.118), channel_id=1, source_target_pairs={{0,96},{16,112},{32,0},{48,16},{64,32},{80,48},{96,64},{112,80},{1... | collective-permute-start | bytes 2359304 | tf_op jit(solution)/shard_map/ppermute | solution.py:204
  287.6 39.7 %all-to-all-start.6 = ((bf16[16,456,128]{2,1,0:T(8,128)(2,1)}), bf16[16,456,128]{2,1,0:T(8,128)(2,1)S(1)}, u32[]{:S(2)}, u32[]{:S(2)}) async-start(bf16[16,456,128]{2,1,0:T(8,128)(2,1)} %pad_maximum_fusion), calls=%async_computation.7 | async-start | bytes 3735552 | tf_op jit(solution)/shard_map/all_to_all | solution.py:258
  (33 other events, 219.3 us)
Sparse Core Ops, SparseCore 0:
  12.4 84.2 all-gather.3
  98.3 40.4 all-gather.5
  235.8 89.7 reduce-scatter.1
